TPU v7x, 512 devices: a whole 4x4x16 slice. The times are simulated.
512 devices in a mesh: frame: 8 (over z_lo, core), seg: 16 (over z_hi, x), coil: 4 (over y).
Axes of the slice: x: 4, y: 4, z: 16 (z_hi: 4, z_lo: 4; z = z_hi * 4 + z_lo), core: 2. Of those that a mesh axis runs over, the one named last changes fastest.
Arguments:
- cal_source: bfloat16 [128, 4608, 384], P('seg', 'frame'), may hold values from -6 to 6
- cal_target: bfloat16 [128, 32, 2, 4608], P('seg', 'coil', None, 'frame'), may hold values from -6 to 6
- app_source: bfloat16 [8, 64, 128, 384], P('frame', 'seg'), may hold values from -6 to 6
- readers: int32 [8, 64], P('frame', 'seg'), may hold values from 0 to 127
- blocks: int32 [8, 64], P('frame', 'seg'), may hold values from 0 to 15
- interp: bfloat16 [8, 64, 256, 128], P('frame', 'seg'), may hold values from -0.5 to 0.5
Outputs:
- combined: float32 [8, 4096], P('frame', 'seg')
All inputs are finite; a program needn't handle non-finite values.
Results may differ from a plain program's by a relative error of at most 0.0025.
Values may be sent and summed in bfloat16 or wider, within the bound.
No kernel may reach another device: no remote copies, remote signals or barrier semaphores. Data moves between devices by JAX's collectives and lax.ppermute only.
A program may use at most 128 MiB of HBM per device.

v0:
```python
import jax
import jax.numpy as jnp
from jax import lax
from jax.sharding import PartitionSpec as P

regular = 0.02
epsilon = 1e-06


def weights_from(gram_real, gram_imag, right_side):
    width = gram_real.shape[0]
    upper = jnp.concatenate([gram_real, -gram_imag], axis=1)
    lower = jnp.concatenate([gram_imag, gram_real], axis=1)
    system = jnp.concatenate([upper, lower], axis=0)
    shift_value = regular * jnp.trace(gram_real) / width
    system = system + shift_value * jnp.eye(2 * width, dtype=system.dtype)
    factor = jnp.linalg.cholesky(system)
    middle = jax.scipy.linalg.solve_triangular(factor, right_side.T, lower=True)
    solved = jax.scipy.linalg.solve_triangular(factor, middle, lower=True, trans=1)
    return solved.T.astype(jnp.bfloat16)


def apply_rows(chosen):
    width = chosen.shape[-1] // 2
    part_real = chosen[..., :width]
    part_imag = chosen[..., width:]
    top_rows = jnp.concatenate([part_real, -part_imag], axis=-1)
    bottom_rows = jnp.concatenate([part_imag, part_real], axis=-1)
    return jnp.concatenate([top_rows, bottom_rows], axis=-2)


def on_device(cal_source, cal_target, app_source, readers, blocks, interp):
    frame_count = lax.axis_size("frame")
    seg_count = lax.axis_size("seg")
    width = cal_source.shape[2] // 2
    coil_local = cal_target.shape[1]
    square = width * width
    gram_size = 2 * square

    def unpack_grams(flat):
        return (flat[:square].reshape(width, width), flat[square:].reshape(width, width))

    def solve_flat(term):
        gram_real, gram_imag = unpack_grams(term[:gram_size])
        right_side = term[gram_size:].reshape(coil_local, 2 * width)
        return weights_from(gram_real, gram_imag, right_side).reshape(-1)

    reads = readers[0]
    places = blocks[0]
    gram = jnp.einsum("gck,gcl->gkl", cal_source, cal_source, preferred_element_type=jnp.float32)
    gram_real = gram[:, :width, :width] + gram[:, width:, width:]
    gram_imag = gram[:, :width, width:] - gram[:, width:, :width]
    proj = jnp.einsum("gjtc,gck->gjtk", cal_target, cal_source, preferred_element_type=jnp.float32)
    rhs_real = proj[:, :, 0, :width] + proj[:, :, 1, width:]
    rhs_imag = proj[:, :, 1, :width] - proj[:, :, 0, width:]
    right_side = jnp.concatenate([rhs_real, rhs_imag], axis=2)
    owned = lax.psum_scatter(
        jnp.concatenate(
            [
                jnp.concatenate(
                    [
                        gram_real.reshape(1 * lax.axis_size("frame"), -1),
                        gram_imag.reshape(1 * lax.axis_size("frame"), -1),
                    ],
                    axis=1,
                ),
                right_side.reshape(1 * lax.axis_size("frame"), -1),
            ],
            axis=1,
        ),
        "frame",
        scatter_dimension=0,
        tiled=True,
    )
    mine = jax.vmap(solve_flat)(owned)
    piece = lax.all_gather(mine, ("frame", "seg"), axis=0, tiled=True)
    position = jnp.arange(piece.shape[0], dtype=jnp.int32)
    segment = position % seg_count * frame_count + position // seg_count
    hits = (reads[:, None] == segment[None, :]).astype(jnp.bfloat16)
    chosen = jnp.dot(hits, piece, preferred_element_type=jnp.float32)
    chosen = chosen.astype(jnp.bfloat16).reshape(reads.shape[0], coil_local, 2 * width)
    matrix = apply_rows(chosen)
    filled = jnp.einsum(
        "rjk,rsk->rjs", matrix, app_source[0], preferred_element_type=jnp.float32
    ).astype(jnp.bfloat16)
    contrib = jnp.einsum("rjs,rcs->rjc", filled, interp[0], preferred_element_type=jnp.float32)
    index = jnp.arange(1 * lax.axis_size("seg"), dtype=jnp.int32)
    hits = (places[:, None] == index[None, :]).astype(jnp.float32)
    grid = lax.psum_scatter(
        jnp.einsum("rb,rjc->bjc", hits, contrib, precision=lax.Precision.HIGHEST).astype(
            jnp.bfloat16
        ),
        "seg",
        scatter_dimension=0,
        tiled=True,
    ).astype(jnp.float32)
    power = lax.psum(jnp.sum(grid * grid, axis=1), "coil")
    return jnp.sqrt(power + epsilon)


def solution(mesh):
    placed = (
        P("seg", "frame", None),
        P("seg", "coil", None, "frame"),
        P("frame", "seg", None, None),
        P("frame", "seg"),
        P("frame", "seg"),
        P("frame", "seg", None, None),
    )
    return jax.shard_map(
        on_device, mesh=mesh, in_specs=placed, out_specs=P("frame", "seg"), check_vma=False
    )
```

profile of v0, /device:TPU:2, one launch (start us, length us, event | category | flops | bytes accessed | tf_op | source)
XLA Modules:
  0.0 804.7 jit_solution(11972200982120203220)
XLA Ops:
  6.5 2.0 copy-done
  8.5 1.5 fusion
  10.2 2.5 fusion.61
  13.4 2.5 slice_add_fusion
  15.9 3.0 reshape.332
  19.0 3.1 reshape.333
  22.1 3.3 pad_maximum_fusion
  26.3 1.6 eq.67
  30.4 92.4 %all-reduce.4.cloned.1.call-done = f32[8,76800]{1,0:T(8,128)} async-done(((f32[8,76800]{1,0:T(8,128)}), f32[8,76800]{1,0:T(8,128)}) %all-reduce.4.cloned.1.call-update) | async-done | bytes 2457616
  122.8 4.2 select_reduce_fusion
  127.0 1.7 reshape.336
  128.7 1.7 copy.35
  130.4 1.6 neg.14
  132.1 1.7 reshape.335
  133.7 1.7 copy.36
  136.0 2.2 maximum_add_fusion
  138.2 2.1 copy.39
  143.3 13.2 %custom-call.29 = f32[1,128,128]{2,1,0:T(8,128)} custom-call(f32[1,128,128]{2,1,0:T(8,128)} %cholesky.189), custom_call_target="Cholesky" | custom-call | tf_op jit(solution)/shard_map/vmap(jit(cholesky))/cholesky | solution.py:17
  156.5 1.5 select_reduce_fusion.3
  157.9 11.3 %custom-call.30 = f32[1,1,128,128]{2,3,1,0:T(8,128)} custom-call(f32[1,1,128,128]{3,2,1,0:T(8,128)} %get-tuple-element.43), custom_call_target="InvertDiagBlocksLowerTriangular" | custom-call | tf_op jit(solution)/shard_map/vmap(jit(cholesky))/cholesky | solution.py:17
  169.2 1.8 fusion.18
  171.0 1.7 copy.40
  175.3 13.3 %custom-call.31 = f32[1,128,128]{2,1,0:T(8,128)} custom-call(f32[1,128,128]{2,1,0:T(8,128)} %cholesky.193), custom_call_target="Cholesky" | custom-call | tf_op jit(solution)/shard_map/vmap(jit(cholesky))/cholesky | solution.py:17
  188.6 1.5 select_reduce_fusion.2
  190.1 1.6 copy.42
  191.6 1.6 copy.41
  193.2 1.7 cholesky.167
  194.9 1.6 constant_dynamic-update-slice_fusion.2
  196.5 11.3 %custom-call.32 = f32[1,1,128,128]{2,3,1,0:T(8,128)} custom-call(f32[1,1,128,128]{3,2,1,0:T(8,128)} %get-tuple-element.41), custom_call_target="InvertDiagBlocksLowerTriangular" | custom-call | tf_op jit(solution)/shard_map/vmap(jit(cholesky))/cholesky | solution.py:17
  209.2 1.8 fusion.3
  211.0 2.0 fusion.4
  213.0 13.2 %custom-call.33 = f32[1,128,128]{2,1,0:T(8,128)} custom-call(f32[1,128,128]{2,1,0:T(8,128)} %fusion.4), custom_call_target="Cholesky" | custom-call | tf_op jit(solution)/shard_map/vmap(jit(cholesky))/cholesky | solution.py:17
  227.0 1.6 copy.44
  233.5 1.9 select_select_fusion
  236.1 19.9 %while.1 = (s32[]{:T(128)}, f32[1,384,384]{1,2,0:T(8,128)}, s32[3,2]{0,1:T(2,128)S(1)}, f32[3,1,128,128]{3,2,1,0:T(8,128)}, s32[]{:T(128)}) while((s32[]{:T(128)}, f32[1,384,384]{1,2,0:T(8,128)}, s32[3,2]{0,1:T(2,128)S(1)}, f32[3,1,128,128]{3,2,1,0:T(8,128)}, s32[]{:T(128)}) %tuple.32), condition=%wide.while_cond, body=%wide.while_body.sunk | while | flops 2 | bytes 393833 | solution.py:19
  236.8 3.0 constant_dynamic-slice_fusion.5
  239.8 1.6 copy.67
  243.5 3.0 constant_dynamic-slice_fusion.5
  246.4 1.6 copy.67
  248.0 1.5 bitcast_dynamic-update-slice_fusion.2
  250.1 2.9 constant_dynamic-slice_fusion.5
  253.0 1.6 copy.67
  256.0 30.9 %custom-call.34 = f32[1,3,128,128]{2,3,1,0:T(8,128)} custom-call(f32[1,3,128,128]{3,2,1,0:T(8,128)} %bitcast.181), custom_call_target="InvertDiagBlocksLowerTriangular" | custom-call | tf_op jit(solution)/shard_map/vmap(jit(_solve_triangular))/triangular_solve | solution.py:19
  287.0 2.3 dynamic-slice_reduce_fusion.2
  301.7 360.3 %all-gather = bf16[128,1,3072]{2,1,0:T(2,128)(2,1)S(1)} all-gather(bf16[1,1,3072]{2,1,0:T(2,128)(2,1)S(1)} %reshape.380), channel_id=1, replica_groups=mesh['frame'=8,'seg'=16,'coil'=4] {'frame','seg'}, dimensions={0}, use_global_device_ids=true | all-gather | bytes 792576 | tf_op jit(solution)/shard_map/all_gather | solution.py:76
  663.7 2.1 fusion.5
  667.9 118.3 %reduce-scatter.2.cloned.1.call-done = bf16[1,16,256]{2,1,0:T(8,128)(2,1)} async-done(((bf16[16,16,256]{2,1,0:T(8,128)(2,1)}), bf16[1,16,256]{2,1,0:T(8,128)(2,1)}) %reduce-scatter.2.cloned.1.call-update) | async-done | bytes 8208 | tf_op jit(solution)/shard_map/reduce_scatter | solution.py:89
  786.9 10.4 %psum.7 = f32[1,256]{1,0:T(1,128)S(1)} all-reduce(f32[1,256]{1,0:T(1,128)S(1)} %bitcast.178), channel_id=1, replica_groups=mesh['frame'=8,'seg'=16,'coil'=4] {'coil'}, use_global_device_ids=true, to_apply=%region_10.11 | all-reduce | flops 256 | bytes 2048 | tf_op jit(solution)/shard_map/psum | solution.py:97
  (58 shorter events, 38.0 us)
Async XLA Ops:
  6.5 2.0 copy-start
  6.5 116.2 %all-reduce.4.cloned.1.call-start = ((), (), s32[]{:S(2)}) async-start(), calls=%async_computation.2 | async-start | bytes 4915200
  25.4 760.8 %reduce-scatter.2.cloned.1.call-start = ((), (), s32[]{:S(2)}) async-start(), calls=%async_computation.1 | async-start | bytes 139264 | tf_op jit(solution)/shard_map/reduce_scatter | solution.py:89
  141.8 0.8 copy-start.1
  174.0 0.6 copy-start.2
  235.4 426.6 %copy-start.3 = (s32[1,4]{1,0:T(1,128)S(1)}, s32[1,4]{1,0:T(1,128)}, u32[]{:S(2)}) copy-start(s32[1,4]{1,0:T(1,128)} %param.9) | copy-start | bytes 52
Sparse Core Ops, SparseCore 0:
  25.5 97.2 all-reduce.3
  668.0 118.1 reduce-scatter.1
where the time goes:
time: 807 us; the launch traced here: 805 us
  blocking collectives  371 us (46%)
  waiting for transfers between devices  211 us (26%)
  other arithmetic  120 us (15%)
  local copies, waits for them, and re-layouts  60.9 us (8%)
  matrix products  25.7 us (3%)
  between operations  16.1 us (2%)
    all_gather x1, blocking collectives, on_device(): piece = lax.all_gather(mine, ('frame', 'seg'), axis=0, tiled=True)  360 us
    reduce_scatter x1, waiting for transfers between devices, on_device(): lax.psum_scatter(jnp.einsum('rb,rjc->bjc', hits, contrib, precision=lax.P...  118 us
    unnamed x3, waiting for transfers between devices  92.4 us
    another operation x10, other arithmetic, weights_from(): factor = jnp.linalg.cholesky(system)  67.5 us
    another operation x3, other arithmetic, weights_from(): jax.scipy.linalg.solve_triangular(factor, middle, lower=True, trans=1)  33.5 us
    another operation x15, local copies, waits for them, and re-layouts  19.9 us
  transfers between devices with their start and end apart: 2, of which 2 were waited for; matrix products, arithmetic and copies ran while one was open for 1% of the time, Pallas kernels for 0%

commit v1 on v0

v1 whole, which is shorter than its diff:
```python
import functools

import jax
import jax.numpy as jnp
from jax import lax
from jax.experimental import pallas as pl
from jax.experimental.pallas import tpu as pltpu
from jax.sharding import PartitionSpec as P

regular = 0.02
epsilon = 1e-06
settled = 1e-7
F32 = jnp.float32
BF16 = jnp.bfloat16
LANES = 128
HIGHEST = lax.Precision.HIGHEST


def across_rows(left, right):
    return lax.dot_general(left, right, (((1,), (1,)), ((), ())), preferred_element_type=F32)


def gram_kernel(part, reads_ref, source_ref, target_ref, out_ref):
    coil = lax.axis_index("coil")
    source = source_ref[0]
    depth = source.shape[1]
    width = depth // 2
    row = lax.broadcasted_iota(jnp.int32, (2 * part, depth), 0)
    column = lax.broadcasted_iota(jnp.int32, (2 * part, depth), 1)
    wanted = coil * part + jnp.where(row < part, row, row - part + width)
    pick = jnp.where(column == wanted, 1.0, 0.0).astype(BF16)
    mine = across_rows(pick, source).astype(BF16)
    left = jnp.concatenate([mine, target_ref[0, :, 0, :], target_ref[0, :, 1, :]], axis=0)
    sums = jnp.dot(left, source, preferred_element_type=F32)
    top, bottom = sums[:part], sums[part : 2 * part]
    gram_real = top[:, :width] + bottom[:, width:]
    gram_imag = top[:, width:] - bottom[:, :width]
    across = lax.broadcasted_iota(jnp.int32, (part, width), 1)
    down = lax.broadcasted_iota(jnp.int32, (part, width), 0) + coil * part
    packed = jnp.where(across <= down, gram_real, gram_imag)
    coils = target_ref.shape[1]
    proj_real = sums[2 * part : 2 * part + coils]
    proj_imag = sums[2 * part + coils :]
    rhs_real = proj_real[:, :width] + proj_imag[:, width:]
    rhs_imag = proj_imag[:, :width] - proj_real[:, width:]
    half = part // 2
    out_ref[0, :part] = packed[:, :LANES]
    out_ref[0, part : part + half] = jnp.concatenate(
        [packed[:half, LANES:], packed[half:, LANES:]], axis=1
    )
    base = part + half
    out_ref[0, base : base + coils] = rhs_real[:, :LANES]
    out_ref[0, base + coils : base + 2 * coils] = rhs_imag[:, :LANES]
    out_ref[0, base + 2 * coils : base + 3 * coils] = jnp.concatenate(
        [rhs_real[:, LANES:], rhs_imag[:, LANES:]], axis=1
    )
    lane = lax.broadcasted_iota(jnp.int32, (8, LANES), 1)
    told = jnp.zeros((8, LANES), jnp.int32)
    for slot in range(reads_ref.shape[1]):
        told = jnp.where(lane == slot, reads_ref[0, slot], told)
    out_ref[0, base + 3 * coils :] = told.astype(F32)


def solve_kernel(part, gram_ref, rhs_ref, out_ref, real_ref, imag_ref, sol_ref):
    width = 4 * part
    half = part // 2
    coils = rhs_ref.shape[0] // 3
    pieces = []
    for coil in range(4):
        block = gram_ref[coil]
        tail = block[part:]
        pieces.append(
            jnp.concatenate(
                [block[:part], jnp.concatenate([tail[:, :64], tail[:, 64:]], axis=0)], axis=1
            )
        )
    packed = jnp.concatenate(pieces, axis=0)
    flipped = packed.T
    down = lax.broadcasted_iota(jnp.int32, (width, width), 0)
    across = lax.broadcasted_iota(jnp.int32, (width, width), 1)
    real = jnp.where(across <= down, packed, flipped)
    imag = jnp.where(across > down, packed, jnp.where(across < down, -flipped, 0.0))
    diagonal = jnp.where(across == down, packed, 0.0)
    shift = regular / width * jnp.sum(diagonal)
    high = jnp.sqrt(jnp.sum(real * real + imag * imag)) + shift
    scale = 2.0 / (high + shift)
    real_ref[...] = (real + jnp.where(across == down, shift, 0.0)) * scale
    imag_ref[...] = imag * scale
    rhs_real = jnp.concatenate([rhs_ref[:coils], rhs_ref[2 * coils :, :64]], axis=1)
    rhs_imag = jnp.concatenate([rhs_ref[coils : 2 * coils], rhs_ref[2 * coils :, 64:]], axis=1)
    sol_ref[...] = jnp.concatenate([rhs_real, rhs_imag], axis=0) * scale

    def step(spread):
        square = spread * spread
        factor = 2.0 / (2.0 - square)
        real, imag, sol = real_ref[...], imag_ref[...], sol_ref[...]
        first = jnp.dot(
            jnp.concatenate([real, sol], axis=0), imag, precision=HIGHEST, preferred_element_type=F32
        )
        second = jnp.dot(
            jnp.concatenate([real - imag, sol], axis=0),
            real + imag,
            precision=HIGHEST,
            preferred_element_type=F32,
        )
        cross, thin = first[:width], first[width:]
        turned = cross.T
        by_real = second[width:] - thin
        change = jnp.concatenate(
            [by_real[:coils] + thin[coils:], by_real[coils:] - thin[:coils]], axis=0
        )
        sol_ref[...] = factor * (2.0 * sol - change)
        real_ref[...] = factor * (2.0 * real - (second[:width] - cross - turned))
        imag_ref[...] = factor * (2.0 * imag - (cross - turned))
        return square / (2.0 - square)

    start = (high - shift) / (high + shift)
    lax.while_loop(lambda spread: spread > settled, step, start)
    sol = sol_ref[...]
    weights = jnp.concatenate([sol[:coils], sol[coils:]], axis=1).astype(BF16)
    for copy in range(out_ref.shape[0]):
        out_ref[copy] = weights


def select_kernel(seg_count, x_count, told_ref, piece_ref, out_ref):
    for frame in range(out_ref.shape[0]):
        for slot in range(out_ref.shape[1]):
            out_ref[frame, slot] = piece_ref[told_ref[frame, slot]]


def fill_kernel(reads_ref, places_ref, weights_ref, source_ref, interp_ref, out_ref, grid_ref):
    frames = weights_ref.shape[0]
    grid_ref[...] = jnp.zeros_like(grid_ref)
    for slot in range(weights_ref.shape[1]):
        chosen = weights_ref[lax.rem(reads_ref[0, slot], frames), slot].astype(F32)
        width = chosen.shape[1] // 2
        real, imag = chosen[:, :width], chosen[:, width:]
        matrix = jnp.concatenate(
            [jnp.concatenate([real, -imag], axis=1), jnp.concatenate([imag, real], axis=1)], axis=0
        ).astype(BF16)
        filled = across_rows(matrix, source_ref[0, slot]).astype(BF16)
        place = places_ref[0, slot]
        grid_ref[place] = grid_ref[place] + across_rows(filled, interp_ref[0, slot])
    out_ref[...] = grid_ref[...].astype(BF16)


def on_device(cal_source, cal_target, app_source, readers, blocks, interp):
    frames = lax.axis_size("frame")
    segs = lax.axis_size("seg")
    coil_count = lax.axis_size("coil")
    held, samples, depth = cal_source.shape
    coils = cal_target.shape[1]
    width = depth // 2
    part = width // coil_count
    gram_rows = part + part // 2
    rows = gram_rows + 3 * coils + 8
    slots = readers.shape[1]
    cells = interp.shape[2]

    partial = pl.pallas_call(
        functools.partial(gram_kernel, part),
        grid=(held,),
        in_specs=[
            pl.BlockSpec(memory_space=pltpu.SMEM),
            pl.BlockSpec((1, samples, depth), lambda g: (g, 0, 0)),
            pl.BlockSpec((1, coils, 2, samples), lambda g: (g, 0, 0, 0)),
        ],
        out_specs=pl.BlockSpec((1, rows, LANES), lambda g: (g, 0, 0)),
        out_shape=jax.ShapeDtypeStruct((held, rows, LANES), F32),
    )(readers, cal_source, cal_target)
    received = lax.all_to_all(partial, "frame", 0, 0, tiled=True)
    told = received[:, rows - 8, :slots].astype(jnp.int32) // frames
    owned = jnp.sum(received[:, : rows - 8], axis=0)
    spread = jnp.broadcast_to(owned[None, :gram_rows], (coil_count, gram_rows, LANES))
    gram = lax.all_to_all(spread, "coil", 0, 0, tiled=True)
    weights = pl.pallas_call(
        functools.partial(solve_kernel, part),
        out_shape=jax.ShapeDtypeStruct((segs, coils, depth), BF16),
        scratch_shapes=[
            pltpu.VMEM((width, width), F32),
            pltpu.VMEM((width, width), F32),
            pltpu.VMEM((2 * coils, width), F32),
        ],
    )(gram, owned[gram_rows:])
    pieces = lax.all_to_all(weights, "seg", 0, 0, tiled=True)
    sent = pl.pallas_call(
        functools.partial(select_kernel, segs, 4),
        in_specs=[
            pl.BlockSpec(memory_space=pltpu.SMEM),
            pl.BlockSpec(memory_space=pltpu.VMEM),
        ],
        out_shape=jax.ShapeDtypeStruct((frames, slots, coils, depth), BF16),
    )(told, pieces)
    chosen = lax.all_to_all(sent, "frame", 0, 0, tiled=True)
    grid = pl.pallas_call(
        fill_kernel,
        in_specs=[
            pl.BlockSpec(memory_space=pltpu.SMEM),
            pl.BlockSpec(memory_space=pltpu.SMEM),
            pl.BlockSpec(memory_space=pltpu.VMEM),
            pl.BlockSpec(memory_space=pltpu.VMEM),
            pl.BlockSpec(memory_space=pltpu.VMEM),
        ],
        out_shape=jax.ShapeDtypeStruct((segs, 2 * coils, cells), BF16),
        scratch_shapes=[pltpu.VMEM((segs, 2 * coils, cells), F32)],
    )(readers, blocks, chosen, app_source, interp)
    terms = lax.all_to_all(grid, "seg", 0, 0, tiled=True)
    total = jnp.sum(terms.astype(F32), axis=0)
    power = lax.psum(jnp.sum(total * total, axis=0, keepdims=True), "coil")
    return jnp.sqrt(power + epsilon)


def solution(mesh):
    placed = (
        P("seg", "frame", None),
        P("seg", "coil", None, "frame"),
        P("frame", "seg", None, None),
        P("frame", "seg"),
        P("frame", "seg"),
        P("frame", "seg", None, None),
    )
    return jax.shard_map(
        on_device, mesh=mesh, in_specs=placed, out_specs=P("frame", "seg"), check_vma=False
    )
```

time: 807 us -> 123 us (0.15)
  the two profiles are of different devices: /device:TPU:2 before, /device:TPU:32 now
where the time goes in v1:
time: 123 us
  blocking collectives  61.8 us (50%)
  Pallas kernels  20.4 us (17%)
  waiting for transfers between devices  19.8 us (16%)
  starting transfers between devices  16.8 us (14%)
  local copies, waits for them, and re-layouts  2.55 us (2%)
  other arithmetic  1.25 us (1%)
    all_to_all x1, blocking collectives, on_device(): received = lax.all_to_all(partial, 'frame', 0, 0, tiled=True)  20.2 us
    all_to_all x1, blocking collectives, on_device(): terms = lax.all_to_all(grid, 'seg', 0, 0, tiled=True)  19.9 us
    all_to_all x1, waiting for transfers between devices, on_device(): pieces = lax.all_to_all(weights, 'seg', 0, 0, tiled=True)  14.3 us
    all_to_all x1, starting transfers between devices, on_device(): pieces = lax.all_to_all(weights, 'seg', 0, 0, tiled=True)  13.4 us
    all_to_all x1, blocking collectives, on_device(): chosen = lax.all_to_all(sent, 'frame', 0, 0, tiled=True)  12.8 us
    psum x1, blocking collectives, on_device(): power = lax.psum(jnp.sum(total * total, axis=0, keepdims=True), 'coil')  8.9 us
    pallas_call x1, Pallas kernels, on_device(): pl.pallas_call(functools.partial(gram_kernel, part), grid=(held,), in_spe...  8.2 us
    pallas_call x1, Pallas kernels, on_device(): pl.pallas_call(functools.partial(solve_kernel, part), out_shape=jax.Shape...  7.9 us
  transfers between devices with their start and end apart: 2, of which 2 were waited for; matrix products, arithmetic and copies ran while one was open for 1% of the time, Pallas kernels for 0%

profile of v1, /device:TPU:32, one launch (start us, length us, event | category | flops | bytes accessed | tf_op | source)
XLA Modules:
  0.0 122.6 jit_solution(5705005074557235141)
XLA Ops:
  0.0 8.2 %shard_map.64 = f32[8,104,128]{2,1,0:T(8,128)} custom-call(s32[1,4]{1,0:T(1,128)} %reads_ref.3, bf16[8,576,384]{2,1,0:T(8,128)(2,1)} %source_ref.2, bf16[8,8,2,576]{3,2,1,0:T(2,128)(2,1)} %target_ref.1), custom_call_target="tpu_custom_call" | custom-call | tf_op jit(solution)/shard_map/pallas_call | solution.py:160
  8.2 20.2 %all_to_all.25 = f32[8,104,128]{2,1,0:T(8,128)S(1)} all-to-all(f32[8,104,128]{2,1,0:T(8,128)} %shard_map.64), channel_id=1, replica_groups=mesh['frame'=8,'seg'=16,'coil'=4] {'frame'}, dimensions={0} | all-to-all | bytes 851968 | tf_op jit(solution)/shard_map/all_to_all | solution.py:171
  28.4 0.7 broadcast_in_dim.4
  29.1 3.3 %all-to-all-start.1 = ((f32[4,72,128]{2,1,0:T(8,128)}), f32[4,72,128]{2,1,0:T(8,128)S(1)}, u32[]{:S(2)}, u32[]{:S(2)}) async-start(f32[4,72,128]{2,1,0:T(8,128)} %broadcast_in_dim.4), calls=%async_computation.1 | async-start | bytes 294912 | tf_op jit(solution)/shard_map/all_to_all | solution.py:175
  32.4 0.6 slice.19.rhs_ref
  33.0 5.4 %all-to-all-done.1.gram_ref = f32[4,72,128]{2,1,0:T(8,128)S(1)} async-done(((f32[4,72,128]{2,1,0:T(8,128)}), f32[4,72,128]{2,1,0:T(8,128)S(1)}, u32[]{:S(2)}, u32[]{:S(2)}) %all-to-all-start.1) | async-done | bytes 147488 | tf_op jit(solution)/shard_map/all_to_all | solution.py:175
  38.5 0.0 copy-start
  38.5 0.7 copy-done
  39.1 7.9 %shard_map.65 = bf16[16,8,384]{2,1,0:T(8,128)(2,1)} custom-call(f32[4,72,128]{2,1,0:T(8,128)} %copy-done, f32[24,128]{1,0:T(8,128)} %slice.19.rhs_ref), custom_call_target="tpu_custom_call" | custom-call | tf_op jit(solution)/shard_map/pallas_call | solution.py:176
  47.0 13.4 %all-to-all-start.2 = ((bf16[16,8,384]{2,1,0:T(8,128)(2,1)}), bf16[16,8,384]{2,1,0:T(8,128)(2,1)S(1)}, u32[]{:S(2)}, u32[]{:S(2)}) async-start(bf16[16,8,384]{2,1,0:T(8,128)(2,1)} %shard_map.65), calls=%async_computation.2 | async-start | bytes 196608 | tf_op jit(solution)/shard_map/all_to_all | solution.py:185
  60.5 0.6 add_select_fusion.told_ref
  61.1 14.3 %all-to-all-done.2.piece_ref = bf16[16,8,384]{2,1,0:T(8,128)(2,1)S(1)} async-done(((bf16[16,8,384]{2,1,0:T(8,128)(2,1)}), bf16[16,8,384]{2,1,0:T(8,128)(2,1)S(1)}, u32[]{:S(2)}, u32[]{:S(2)}) %all-to-all-start.2) | async-done | bytes 98336 | tf_op jit(solution)/shard_map/all_to_all | solution.py:185
  75.4 0.0 copy-start.1
  75.4 0.6 copy-done.1
  76.1 1.6 %shard_map.66 = bf16[8,4,8,384]{3,2,1,0:T(8,128)(2,1)} custom-call(s32[8,4]{1,0:T(8,128)} %add_select_fusion.told_ref, bf16[16,8,384]{2,1,0:T(8,128)(2,1)} %copy-done.1), custom_call_target="tpu_custom_call" | custom-call | tf_op jit(solution)/shard_map/pallas_call | solution.py:186
  77.7 12.8 %all_to_all.26.weights_ref = bf16[8,4,8,384]{3,2,1,0:T(8,128)(2,1)} all-to-all(bf16[8,4,8,384]{3,2,1,0:T(8,128)(2,1)} %shard_map.66), channel_id=1, replica_groups=mesh['frame'=8,'seg'=16,'coil'=4] {'frame'}, dimensions={0} | all-to-all | bytes 393216 | tf_op jit(solution)/shard_map/all_to_all | solution.py:194
  90.5 2.7 %shard_map.67 = bf16[16,16,256]{2,1,0:T(8,128)(2,1)} custom-call(s32[1,4]{1,0:T(1,128)} %reads_ref.3, s32[1,4]{1,0:T(1,128)} %places_ref.1, bf16[8,4,8,384]{3,2,1,0:T(8,128)(2,1)} %all_to_all.26.weights_ref, bf16[1,4,128,384]{3,2,1,0:T(8,128)(2,1)} %source_ref.3, bf16[1,4,256,128]{3,2,1,0:T(8,128)(2,1)} %interp_ref.1), custom_call_target="tpu_custom_call" | custom-call | tf_op jit(solution)/shard_map/pallas_call | solution.py:195
  93.2 19.9 %all_to_all.27 = bf16[16,16,256]{2,1,0:T(8,128)(2,1)S(1)} all-to-all(bf16[16,16,256]{2,1,0:T(8,128)(2,1)} %shard_map.67), channel_id=1, replica_groups=mesh['frame'=8,'seg'=16,'coil'=4] {'seg'}, dimensions={0} | all-to-all | bytes 262144 | tf_op jit(solution)/shard_map/all_to_all | solution.py:207
  113.2 8.9 %psum.7 = f32[1,256]{1,0:T(1,128)S(1)} all-reduce(f32[1,256]{1,0:T(1,128)S(1)} %bitcast.3), channel_id=1, replica_groups=mesh['frame'=8,'seg'=16,'coil'=4] {'coil'}, use_global_device_ids=true, to_apply=%region_3.4 | all-reduce | flops 256 | bytes 2048 | tf_op jit(solution)/shard_map/psum | solution.py:209
  122.1 0.6 add_sqrt_fusion
  (5 shorter events, 0.1 us)
Async XLA Ops:
  29.1 9.4 %all-to-all-start.1 = ((f32[4,72,128]{2,1,0:T(8,128)}), f32[4,72,128]{2,1,0:T(8,128)S(1)}, u32[]{:S(2)}, u32[]{:S(2)}) async-start(f32[4,72,128]{2,1,0:T(8,128)} %broadcast_in_dim.4), calls=%async_computation.1 | async-start | bytes 294912 | tf_op jit(solution)/shard_map/all_to_all | solution.py:175
  38.5 0.7 copy-start
  47.0 28.4 %all-to-all-start.2 = ((bf16[16,8,384]{2,1,0:T(8,128)(2,1)}), bf16[16,8,384]{2,1,0:T(8,128)(2,1)S(1)}, u32[]{:S(2)}, u32[]{:S(2)}) async-start(bf16[16,8,384]{2,1,0:T(8,128)(2,1)} %shard_map.65), calls=%async_computation.2 | async-start | bytes 196608 | tf_op jit(solution)/shard_map/all_to_all | solution.py:185
  75.4 0.6 copy-start.1

commit v2 on v1

--- a/solution.py
+++ b/solution.py
@@ -14,13 +14,14 @@
 BF16 = jnp.bfloat16
 LANES = 128
 HIGHEST = lax.Precision.HIGHEST
+SMALL = pltpu.CompilerParams(vmem_limit_bytes=16 * 1024 * 1024)
 
 
 def across_rows(left, right):
     return lax.dot_general(left, right, (((1,), (1,)), ((), ())), preferred_element_type=F32)
 
 
-def gram_kernel(part, reads_ref, source_ref, target_ref, out_ref):
+def gram_kernel(part, frames, reads_ref, source_ref, target_ref, out_ref):
     coil = lax.axis_index("coil")
     source = source_ref[0]
     depth = source.shape[1]
@@ -57,8 +58,19 @@
     lane = lax.broadcasted_iota(jnp.int32, (8, LANES), 1)
     told = jnp.zeros((8, LANES), jnp.int32)
     for slot in range(reads_ref.shape[1]):
-        told = jnp.where(lane == slot, reads_ref[0, slot], told)
+        told = jnp.where(lane == slot, lax.div(reads_ref[0, slot], frames), told)
     out_ref[0, base + 3 * coils :] = told.astype(F32)
+
+
+def sum_kernel(gram_rows, partial_ref, spread_ref, rhs_ref, told_ref):
+    rows = gram_rows + rhs_ref.shape[0]
+    total = partial_ref[0, :rows]
+    for frame in range(1, partial_ref.shape[0]):
+        total = total + partial_ref[frame, :rows]
+    for copy in range(spread_ref.shape[0]):
+        spread_ref[copy] = total[:gram_rows]
+    rhs_ref[...] = total[gram_rows:]
+    told_ref[...] = partial_ref[:, rows, :].astype(jnp.int32)
 
 
 def solve_kernel(part, gram_ref, rhs_ref, out_ref, real_ref, imag_ref, sol_ref):
@@ -122,7 +134,7 @@
         out_ref[copy] = weights
 
 
-def select_kernel(seg_count, x_count, told_ref, piece_ref, out_ref):
+def select_kernel(told_ref, piece_ref, out_ref):
     for frame in range(out_ref.shape[0]):
         for slot in range(out_ref.shape[1]):
             out_ref[frame, slot] = piece_ref[told_ref[frame, slot]]
@@ -158,7 +170,7 @@
     cells = interp.shape[2]
 
     partial = pl.pallas_call(
-        functools.partial(gram_kernel, part),
+        functools.partial(gram_kernel, part, frames),
         grid=(held,),
         in_specs=[
             pl.BlockSpec(memory_space=pltpu.SMEM),
@@ -169,9 +181,15 @@
         out_shape=jax.ShapeDtypeStruct((held, rows, LANES), F32),
     )(readers, cal_source, cal_target)
     received = lax.all_to_all(partial, "frame", 0, 0, tiled=True)
-    told = received[:, rows - 8, :slots].astype(jnp.int32) // frames
-    owned = jnp.sum(received[:, : rows - 8], axis=0)
-    spread = jnp.broadcast_to(owned[None, :gram_rows], (coil_count, gram_rows, LANES))
+    spread, rhs, told = pl.pallas_call(
+        functools.partial(sum_kernel, gram_rows),
+        out_shape=[
+            jax.ShapeDtypeStruct((coil_count, gram_rows, LANES), F32),
+            jax.ShapeDtypeStruct((3 * coils, LANES), F32),
+            jax.ShapeDtypeStruct((frames, LANES), jnp.int32),
+        ],
+        compiler_params=SMALL,
+    )(received)
     gram = lax.all_to_all(spread, "coil", 0, 0, tiled=True)
     weights = pl.pallas_call(
         functools.partial(solve_kernel, part),
@@ -181,15 +199,17 @@
             pltpu.VMEM((width, width), F32),
             pltpu.VMEM((2 * coils, width), F32),
         ],
-    )(gram, owned[gram_rows:])
+        compiler_params=SMALL,
+    )(gram, rhs)
     pieces = lax.all_to_all(weights, "seg", 0, 0, tiled=True)
     sent = pl.pallas_call(
-        functools.partial(select_kernel, segs, 4),
+        select_kernel,
         in_specs=[
             pl.BlockSpec(memory_space=pltpu.SMEM),
             pl.BlockSpec(memory_space=pltpu.VMEM),
         ],
         out_shape=jax.ShapeDtypeStruct((frames, slots, coils, depth), BF16),
+        compiler_params=SMALL,
     )(told, pieces)
     chosen = lax.all_to_all(sent, "frame", 0, 0, tiled=True)
     grid = pl.pallas_call(
@@ -203,6 +223,7 @@
         ],
         out_shape=jax.ShapeDtypeStruct((segs, 2 * coils, cells), BF16),
         scratch_shapes=[pltpu.VMEM((segs, 2 * coils, cells), F32)],
+        compiler_params=SMALL,
     )(readers, blocks, chosen, app_source, interp)
     terms = lax.all_to_all(grid, "seg", 0, 0, tiled=True)
     total = jnp.sum(terms.astype(F32), axis=0)

time: 123 us -> 115 us (0.935)
  the two profiles are of different devices: /device:TPU:32 before, /device:TPU:8 now
where the time goes in v2:
time: 115 us
  blocking collectives  97.3 us (85%)
  Pallas kernels  16.7 us (15%)
    all_to_all x1, blocking collectives, on_device(): pieces = lax.all_to_all(weights, 'seg', 0, 0, tiled=True)  29.2 us
    all_to_all x1, blocking collectives, on_device(): received = lax.all_to_all(partial, 'frame', 0, 0, tiled=True)  19.1 us
    all_to_all x1, blocking collectives, on_device(): terms = lax.all_to_all(grid, 'seg', 0, 0, tiled=True)  18.8 us
    all_to_all x1, blocking collectives, on_device(): chosen = lax.all_to_all(sent, 'frame', 0, 0, tiled=True)  10.7 us
    all_to_all x1, blocking collectives, on_device(): gram = lax.all_to_all(spread, 'coil', 0, 0, tiled=True)  10.2 us
    psum x1, blocking collectives, on_device(): power = lax.psum(jnp.sum(total * total, axis=0, keepdims=True), 'coil')  9.19 us
    pallas_call x1, Pallas kernels, on_device(): pl.pallas_call(functools.partial(gram_kernel, part, frames), grid=(held,)...  8.27 us
    pallas_call x1, Pallas kernels, on_device(): pl.pallas_call(functools.partial(solve_kernel, part), out_shape=jax.Shape...  6.35 us

profile of v2, /device:TPU:8, one launch (start us, length us, event | category | flops | bytes accessed | tf_op | source)
XLA Modules:
  0.0 114.7 jit_solution(12519414057286281446)
XLA Ops:
  0.0 0.0 copy-start.2
  0.0 0.0 copy-start.1
  0.0 0.0 copy-start.3
  0.0 0.0 copy-start
  0.0 8.3 %shard_map.64 = f32[8,104,128]{2,1,0:T(8,128)} custom-call(s32[1,4]{1,0:T(1,128)} %reads_ref.3, bf16[8,576,384]{2,1,0:T(8,128)(2,1)} %source_ref.2, bf16[8,8,2,576]{3,2,1,0:T(2,128)(2,1)} %target_ref.1), custom_call_target="tpu_custom_call" | custom-call | tf_op jit(solution)/shard_map/pallas_call | solution.py:172
  8.3 19.1 %all_to_all.25.partial_ref = f32[8,104,128]{2,1,0:T(8,128)S(1)} all-to-all(f32[8,104,128]{2,1,0:T(8,128)} %shard_map.64), channel_id=1, replica_groups=mesh['frame'=8,'seg'=16,'coil'=4] {'frame'}, dimensions={0} | all-to-all | bytes 851968 | tf_op jit(solution)/shard_map/all_to_all | solution.py:183
  27.5 10.2 %all_to_all.26.gram_ref = f32[4,72,128]{2,1,0:T(8,128)S(1)} all-to-all(f32[4,72,128]{2,1,0:T(8,128)S(1)} %get-tuple-element.9), channel_id=1, replica_groups=mesh['frame'=8,'seg'=16,'coil'=4] {'coil'}, dimensions={0} | all-to-all | bytes 294912 | tf_op jit(solution)/shard_map/all_to_all | solution.py:193
  37.7 6.4 %shard_map.66 = bf16[16,8,384]{2,1,0:T(8,128)(2,1)S(1)} custom-call(f32[4,72,128]{2,1,0:T(8,128)S(1)} %all_to_all.26.gram_ref, f32[24,128]{1,0:T(8,128)S(1)} %get-tuple-element.10.rhs_ref), custom_call_target="tpu_custom_call" | custom-call | tf_op jit(solution)/shard_map/pallas_call | solution.py:194
  44.1 29.2 %all_to_all.27.piece_ref = bf16[16,8,384]{2,1,0:T(8,128)(2,1)S(1)} all-to-all(bf16[16,8,384]{2,1,0:T(8,128)(2,1)S(1)} %shard_map.66), channel_id=1, replica_groups=mesh['frame'=8,'seg'=16,'coil'=4] {'seg'}, dimensions={0} | all-to-all | bytes 196608 | tf_op jit(solution)/shard_map/all_to_all | solution.py:204
  73.2 0.6 shard_map.67
  73.9 10.7 %all_to_all.28.weights_ref = bf16[8,4,8,384]{3,2,1,0:T(8,128)(2,1)S(1)} all-to-all(bf16[8,4,8,384]{3,2,1,0:T(8,128)(2,1)S(1)} %shard_map.67), channel_id=1, replica_groups=mesh['frame'=8,'seg'=16,'coil'=4] {'frame'}, dimensions={0} | all-to-all | bytes 393216 | tf_op jit(solution)/shard_map/all_to_all | solution.py:214
  84.6 0.0 copy-done.2
  84.6 0.0 copy-done.1
  84.6 0.0 copy-done.3
  84.6 0.0 copy-done
  84.6 1.5 %shard_map.68 = bf16[16,16,256]{2,1,0:T(8,128)(2,1)S(1)} custom-call(s32[1,4]{1,0:T(1,128)S(1)} %copy-done.2, s32[1,4]{1,0:T(1,128)S(1)} %copy-done.3, bf16[8,4,8,384]{3,2,1,0:T(8,128)(2,1)S(1)} %all_to_all.28.weights_ref, bf16[1,4,128,384]{3,2,1,0:T(8,128)(2,1)S(1)} %copy-done, bf16[1,4,256,128]{3,2,1,0:T(8,128)(2,1)S(1)} %copy-done.1), custom_call_target="tpu_custom_call" | custom-call | tf_op jit(solution)/shard_map/pallas_call | solution.py:215
  86.1 18.8 %all_to_all.29 = bf16[16,16,256]{2,1,0:T(8,128)(2,1)S(1)} all-to-all(bf16[16,16,256]{2,1,0:T(8,128)(2,1)S(1)} %shard_map.68), channel_id=1, replica_groups=mesh['frame'=8,'seg'=16,'coil'=4] {'seg'}, dimensions={0} | all-to-all | bytes 262144 | tf_op jit(solution)/shard_map/all_to_all | solution.py:228
  104.9 9.2 %psum.7 = f32[1,256]{1,0:T(1,128)S(1)} all-reduce(f32[1,256]{1,0:T(1,128)S(1)} %bitcast.1), channel_id=1, replica_groups=mesh['frame'=8,'seg'=16,'coil'=4] {'coil'}, use_global_device_ids=true, to_apply=%region_2.0 | all-reduce | flops 256 | bytes 2048 | tf_op jit(solution)/shard_map/psum | solution.py:230
  114.1 0.6 add_sqrt_fusion
  (3 shorter events, 0.1 us)
Async XLA Ops:
  0.0 84.6 %copy-start.2 = (s32[1,4]{1,0:T(1,128)S(1)}, s32[1,4]{1,0:T(1,128)}, u32[]{:S(2)}) copy-start(s32[1,4]{1,0:T(1,128)} %reads_ref.3) | copy-start | bytes 52
  0.0 84.6 %copy-start.1 = (bf16[1,4,256,128]{3,2,1,0:T(8,128)(2,1)S(1)}, bf16[1,4,256,128]{3,2,1,0:T(8,128)(2,1)}, u32[]{:S(2)}) copy-start(bf16[1,4,256,128]{3,2,1,0:T(8,128)(2,1)} %interp_ref.1) | copy-start | bytes 786436
  0.0 84.6 %copy-start.3 = (s32[1,4]{1,0:T(1,128)S(1)}, s32[1,4]{1,0:T(1,128)}, u32[]{:S(2)}) copy-start(s32[1,4]{1,0:T(1,128)} %places_ref.1) | copy-start | bytes 52
  0.0 84.6 %copy-start = (bf16[1,4,128,384]{3,2,1,0:T(8,128)(2,1)S(1)}, bf16[1,4,128,384]{3,2,1,0:T(8,128)(2,1)}, u32[]{:S(2)}) copy-start(bf16[1,4,128,384]{3,2,1,0:T(8,128)(2,1)} %source_ref.3) | copy-start | bytes 1179652

commit v3 on v2

--- a/solution.py
+++ b/solution.py
@@ -9,11 +9,10 @@
 
 regular = 0.02
 epsilon = 1e-06
-settled = 1e-7
+settled = 1e-3
 F32 = jnp.float32
 BF16 = jnp.bfloat16
 LANES = 128
-HIGHEST = lax.Precision.HIGHEST
 SMALL = pltpu.CompilerParams(vmem_limit_bytes=16 * 1024 * 1024)
 
 
@@ -21,56 +20,118 @@
     return lax.dot_general(left, right, (((1,), (1,)), ((), ())), preferred_element_type=F32)
 
 
-def gram_kernel(part, frames, reads_ref, source_ref, target_ref, out_ref):
+def pieces_of(value, count):
+    out = []
+    for _ in range(count):
+        piece = value.astype(BF16)
+        value = value - piece.astype(F32)
+        out.append(piece)
+    return out
+
+
+def product(left, right):
+    a, b = pieces_of(left, 2), pieces_of(right, 2)
+    dot = functools.partial(jnp.dot, preferred_element_type=F32)
+    return dot(a[0], b[0]) + (dot(a[1], b[0]) + dot(a[0], b[1]))
+
+
+def fine_product(left, right):
+    a, b = pieces_of(left, 3), pieces_of(right, 3)
+    dot = functools.partial(jnp.dot, preferred_element_type=F32)
+    return dot(a[0], b[0]) + (
+        (dot(a[0], b[1]) + dot(a[1], b[0]))
+        + (dot(a[1], b[1]) + (dot(a[0], b[2]) + dot(a[2], b[0])))
+    )
+
+
+def gram_kernel(
+    part, frames, reads_ref, source_ref, target_ref, send_ref, keep_ref, held_ref, goal_ref, turned_ref, sem
+):
     coil = lax.axis_index("coil")
-    source = source_ref[0]
-    depth = source.shape[1]
+    core = lax.rem(lax.axis_index("frame"), 2)
+    count, depth, samples = turned_ref.shape
     width = depth // 2
-    row = lax.broadcasted_iota(jnp.int32, (2 * part, depth), 0)
-    column = lax.broadcasted_iota(jnp.int32, (2 * part, depth), 1)
-    wanted = coil * part + jnp.where(row < part, row, row - part + width)
-    pick = jnp.where(column == wanted, 1.0, 0.0).astype(BF16)
-    mine = across_rows(pick, source).astype(BF16)
-    left = jnp.concatenate([mine, target_ref[0, :, 0, :], target_ref[0, :, 1, :]], axis=0)
-    sums = jnp.dot(left, source, preferred_element_type=F32)
-    top, bottom = sums[:part], sums[part : 2 * part]
-    gram_real = top[:, :width] + bottom[:, width:]
-    gram_imag = top[:, width:] - bottom[:, :width]
+    half = part // 2
+    coils = target_ref.shape[1]
+    each = count // 2
+    copies = []
+    for slot in range(count):
+        segment = 2 * (slot % each) + (1 - core if slot < each else core)
+        copies.append(
+            (
+                pltpu.make_async_copy(source_ref.at[segment], held_ref.at[slot], sem.at[0, slot]),
+                pltpu.make_async_copy(target_ref.at[segment], goal_ref.at[slot], sem.at[1, slot]),
+            )
+        )
+    for pair in copies:
+        for copy in pair:
+            copy.start()
+    row = lax.broadcasted_iota(jnp.int32, (8, LANES), 0)
+    lane = lax.broadcasted_iota(jnp.int32, (8, LANES), 1)
+    told = jnp.zeros((8, LANES), jnp.int32)
+    for place in range(reads_ref.shape[1]):
+        told = jnp.where((row == core) & (lane == place), lax.div(reads_ref[0, place], frames), told)
+    told = told.astype(F32)
     across = lax.broadcasted_iota(jnp.int32, (part, width), 1)
     down = lax.broadcasted_iota(jnp.int32, (part, width), 0) + coil * part
-    packed = jnp.where(across <= down, gram_real, gram_imag)
-    coils = target_ref.shape[1]
-    proj_real = sums[2 * part : 2 * part + coils]
-    proj_imag = sums[2 * part + coils :]
-    rhs_real = proj_real[:, :width] + proj_imag[:, width:]
-    rhs_imag = proj_imag[:, :width] - proj_real[:, width:]
-    half = part // 2
-    out_ref[0, :part] = packed[:, :LANES]
-    out_ref[0, part : part + half] = jnp.concatenate(
-        [packed[:half, LANES:], packed[half:, LANES:]], axis=1
-    )
-    base = part + half
-    out_ref[0, base : base + coils] = rhs_real[:, :LANES]
-    out_ref[0, base + coils : base + 2 * coils] = rhs_imag[:, :LANES]
-    out_ref[0, base + 2 * coils : base + 3 * coils] = jnp.concatenate(
-        [rhs_real[:, LANES:], rhs_imag[:, LANES:]], axis=1
-    )
-    lane = lax.broadcasted_iota(jnp.int32, (8, LANES), 1)
-    told = jnp.zeros((8, LANES), jnp.int32)
-    for slot in range(reads_ref.shape[1]):
-        told = jnp.where(lane == slot, lax.div(reads_ref[0, slot], frames), told)
-    out_ref[0, base + 3 * coils :] = told.astype(F32)
+    first = pl.multiple_of(coil * part, 16)
+    second = pl.multiple_of(width + coil * part, 16)
+    for group in range(2):
+        slots = range(group * each, (group + 1) * each)
+        for slot in slots:
+            for copy in copies[slot]:
+                copy.wait()
+        lefts = []
+        for slot in slots:
+            turned_ref[slot] = held_ref[slot].T
+            lefts.append(
+                jnp.concatenate(
+                    [
+                        turned_ref[slot, pl.ds(first, part)],
+                        turned_ref[slot, pl.ds(second, part)],
+                        goal_ref[slot, :, 0, :],
+                        goal_ref[slot, :, 1, :],
+                    ],
+                    axis=0,
+                )
+            )
+        products = [
+            jnp.dot(left, held_ref[slot], preferred_element_type=F32)
+            for left, slot in zip(lefts, slots)
+        ]
+        for slot, sums in zip(slots, products):
+            out = (send_ref if group == 0 else keep_ref).at[slot % each]
+            top, bottom = sums[:part], sums[part : 2 * part]
+            gram_real = top[:, :width] + bottom[:, width:]
+            gram_imag = top[:, width:] - bottom[:, :width]
+            packed = jnp.where(across <= down, gram_real, gram_imag)
+            proj_real = sums[2 * part : 2 * part + coils]
+            proj_imag = sums[2 * part + coils :]
+            rhs_real = proj_real[:, :width] + proj_imag[:, width:]
+            rhs_imag = proj_imag[:, :width] - proj_real[:, width:]
+            out[:part] = packed[:, :LANES]
+            out[part : part + half] = jnp.concatenate(
+                [packed[:half, LANES:], packed[half:, LANES:]], axis=1
+            )
+            base = part + half
+            out[base : base + coils] = rhs_real[:, :LANES]
+            out[base + coils : base + 2 * coils] = rhs_imag[:, :LANES]
+            out[base + 2 * coils : base + 3 * coils] = jnp.concatenate(
+                [rhs_real[:, LANES:], rhs_imag[:, LANES:]], axis=1
+            )
+            out[base + 3 * coils :] = told
 
 
 def sum_kernel(gram_rows, partial_ref, spread_ref, rhs_ref, told_ref):
     rows = gram_rows + rhs_ref.shape[0]
     total = partial_ref[0, :rows]
-    for frame in range(1, partial_ref.shape[0]):
-        total = total + partial_ref[frame, :rows]
+    for chip in range(1, partial_ref.shape[0]):
+        total = total + partial_ref[chip, :rows]
     for copy in range(spread_ref.shape[0]):
         spread_ref[copy] = total[:gram_rows]
     rhs_ref[...] = total[gram_rows:]
-    told_ref[...] = partial_ref[:, rows, :].astype(jnp.int32)
+    for chip in range(partial_ref.shape[0]):
+        told_ref[2 * chip : 2 * chip + 2] = partial_ref[chip, rows : rows + 2].astype(jnp.int32)
 
 
 def solve_kernel(part, gram_ref, rhs_ref, out_ref, real_ref, imag_ref, sol_ref):
@@ -102,19 +163,12 @@
     rhs_imag = jnp.concatenate([rhs_ref[coils : 2 * coils], rhs_ref[2 * coils :, 64:]], axis=1)
     sol_ref[...] = jnp.concatenate([rhs_real, rhs_imag], axis=0) * scale
 
-    def step(spread):
+    def step(product, spread):
         square = spread * spread
         factor = 2.0 / (2.0 - square)
         real, imag, sol = real_ref[...], imag_ref[...], sol_ref[...]
-        first = jnp.dot(
-            jnp.concatenate([real, sol], axis=0), imag, precision=HIGHEST, preferred_element_type=F32
-        )
-        second = jnp.dot(
-            jnp.concatenate([real - imag, sol], axis=0),
-            real + imag,
-            precision=HIGHEST,
-            preferred_element_type=F32,
-        )
+        first = product(jnp.concatenate([real, sol], axis=0), imag)
+        second = product(jnp.concatenate([real - imag, sol], axis=0), real + imag)
         cross, thin = first[:width], first[width:]
         turned = cross.T
         by_real = second[width:] - thin
@@ -126,9 +180,21 @@
         imag_ref[...] = factor * (2.0 * imag - (cross - turned))
         return square / (2.0 - square)
 
-    start = (high - shift) / (high + shift)
-    lax.while_loop(lambda spread: spread > settled, step, start)
+    spread = (high - shift) / (high + shift)
+    spread = lax.while_loop(
+        lambda spread: spread > 0.9, functools.partial(step, fine_product), spread
+    )
+    spread = lax.while_loop(
+        lambda spread: spread > settled, functools.partial(step, product), spread
+    )
+    square = spread * spread
     sol = sol_ref[...]
+    by_real = product(sol, real_ref[...])
+    by_imag = product(sol, imag_ref[...])
+    change = jnp.concatenate(
+        [by_real[:coils] + by_imag[coils:], by_real[coils:] - by_imag[:coils]], axis=0
+    )
+    sol = 2.0 / (2.0 - square) * (2.0 * sol - change)
     weights = jnp.concatenate([sol[:coils], sol[coils:]], axis=1).astype(BF16)
     for copy in range(out_ref.shape[0]):
         out_ref[copy] = weights
@@ -169,18 +235,29 @@
     slots = readers.shape[1]
     cells = interp.shape[2]
 
-    partial = pl.pallas_call(
+    each = held // 2
+    block = jax.ShapeDtypeStruct((each, rows, LANES), F32)
+    send, keep = pl.pallas_call(
         functools.partial(gram_kernel, part, frames),
-        grid=(held,),
         in_specs=[
             pl.BlockSpec(memory_space=pltpu.SMEM),
-            pl.BlockSpec((1, samples, depth), lambda g: (g, 0, 0)),
-            pl.BlockSpec((1, coils, 2, samples), lambda g: (g, 0, 0, 0)),
-        ],
-        out_specs=pl.BlockSpec((1, rows, LANES), lambda g: (g, 0, 0)),
-        out_shape=jax.ShapeDtypeStruct((held, rows, LANES), F32),
+            pl.BlockSpec(memory_space=pl.ANY),
+            pl.BlockSpec(memory_space=pl.ANY),
+        ],
+        out_shape=[block, block],
+        scratch_shapes=[
+            pltpu.VMEM((held, samples, depth), BF16),
+            pltpu.VMEM((held, coils, 2, samples), BF16),
+            pltpu.VMEM((held, depth, samples), BF16),
+            pltpu.SemaphoreType.DMA((2, held)),
+        ],
+        compiler_params=pltpu.CompilerParams(vmem_limit_bytes=32 * 1024 * 1024),
     )(readers, cal_source, cal_target)
-    received = lax.all_to_all(partial, "frame", 0, 0, tiled=True)
+    other = lax.ppermute(send, "frame", [(frame, frame ^ 1) for frame in range(frames)])
+    chips = [[2 * chip + core for chip in range(frames // 2)] for core in range(2)]
+    received = lax.all_to_all(
+        keep + other, "frame", 0, 0, tiled=True, axis_index_groups=chips
+    )
     spread, rhs, told = pl.pallas_call(
         functools.partial(sum_kernel, gram_rows),
         out_shape=[

time: 115 us -> 112 us (0.974)
  the two profiles are of different devices: /device:TPU:8 before, /device:TPU:32 now
where the time goes in v3:
time: 112 us
  blocking collectives  91.7 us (82%)
  Pallas kernels  12.5 us (11%)
  local copies, waits for them, and re-layouts  3.58 us (3%)
  starting transfers between devices  1.92 us (2%)
  waiting for transfers between devices  1.43 us (1%)
    all_to_all x1, blocking collectives, on_device(): pieces = lax.all_to_all(weights, 'seg', 0, 0, tiled=True)  29.9 us
    all_to_all x1, blocking collectives, on_device(): terms = lax.all_to_all(grid, 'seg', 0, 0, tiled=True)  19.2 us
    all_to_all x1, blocking collectives, on_device(): lax.all_to_all(keep + other, 'frame', 0, 0, tiled=True, axis_index_groups...  14.6 us
    all_to_all x1, blocking collectives, on_device(): chosen = lax.all_to_all(sent, 'frame', 0, 0, tiled=True)  10.7 us
    psum x1, blocking collectives, on_device(): power = lax.psum(jnp.sum(total * total, axis=0, keepdims=True), 'coil')  8.9 us
    all_to_all x1, blocking collectives, on_device(): gram = lax.all_to_all(spread, 'coil', 0, 0, tiled=True)  8.41 us
    pallas_call x1, Pallas kernels, on_device(): pl.pallas_call(functools.partial(gram_kernel, part, frames), in_specs=[pl...  5.52 us
    pallas_call x1, Pallas kernels, on_device(): pl.pallas_call(functools.partial(solve_kernel, part), out_shape=jax.Shape...  4.9 us
  transfers between devices with their start and end apart: 1, of which 1 were waited for; matrix products, arithmetic and copies ran while one was open for 0% of the time, Pallas kernels for 0%

profile of v3, /device:TPU:32, one launch (start us, length us, event | category | flops | bytes accessed | tf_op | source)
XLA Modules:
  0.0 111.8 jit_solution(3926537396315017287)
XLA Ops:
  0.0 0.0 copy-start
  0.0 2.0 %copy-done = bf16[8,576,384]{2,1,0:T(8,128)(2,1)S(1)} copy-done((bf16[8,576,384]{2,1,0:T(8,128)(2,1)S(1)}, bf16[8,576,384]{2,1,0:T(8,128)(2,1)}, u32[]{:S(2)}) %copy-start) | copy-done | bytes 3538968
  2.0 0.0 copy-start.3
  2.0 0.9 copy-done.3
  2.9 0.0 copy-start.4
  2.9 0.7 copy-done.4
  3.6 0.0 copy-start.1
  3.6 0.0 copy-start.2
  3.6 0.0 copy-start.5
  3.6 5.5 %shard_map.64 = (f32[4,104,128]{2,1,0:T(8,128)S(1)}, f32[4,104,128]{2,1,0:T(8,128)S(1)}) custom-call(s32[1,4]{1,0:T(1,128)S(1)} %copy-done.4, bf16[8,576,384]{2,1,0:T(8,128)(2,1)S(1)} %copy-done, bf16[8,8,2,576]{3,2,1,0:T(2,128)(2,1)S(1)} %copy-done.3), custom_call_target="tpu_custom_call" | custom-call | tf_op jit(solution)/shard_map/pallas_call | solution.py:240
  9.1 1.9 %collective-permute-start = (f32[4,104,128]{2,1,0:T(8,128)S(1)}, f32[4,104,128]{2,1,0:T(8,128)S(1)}, u32[]{:S(2)}, u32[]{:S(2)}) collective-permute-start(f32[4,104,128]{2,1,0:T(8,128)S(1)} %get-tuple-element.11), channel_id=1, source_target_pairs={{0,64},{64,0},{128,192},{192,128},{256,320},{320,256},{384,448},{4... | collective-permute-start | bytes 638984 | tf_op jit(solution)/shard_map/ppermute | solution.py:256
  11.0 1.4 %collective-permute-done = f32[4,104,128]{2,1,0:T(8,128)S(1)} collective-permute-done((f32[4,104,128]{2,1,0:T(8,128)S(1)}, f32[4,104,128]{2,1,0:T(8,128)S(1)}, u32[]{:S(2)}, u32[]{:S(2)}) %collective-permute-start) | collective-permute-done | bytes 213024 | tf_op jit(solution)/shard_map/ppermute | solution.py:256
  12.5 14.6 %all_to_all.25.partial_ref = f32[4,104,128]{2,1,0:T(8,128)S(1)} all-to-all(f32[4,104,128]{2,1,0:T(8,128)S(1)} %add.11), channel_id=1, replica_groups={{0,128,256,384},{64,192,320,448},{1,129,257,385},{65,193,321,449},{2,13..., dimensions={0} | all-to-all | bytes 425984 | tf_op jit(solution)/shard_map/all_to_all | solution.py:258
  27.1 8.4 %all_to_all.26.gram_ref = f32[4,72,128]{2,1,0:T(8,128)S(1)} all-to-all(f32[4,72,128]{2,1,0:T(8,128)S(1)} %get-tuple-element.13), channel_id=1, replica_groups=mesh['frame'=8,'seg'=16,'coil'=4] {'coil'}, dimensions={0} | all-to-all | bytes 294912 | tf_op jit(solution)/shard_map/all_to_all | solution.py:270
  35.5 4.9 %shard_map.66 = bf16[16,8,384]{2,1,0:T(8,128)(2,1)S(1)} custom-call(f32[4,72,128]{2,1,0:T(8,128)S(1)} %all_to_all.26.gram_ref, f32[24,128]{1,0:T(8,128)S(1)} %get-tuple-element.14.rhs_ref), custom_call_target="tpu_custom_call" | custom-call | tf_op jit(solution)/shard_map/pallas_call | solution.py:271
  40.4 29.9 %all_to_all.27.piece_ref = bf16[16,8,384]{2,1,0:T(8,128)(2,1)S(1)} all-to-all(bf16[16,8,384]{2,1,0:T(8,128)(2,1)S(1)} %shard_map.66), channel_id=1, replica_groups=mesh['frame'=8,'seg'=16,'coil'=4] {'seg'}, dimensions={0} | all-to-all | bytes 196608 | tf_op jit(solution)/shard_map/all_to_all | solution.py:281
  70.3 0.6 shard_map.67
  70.9 10.7 %all_to_all.28.weights_ref = bf16[8,4,8,384]{3,2,1,0:T(8,128)(2,1)S(1)} all-to-all(bf16[8,4,8,384]{3,2,1,0:T(8,128)(2,1)S(1)} %shard_map.67), channel_id=1, replica_groups=mesh['frame'=8,'seg'=16,'coil'=4] {'frame'}, dimensions={0} | all-to-all | bytes 393216 | tf_op jit(solution)/shard_map/all_to_all | solution.py:291
  81.6 0.0 copy-done.1
  81.6 0.0 copy-done.2
  81.6 0.0 copy-done.5
  81.6 1.5 %shard_map.68 = bf16[16,16,256]{2,1,0:T(8,128)(2,1)S(1)} custom-call(s32[1,4]{1,0:T(1,128)S(1)} %copy-done.4, s32[1,4]{1,0:T(1,128)S(1)} %copy-done.5, bf16[8,4,8,384]{3,2,1,0:T(8,128)(2,1)S(1)} %all_to_all.28.weights_ref, bf16[1,4,128,384]{3,2,1,0:T(8,128)(2,1)S(1)} %copy-done.1, bf16[1,4,256,128]{3,2,1,0:T(8,128)(2,1)S(1)} %copy-done.2), custom_call_target="tpu_custom_call" | custom-call | tf_op jit(solution)/shard_map/pallas_call | solution.py:292
  83.1 19.2 %all_to_all.29 = bf16[16,16,256]{2,1,0:T(8,128)(2,1)S(1)} all-to-all(bf16[16,16,256]{2,1,0:T(8,128)(2,1)S(1)} %shard_map.68), channel_id=1, replica_groups=mesh['frame'=8,'seg'=16,'coil'=4] {'seg'}, dimensions={0} | all-to-all | bytes 262144 | tf_op jit(solution)/shard_map/all_to_all | solution.py:305
  102.4 8.9 %psum.7 = f32[1,256]{1,0:T(1,128)S(1)} all-reduce(f32[1,256]{1,0:T(1,128)S(1)} %bitcast.1), channel_id=1, replica_groups=mesh['frame'=8,'seg'=16,'coil'=4] {'coil'}, use_global_device_ids=true, to_apply=%region_2.0 | all-reduce | flops 256 | bytes 2048 | tf_op jit(solution)/shard_map/psum | solution.py:307
  111.3 0.6 add_sqrt_fusion
  (4 shorter events, 0.1 us)
Async XLA Ops:
  0.0 2.0 %copy-start = (bf16[8,576,384]{2,1,0:T(8,128)(2,1)S(1)}, bf16[8,576,384]{2,1,0:T(8,128)(2,1)}, u32[]{:S(2)}) copy-start(bf16[8,576,384]{2,1,0:T(8,128)(2,1)} %source_ref.2) | copy-start | bytes 10616836
  2.0 0.9 copy-start.3
  2.9 0.7 copy-start.4
  3.6 78.1 %copy-start.1 = (bf16[1,4,128,384]{3,2,1,0:T(8,128)(2,1)S(1)}, bf16[1,4,128,384]{3,2,1,0:T(8,128)(2,1)}, u32[]{:S(2)}) copy-start(bf16[1,4,128,384]{3,2,1,0:T(8,128)(2,1)} %source_ref.3) | copy-start | bytes 1179652
  3.6 78.1 %copy-start.2 = (bf16[1,4,256,128]{3,2,1,0:T(8,128)(2,1)S(1)}, bf16[1,4,256,128]{3,2,1,0:T(8,128)(2,1)}, u32[]{:S(2)}) copy-start(bf16[1,4,256,128]{3,2,1,0:T(8,128)(2,1)} %interp_ref.1) | copy-start | bytes 786436
  3.6 78.1 %copy-start.5 = (s32[1,4]{1,0:T(1,128)S(1)}, s32[1,4]{1,0:T(1,128)}, u32[]{:S(2)}) copy-start(s32[1,4]{1,0:T(1,128)} %places_ref.1) | copy-start | bytes 52
  9.1 3.4 %collective-permute-start = (f32[4,104,128]{2,1,0:T(8,128)S(1)}, f32[4,104,128]{2,1,0:T(8,128)S(1)}, u32[]{:S(2)}, u32[]{:S(2)}) collective-permute-start(f32[4,104,128]{2,1,0:T(8,128)S(1)} %get-tuple-element.11), channel_id=1, source_target_pairs={{0,64},{64,0},{128,192},{192,128},{256,320},{320,256},{384,448},{4... | collective-permute-start | bytes 638984 | tf_op jit(solution)/shard_map/ppermute | solution.py:256

commit v4 on v3

--- a/solution.py
+++ b/solution.py
@@ -13,6 +13,8 @@
 F32 = jnp.float32
 BF16 = jnp.bfloat16
 LANES = 128
+GROUPS = ((0, 1), (2, 3))
+GRANT = 60 * 1024 * 1024
 SMALL = pltpu.CompilerParams(vmem_limit_bytes=16 * 1024 * 1024)
 
 
@@ -45,7 +47,7 @@
 
 
 def gram_kernel(
-    part, frames, reads_ref, source_ref, target_ref, send_ref, keep_ref, held_ref, goal_ref, turned_ref, sem
+    part, frames, kept, reads_ref, source_ref, target_ref, out_ref, held_ref, goal_ref, turned_ref, sem
 ):
     coil = lax.axis_index("coil")
     core = lax.rem(lax.axis_index("frame"), 2)
@@ -53,10 +55,9 @@
     width = depth // 2
     half = part // 2
     coils = target_ref.shape[1]
-    each = count // 2
     copies = []
     for slot in range(count):
-        segment = 2 * (slot % each) + (1 - core if slot < each else core)
+        segment = 2 * slot + (core if kept else 1 - core)
         copies.append(
             (
                 pltpu.make_async_copy(source_ref.at[segment], held_ref.at[slot], sem.at[0, slot]),
@@ -76,8 +77,8 @@
     down = lax.broadcasted_iota(jnp.int32, (part, width), 0) + coil * part
     first = pl.multiple_of(coil * part, 16)
     second = pl.multiple_of(width + coil * part, 16)
-    for group in range(2):
-        slots = range(group * each, (group + 1) * each)
+    for group in GROUPS:
+        slots = [slot for slot in group if slot < count]
         for slot in slots:
             for copy in copies[slot]:
                 copy.wait()
@@ -100,7 +101,7 @@
             for left, slot in zip(lefts, slots)
         ]
         for slot, sums in zip(slots, products):
-            out = (send_ref if group == 0 else keep_ref).at[slot % each]
+            out = out_ref.at[slot]
             top, bottom = sums[:part], sums[part : 2 * part]
             gram_real = top[:, :width] + bottom[:, width:]
             gram_imag = top[:, width:] - bottom[:, :width]
@@ -236,23 +237,31 @@
     cells = interp.shape[2]
 
     each = held // 2
-    block = jax.ShapeDtypeStruct((each, rows, LANES), F32)
-    send, keep = pl.pallas_call(
-        functools.partial(gram_kernel, part, frames),
-        in_specs=[
-            pl.BlockSpec(memory_space=pltpu.SMEM),
-            pl.BlockSpec(memory_space=pl.ANY),
-            pl.BlockSpec(memory_space=pl.ANY),
-        ],
-        out_shape=[block, block],
-        scratch_shapes=[
-            pltpu.VMEM((held, samples, depth), BF16),
-            pltpu.VMEM((held, coils, 2, samples), BF16),
-            pltpu.VMEM((held, depth, samples), BF16),
-            pltpu.SemaphoreType.DMA((2, held)),
-        ],
-        compiler_params=pltpu.CompilerParams(vmem_limit_bytes=32 * 1024 * 1024),
-    )(readers, cal_source, cal_target)
+    partials = [
+        pl.pallas_call(
+            functools.partial(gram_kernel, part, frames, kept),
+            in_specs=[
+                pl.BlockSpec(memory_space=pltpu.SMEM),
+                pl.BlockSpec(memory_space=pl.ANY),
+                pl.BlockSpec(memory_space=pl.ANY),
+            ],
+            out_shape=jax.ShapeDtypeStruct((each, rows, LANES), F32),
+            scratch_shapes=[
+                pltpu.VMEM((each, samples, depth), BF16),
+                pltpu.VMEM((each, coils, 2, samples), BF16),
+                pltpu.VMEM((each, depth, samples), BF16),
+                pltpu.SemaphoreType.DMA((2, each)),
+            ],
+            compiler_params=pltpu.CompilerParams(vmem_limit_bytes=GRANT),
+            cost_estimate=pl.CostEstimate(
+                flops=2 * each * samples * depth * (2 * part + 2 * coils),
+                bytes_accessed=2 * each * samples * (depth + 2 * coils),
+                transcendentals=0,
+            ),
+        )(readers, cal_source, cal_target)
+        for kept in (False, True)
+    ]
+    send, keep = partials
     other = lax.ppermute(send, "frame", [(frame, frame ^ 1) for frame in range(frames)])
     chips = [[2 * chip + core for chip in range(frames // 2)] for core in range(2)]
     received = lax.all_to_all(

time: 112 us -> 112 us (level)
  local copies, waits for them, and re-layouts: 3.58 us -> 0.03 us
  Pallas kernels: 12.5 us -> 15.4 us
  waiting for transfers between devices: 1.43 us -> 0.01 us
    unnamed x12 -> x8, local copies, waits for them, and re-layouts: 3.58 us -> 0.03 us
    pallas_call x1 -> x2, Pallas kernels: 5.52 us -> 8.35 us  [on_device(): pl.pallas_call(functools.partial(gram_kernel, part, frames, kept), in_spe...]
    ppermute x1, waiting for transfers between devices: 1.43 us -> 0.01 us  [on_device(): lax.ppermute(send, 'frame', [(frame, frame ^ 1) for frame in range(frames)])]
  transfers between devices with their start and end apart: 1 -> 1, of which waited for: 1 -> 0; matrix products, arithmetic and copies ran while one was open for 0% -> 0% of each run, Pallas kernels for 0% -> 4%
where the time goes in v4:
time: 112 us; the launch traced here: 111 us
  blocking collectives  92.4 us (82%)
  Pallas kernels  15.4 us (14%)
  starting transfers between devices  2.05 us (2%)
  other arithmetic  1.59 us (1%)
    all_to_all x1, blocking collectives, on_device(): pieces = lax.all_to_all(weights, 'seg', 0, 0, tiled=True)  29.6 us
    all_to_all x1, blocking collectives, on_device(): terms = lax.all_to_all(grid, 'seg', 0, 0, tiled=True)  19.8 us
    all_to_all x1, blocking collectives, on_device(): lax.all_to_all(keep + other, 'frame', 0, 0, tiled=True, axis_index_groups...  14.9 us
    all_to_all x1, blocking collectives, on_device(): chosen = lax.all_to_all(sent, 'frame', 0, 0, tiled=True)  10.7 us
    psum x1, blocking collectives, on_device(): power = lax.psum(jnp.sum(total * total, axis=0, keepdims=True), 'coil')  8.9 us
    all_to_all x1, blocking collectives, on_device(): gram = lax.all_to_all(spread, 'coil', 0, 0, tiled=True)  8.41 us
    pallas_call x2, Pallas kernels, on_device(): pl.pallas_call(functools.partial(gram_kernel, part, frames, kept), in_spe...  8.35 us
    pallas_call x1, Pallas kernels, on_device(): pl.pallas_call(functools.partial(solve_kernel, part), out_shape=jax.Shape...  4.9 us
  transfers between devices with their start and end apart: 1, of which 0 were waited for; matrix products, arithmetic and copies ran while one was open for 0% of the time, Pallas kernels for 4%

profile of v4, /device:TPU:32, one launch (start us, length us, event | category | flops | bytes accessed | tf_op | source)
XLA Modules:
  0.0 111.5 jit_solution(10262145086652156665)
XLA Ops:
  0.0 4.2 %shard_map.65 = f32[4,104,128]{2,1,0:T(8,128)} custom-call(s32[1,4]{1,0:T(1,128)} %reads_ref.5, bf16[8,576,384]{2,1,0:T(8,128)(2,1)} %source_ref.4, bf16[8,8,2,576]{3,2,1,0:T(2,128)(2,1)} %target_ref.3), custom_call_target="tpu_custom_call" | custom-call | flops 198180864 | bytes 1843200 | tf_op jit(solution)/shard_map/pallas_call | solution.py:241
  4.2 0.0 copy-start
  4.2 0.0 copy-start.1
  4.2 0.0 copy-start.2
  4.2 0.0 copy-start.3
  4.3 2.1 %collective-permute-start = (f32[4,104,128]{2,1,0:T(8,128)}, f32[4,104,128]{2,1,0:T(8,128)S(1)}, u32[]{:S(2)}, u32[]{:S(2)}) collective-permute-start(f32[4,104,128]{2,1,0:T(8,128)} %shard_map.65), channel_id=1, source_target_pairs={{0,64},{64,0},{128,192},{192,128},{256,320},{320,256},{384,448},{4... | collective-permute-start | bytes 638984 | tf_op jit(solution)/shard_map/ppermute | solution.py:265
  6.3 4.2 %shard_map.64 = f32[4,104,128]{2,1,0:T(8,128)} custom-call(s32[1,4]{1,0:T(1,128)} %reads_ref.5, bf16[8,576,384]{2,1,0:T(8,128)(2,1)} %source_ref.4, bf16[8,8,2,576]{3,2,1,0:T(2,128)(2,1)} %target_ref.3), custom_call_target="tpu_custom_call" | custom-call | flops 198180864 | bytes 1843200 | tf_op jit(solution)/shard_map/pallas_call | solution.py:241
  10.5 0.0 collective-permute-done
  10.5 1.0 add.11
  11.5 14.9 %all_to_all.25.partial_ref = f32[4,104,128]{2,1,0:T(8,128)S(1)} all-to-all(f32[4,104,128]{2,1,0:T(8,128)S(1)} %add.11), channel_id=1, replica_groups={{0,128,256,384},{64,192,320,448},{1,129,257,385},{65,193,321,449},{2,13..., dimensions={0} | all-to-all | bytes 425984 | tf_op jit(solution)/shard_map/all_to_all | solution.py:267
  26.4 8.4 %all_to_all.26.gram_ref = f32[4,72,128]{2,1,0:T(8,128)S(1)} all-to-all(f32[4,72,128]{2,1,0:T(8,128)S(1)} %get-tuple-element.9), channel_id=1, replica_groups=mesh['frame'=8,'seg'=16,'coil'=4] {'coil'}, dimensions={0} | all-to-all | bytes 294912 | tf_op jit(solution)/shard_map/all_to_all | solution.py:279
  34.8 4.9 %shard_map.67 = bf16[16,8,384]{2,1,0:T(8,128)(2,1)S(1)} custom-call(f32[4,72,128]{2,1,0:T(8,128)S(1)} %all_to_all.26.gram_ref, f32[24,128]{1,0:T(8,128)S(1)} %get-tuple-element.10.rhs_ref), custom_call_target="tpu_custom_call" | custom-call | tf_op jit(solution)/shard_map/pallas_call | solution.py:280
  39.7 29.6 %all_to_all.27.piece_ref = bf16[16,8,384]{2,1,0:T(8,128)(2,1)S(1)} all-to-all(bf16[16,8,384]{2,1,0:T(8,128)(2,1)S(1)} %shard_map.67), channel_id=1, replica_groups=mesh['frame'=8,'seg'=16,'coil'=4] {'seg'}, dimensions={0} | all-to-all | bytes 196608 | tf_op jit(solution)/shard_map/all_to_all | solution.py:290
  69.3 0.6 shard_map.68
  70.0 10.7 %all_to_all.28.weights_ref = bf16[8,4,8,384]{3,2,1,0:T(8,128)(2,1)S(1)} all-to-all(bf16[8,4,8,384]{3,2,1,0:T(8,128)(2,1)S(1)} %shard_map.68), channel_id=1, replica_groups=mesh['frame'=8,'seg'=16,'coil'=4] {'frame'}, dimensions={0} | all-to-all | bytes 393216 | tf_op jit(solution)/shard_map/all_to_all | solution.py:300
  80.7 0.0 copy-done
  80.7 0.0 copy-done.1
  80.7 0.0 copy-done.2
  80.7 0.0 copy-done.3
  80.7 1.5 %shard_map.69 = bf16[16,16,256]{2,1,0:T(8,128)(2,1)S(1)} custom-call(s32[1,4]{1,0:T(1,128)S(1)} %copy-done.2, s32[1,4]{1,0:T(1,128)S(1)} %copy-done.3, bf16[8,4,8,384]{3,2,1,0:T(8,128)(2,1)S(1)} %all_to_all.28.weights_ref, bf16[1,4,128,384]{3,2,1,0:T(8,128)(2,1)S(1)} %copy-done, bf16[1,4,256,128]{3,2,1,0:T(8,128)(2,1)S(1)} %copy-done.1), custom_call_target="tpu_custom_call" | custom-call | tf_op jit(solution)/shard_map/pallas_call | solution.py:301
  82.2 19.8 %all_to_all.29 = bf16[16,16,256]{2,1,0:T(8,128)(2,1)S(1)} all-to-all(bf16[16,16,256]{2,1,0:T(8,128)(2,1)S(1)} %shard_map.69), channel_id=1, replica_groups=mesh['frame'=8,'seg'=16,'coil'=4] {'seg'}, dimensions={0} | all-to-all | bytes 262144 | tf_op jit(solution)/shard_map/all_to_all | solution.py:314
  102.0 8.9 %psum.7 = f32[1,256]{1,0:T(1,128)S(1)} all-reduce(f32[1,256]{1,0:T(1,128)S(1)} %bitcast.1), channel_id=1, replica_groups=mesh['frame'=8,'seg'=16,'coil'=4] {'coil'}, use_global_device_ids=true, to_apply=%region_2.0 | all-reduce | flops 256 | bytes 2048 | tf_op jit(solution)/shard_map/psum | solution.py:316
  110.9 0.6 add_sqrt_fusion
  (3 shorter events, 0.1 us)
Async XLA Ops:
  4.2 76.5 %copy-start = (bf16[1,4,128,384]{3,2,1,0:T(8,128)(2,1)S(1)}, bf16[1,4,128,384]{3,2,1,0:T(8,128)(2,1)}, u32[]{:S(2)}) copy-start(bf16[1,4,128,384]{3,2,1,0:T(8,128)(2,1)} %source_ref.5) | copy-start | bytes 1179652
  4.2 76.5 %copy-start.1 = (bf16[1,4,256,128]{3,2,1,0:T(8,128)(2,1)S(1)}, bf16[1,4,256,128]{3,2,1,0:T(8,128)(2,1)}, u32[]{:S(2)}) copy-start(bf16[1,4,256,128]{3,2,1,0:T(8,128)(2,1)} %interp_ref.1) | copy-start | bytes 786436
  4.2 76.5 %copy-start.2 = (s32[1,4]{1,0:T(1,128)S(1)}, s32[1,4]{1,0:T(1,128)}, u32[]{:S(2)}) copy-start(s32[1,4]{1,0:T(1,128)} %reads_ref.5) | copy-start | bytes 52
  4.2 76.5 %copy-start.3 = (s32[1,4]{1,0:T(1,128)S(1)}, s32[1,4]{1,0:T(1,128)}, u32[]{:S(2)}) copy-start(s32[1,4]{1,0:T(1,128)} %places_ref.1) | copy-start | bytes 52
  4.3 6.2 %collective-permute-start = (f32[4,104,128]{2,1,0:T(8,128)}, f32[4,104,128]{2,1,0:T(8,128)S(1)}, u32[]{:S(2)}, u32[]{:S(2)}) collective-permute-start(f32[4,104,128]{2,1,0:T(8,128)} %shard_map.65), channel_id=1, source_target_pairs={{0,64},{64,0},{128,192},{192,128},{256,320},{320,256},{384,448},{4... | collective-permute-start | bytes 638984 | tf_op jit(solution)/shard_map/ppermute | solution.py:265

commit v5 on v3

--- a/solution.py
+++ b/solution.py
@@ -241,8 +241,8 @@
         functools.partial(gram_kernel, part, frames),
         in_specs=[
             pl.BlockSpec(memory_space=pltpu.SMEM),
-            pl.BlockSpec(memory_space=pl.ANY),
-            pl.BlockSpec(memory_space=pl.ANY),
+            pl.BlockSpec(memory_space=pltpu.HBM),
+            pl.BlockSpec(memory_space=pltpu.HBM),
         ],
         out_shape=[block, block],
         scratch_shapes=[
@@ -251,8 +251,12 @@
             pltpu.VMEM((held, depth, samples), BF16),
             pltpu.SemaphoreType.DMA((2, held)),
         ],
-        compiler_params=pltpu.CompilerParams(vmem_limit_bytes=32 * 1024 * 1024),
-    )(readers, cal_source, cal_target)
+        compiler_params=SMALL,
+    )(
+        pltpu.with_memory_space_constraint(readers, pltpu.HBM),
+        pltpu.with_memory_space_constraint(cal_source, pltpu.HBM),
+        pltpu.with_memory_space_constraint(cal_target, pltpu.HBM),
+    )
     other = lax.ppermute(send, "frame", [(frame, frame ^ 1) for frame in range(frames)])
     chips = [[2 * chip + core for chip in range(frames // 2)] for core in range(2)]
     received = lax.all_to_all(

time: 112 us -> 108 us (0.964)
  local copies, waits for them, and re-layouts: 3.58 us -> 0.02 us
    unnamed x12 -> x8, local copies, waits for them, and re-layouts: 3.58 us -> 0.02 us
where the time goes in v5:
time: 108 us
  blocking collectives  91.7 us (85%)
  Pallas kernels  12 us (11%)
  starting transfers between devices  1.92 us (2%)
  waiting for transfers between devices  1.43 us (1%)
    all_to_all x1, blocking collectives, on_device(): pieces = lax.all_to_all(weights, 'seg', 0, 0, tiled=True)  29.9 us
    all_to_all x1, blocking collectives, on_device(): terms = lax.all_to_all(grid, 'seg', 0, 0, tiled=True)  19.2 us
    all_to_all x1, blocking collectives, on_device(): lax.all_to_all(keep + other, 'frame', 0, 0, tiled=True, axis_index_groups...  14.6 us
    all_to_all x1, blocking collectives, on_device(): chosen = lax.all_to_all(sent, 'frame', 0, 0, tiled=True)  10.7 us
    psum x1, blocking collectives, on_device(): power = lax.psum(jnp.sum(total * total, axis=0, keepdims=True), 'coil')  8.91 us
    all_to_all x1, blocking collectives, on_device(): gram = lax.all_to_all(spread, 'coil', 0, 0, tiled=True)  8.41 us
    pallas_call x1, Pallas kernels, on_device(): pl.pallas_call(functools.partial(gram_kernel, part, frames), in_specs=[pl...  5 us
    pallas_call x1, Pallas kernels, on_device(): pl.pallas_call(functools.partial(solve_kernel, part), out_shape=jax.Shape...  4.9 us
  transfers between devices with their start and end apart: 1, of which 1 were waited for; matrix products, arithmetic and copies ran while one was open for 0% of the time, Pallas kernels for 0%

profile of v5, /device:TPU:32, one launch (start us, length us, event | category | flops | bytes accessed | tf_op | source)
XLA Modules:
  0.0 107.8 jit_solution(10116190609230324919)
XLA Ops:
  0.0 0.0 copy-start.2
  0.0 0.0 copy-start.1
  0.0 0.0 copy-start.3
  0.0 0.0 copy-start
  0.0 5.0 %shard_map.64 = (f32[4,104,128]{2,1,0:T(8,128)S(1)}, f32[4,104,128]{2,1,0:T(8,128)S(1)}) custom-call(s32[1,4]{1,0:T(1,128)} %reads_ref.3, bf16[8,576,384]{2,1,0:T(8,128)(2,1)} %source_ref.2, bf16[8,8,2,576]{3,2,1,0:T(2,128)(2,1)} %target_ref.1), custom_call_target="tpu_custom_call" | custom-call | tf_op jit(solution)/shard_map/pallas_call | solution.py:240
  5.0 1.9 %collective-permute-start = (f32[4,104,128]{2,1,0:T(8,128)S(1)}, f32[4,104,128]{2,1,0:T(8,128)S(1)}, u32[]{:S(2)}, u32[]{:S(2)}) collective-permute-start(f32[4,104,128]{2,1,0:T(8,128)S(1)} %get-tuple-element.11), channel_id=1, source_target_pairs={{0,64},{64,0},{128,192},{192,128},{256,320},{320,256},{384,448},{4... | collective-permute-start | bytes 638984 | tf_op jit(solution)/shard_map/ppermute | solution.py:260
  7.0 1.4 %collective-permute-done = f32[4,104,128]{2,1,0:T(8,128)S(1)} collective-permute-done((f32[4,104,128]{2,1,0:T(8,128)S(1)}, f32[4,104,128]{2,1,0:T(8,128)S(1)}, u32[]{:S(2)}, u32[]{:S(2)}) %collective-permute-start) | collective-permute-done | bytes 213024 | tf_op jit(solution)/shard_map/ppermute | solution.py:260
  8.4 14.6 %all_to_all.25.partial_ref = f32[4,104,128]{2,1,0:T(8,128)S(1)} all-to-all(f32[4,104,128]{2,1,0:T(8,128)S(1)} %add.11), channel_id=1, replica_groups={{0,128,256,384},{64,192,320,448},{1,129,257,385},{65,193,321,449},{2,13..., dimensions={0} | all-to-all | bytes 425984 | tf_op jit(solution)/shard_map/all_to_all | solution.py:262
  23.0 8.4 %all_to_all.26.gram_ref = f32[4,72,128]{2,1,0:T(8,128)S(1)} all-to-all(f32[4,72,128]{2,1,0:T(8,128)S(1)} %get-tuple-element.13), channel_id=1, replica_groups=mesh['frame'=8,'seg'=16,'coil'=4] {'coil'}, dimensions={0} | all-to-all | bytes 294912 | tf_op jit(solution)/shard_map/all_to_all | solution.py:274
  31.4 4.9 %shard_map.66 = bf16[16,8,384]{2,1,0:T(8,128)(2,1)S(1)} custom-call(f32[4,72,128]{2,1,0:T(8,128)S(1)} %all_to_all.26.gram_ref, f32[24,128]{1,0:T(8,128)S(1)} %get-tuple-element.14.rhs_ref), custom_call_target="tpu_custom_call" | custom-call | tf_op jit(solution)/shard_map/pallas_call | solution.py:275
  36.3 29.9 %all_to_all.27.piece_ref = bf16[16,8,384]{2,1,0:T(8,128)(2,1)S(1)} all-to-all(bf16[16,8,384]{2,1,0:T(8,128)(2,1)S(1)} %shard_map.66), channel_id=1, replica_groups=mesh['frame'=8,'seg'=16,'coil'=4] {'seg'}, dimensions={0} | all-to-all | bytes 196608 | tf_op jit(solution)/shard_map/all_to_all | solution.py:285
  66.2 0.6 shard_map.67
  66.8 10.7 %all_to_all.28.weights_ref = bf16[8,4,8,384]{3,2,1,0:T(8,128)(2,1)S(1)} all-to-all(bf16[8,4,8,384]{3,2,1,0:T(8,128)(2,1)S(1)} %shard_map.67), channel_id=1, replica_groups=mesh['frame'=8,'seg'=16,'coil'=4] {'frame'}, dimensions={0} | all-to-all | bytes 393216 | tf_op jit(solution)/shard_map/all_to_all | solution.py:295
  77.6 0.0 copy-done.2
  77.6 0.0 copy-done.1
  77.6 0.0 copy-done.3
  77.6 0.0 copy-done
  77.6 1.5 %shard_map.68 = bf16[16,16,256]{2,1,0:T(8,128)(2,1)S(1)} custom-call(s32[1,4]{1,0:T(1,128)S(1)} %copy-done.2, s32[1,4]{1,0:T(1,128)S(1)} %copy-done.3, bf16[8,4,8,384]{3,2,1,0:T(8,128)(2,1)S(1)} %all_to_all.28.weights_ref, bf16[1,4,128,384]{3,2,1,0:T(8,128)(2,1)S(1)} %copy-done, bf16[1,4,256,128]{3,2,1,0:T(8,128)(2,1)S(1)} %copy-done.1), custom_call_target="tpu_custom_call" | custom-call | tf_op jit(solution)/shard_map/pallas_call | solution.py:296
  79.0 19.2 %all_to_all.29 = bf16[16,16,256]{2,1,0:T(8,128)(2,1)S(1)} all-to-all(bf16[16,16,256]{2,1,0:T(8,128)(2,1)S(1)} %shard_map.68), channel_id=1, replica_groups=mesh['frame'=8,'seg'=16,'coil'=4] {'seg'}, dimensions={0} | all-to-all | bytes 262144 | tf_op jit(solution)/shard_map/all_to_all | solution.py:309
  98.3 8.9 %psum.7 = f32[1,256]{1,0:T(1,128)S(1)} all-reduce(f32[1,256]{1,0:T(1,128)S(1)} %bitcast.1), channel_id=1, replica_groups=mesh['frame'=8,'seg'=16,'coil'=4] {'coil'}, use_global_device_ids=true, to_apply=%region_2.0 | all-reduce | flops 256 | bytes 2048 | tf_op jit(solution)/shard_map/psum | solution.py:311
  107.2 0.6 add_sqrt_fusion
  (4 shorter events, 0.1 us)
Async XLA Ops:
  0.0 77.6 %copy-start.2 = (s32[1,4]{1,0:T(1,128)S(1)}, s32[1,4]{1,0:T(1,128)}, u32[]{:S(2)}) copy-start(s32[1,4]{1,0:T(1,128)} %reads_ref.3) | copy-start | bytes 52
  0.0 77.6 %copy-start.1 = (bf16[1,4,256,128]{3,2,1,0:T(8,128)(2,1)S(1)}, bf16[1,4,256,128]{3,2,1,0:T(8,128)(2,1)}, u32[]{:S(2)}) copy-start(bf16[1,4,256,128]{3,2,1,0:T(8,128)(2,1)} %interp_ref.1) | copy-start | bytes 786436
  0.0 77.6 %copy-start.3 = (s32[1,4]{1,0:T(1,128)S(1)}, s32[1,4]{1,0:T(1,128)}, u32[]{:S(2)}) copy-start(s32[1,4]{1,0:T(1,128)} %places_ref.1) | copy-start | bytes 52
  0.0 77.6 %copy-start = (bf16[1,4,128,384]{3,2,1,0:T(8,128)(2,1)S(1)}, bf16[1,4,128,384]{3,2,1,0:T(8,128)(2,1)}, u32[]{:S(2)}) copy-start(bf16[1,4,128,384]{3,2,1,0:T(8,128)(2,1)} %source_ref.3) | copy-start | bytes 1179652
  5.0 3.4 %collective-permute-start = (f32[4,104,128]{2,1,0:T(8,128)S(1)}, f32[4,104,128]{2,1,0:T(8,128)S(1)}, u32[]{:S(2)}, u32[]{:S(2)}) collective-permute-start(f32[4,104,128]{2,1,0:T(8,128)S(1)} %get-tuple-element.11), channel_id=1, source_target_pairs={{0,64},{64,0},{128,192},{192,128},{256,320},{320,256},{384,448},{4... | collective-permute-start | bytes 638984 | tf_op jit(solution)/shard_map/ppermute | solution.py:260

commit v6 on v5

--- a/solution.py
+++ b/solution.py
@@ -13,6 +13,7 @@
 F32 = jnp.float32
 BF16 = jnp.bfloat16
 LANES = 128
+GROUPS = ((0, 1), (2, 3, 4), (5, 6, 7))
 SMALL = pltpu.CompilerParams(vmem_limit_bytes=16 * 1024 * 1024)
 
 
@@ -76,8 +77,7 @@
     down = lax.broadcasted_iota(jnp.int32, (part, width), 0) + coil * part
     first = pl.multiple_of(coil * part, 16)
     second = pl.multiple_of(width + coil * part, 16)
-    for group in range(2):
-        slots = range(group * each, (group + 1) * each)
+    for slots in GROUPS:
         for slot in slots:
             for copy in copies[slot]:
                 copy.wait()
@@ -100,7 +100,7 @@
             for left, slot in zip(lefts, slots)
         ]
         for slot, sums in zip(slots, products):
-            out = (send_ref if group == 0 else keep_ref).at[slot % each]
+            out = (send_ref if slot < each else keep_ref).at[slot % each]
             top, bottom = sums[:part], sums[part : 2 * part]
             gram_real = top[:, :width] + bottom[:, width:]
             gram_imag = top[:, width:] - bottom[:, :width]
@@ -308,8 +308,8 @@
     )(readers, blocks, chosen, app_source, interp)
     terms = lax.all_to_all(grid, "seg", 0, 0, tiled=True)
     total = jnp.sum(terms.astype(F32), axis=0)
-    power = lax.psum(jnp.sum(total * total, axis=0, keepdims=True), "coil")
-    return jnp.sqrt(power + epsilon)
+    power = lax.all_gather(jnp.sum(total * total, axis=0, keepdims=True), "coil", tiled=True)
+    return jnp.sqrt(jnp.sum(power, axis=0, keepdims=True) + epsilon)
 
 
 def solution(mesh):

time: 108 us -> 107 us (level)
    psum x1 -> x0, blocking collectives: 8.91 us -> none  [on_device(): power = lax.psum(jnp.sum(total * total, axis=0, keepdims=True), 'coil')]
    all_gather x0 -> x1, blocking collectives: none -> 8.13 us  [on_device(): lax.all_gather(jnp.sum(total * total, axis=0, keepdims=True), 'coil', til...]
where the time goes in v6:
time: 107 us
  blocking collectives  90.9 us (85%)
  Pallas kernels  11.9 us (11%)
  starting transfers between devices  1.92 us (2%)
  waiting for transfers between devices  1.43 us (1%)
    all_to_all x1, blocking collectives, on_device(): pieces = lax.all_to_all(weights, 'seg', 0, 0, tiled=True)  29.9 us
    all_to_all x1, blocking collectives, on_device(): terms = lax.all_to_all(grid, 'seg', 0, 0, tiled=True)  19.2 us
    all_to_all x1, blocking collectives, on_device(): lax.all_to_all(keep + other, 'frame', 0, 0, tiled=True, axis_index_groups...  14.5 us
    all_to_all x1, blocking collectives, on_device(): chosen = lax.all_to_all(sent, 'frame', 0, 0, tiled=True)  10.7 us
    all_to_all x1, blocking collectives, on_device(): gram = lax.all_to_all(spread, 'coil', 0, 0, tiled=True)  8.41 us
    all_gather x1, blocking collectives, on_device(): lax.all_gather(jnp.sum(total * total, axis=0, keepdims=True), 'coil', til...  8.13 us
    pallas_call x1, Pallas kernels, on_device(): pl.pallas_call(functools.partial(gram_kernel, part, frames), in_specs=[pl...  4.91 us
    pallas_call x1, Pallas kernels, on_device(): pl.pallas_call(functools.partial(solve_kernel, part), out_shape=jax.Shape...  4.9 us
  transfers between devices with their start and end apart: 1, of which 1 were waited for; matrix products, arithmetic and copies ran while one was open for 0% of the time, Pallas kernels for 0%

profile of v6, /device:TPU:32, one launch (start us, length us, event | category | flops | bytes accessed | tf_op | source)
XLA Modules:
  0.0 106.9 jit_solution(6553534174693191678)
XLA Ops:
  0.0 0.0 copy-start.2
  0.0 0.0 copy-start.1
  0.0 0.0 copy-start.3
  0.0 0.0 copy-start
  0.0 4.9 %shard_map.64 = (f32[4,104,128]{2,1,0:T(8,128)S(1)}, f32[4,104,128]{2,1,0:T(8,128)S(1)}) custom-call(s32[1,4]{1,0:T(1,128)} %reads_ref.3, bf16[8,576,384]{2,1,0:T(8,128)(2,1)} %source_ref.2, bf16[8,8,2,576]{3,2,1,0:T(2,128)(2,1)} %target_ref.1), custom_call_target="tpu_custom_call" | custom-call | tf_op jit(solution)/shard_map/pallas_call | solution.py:240
  4.9 1.9 %collective-permute-start = (f32[4,104,128]{2,1,0:T(8,128)S(1)}, f32[4,104,128]{2,1,0:T(8,128)S(1)}, u32[]{:S(2)}, u32[]{:S(2)}) collective-permute-start(f32[4,104,128]{2,1,0:T(8,128)S(1)} %get-tuple-element.11), channel_id=1, source_target_pairs={{0,64},{64,0},{128,192},{192,128},{256,320},{320,256},{384,448},{4... | collective-permute-start | bytes 638984 | tf_op jit(solution)/shard_map/ppermute | solution.py:260
  6.9 1.4 %collective-permute-done = f32[4,104,128]{2,1,0:T(8,128)S(1)} collective-permute-done((f32[4,104,128]{2,1,0:T(8,128)S(1)}, f32[4,104,128]{2,1,0:T(8,128)S(1)}, u32[]{:S(2)}, u32[]{:S(2)}) %collective-permute-start) | collective-permute-done | bytes 213024 | tf_op jit(solution)/shard_map/ppermute | solution.py:260
  8.3 14.5 %all_to_all.25.partial_ref = f32[4,104,128]{2,1,0:T(8,128)S(1)} all-to-all(f32[4,104,128]{2,1,0:T(8,128)S(1)} %add.18), channel_id=1, replica_groups={{0,128,256,384},{64,192,320,448},{1,129,257,385},{65,193,321,449},{2,13..., dimensions={0} | all-to-all | bytes 425984 | tf_op jit(solution)/shard_map/all_to_all | solution.py:262
  22.9 8.4 %all_to_all.26.gram_ref = f32[4,72,128]{2,1,0:T(8,128)S(1)} all-to-all(f32[4,72,128]{2,1,0:T(8,128)S(1)} %get-tuple-element.13), channel_id=1, replica_groups=mesh['frame'=8,'seg'=16,'coil'=4] {'coil'}, dimensions={0} | all-to-all | bytes 294912 | tf_op jit(solution)/shard_map/all_to_all | solution.py:274
  31.3 4.9 %shard_map.66 = bf16[16,8,384]{2,1,0:T(8,128)(2,1)S(1)} custom-call(f32[4,72,128]{2,1,0:T(8,128)S(1)} %all_to_all.26.gram_ref, f32[24,128]{1,0:T(8,128)S(1)} %get-tuple-element.14.rhs_ref), custom_call_target="tpu_custom_call" | custom-call | tf_op jit(solution)/shard_map/pallas_call | solution.py:275
  36.2 29.9 %all_to_all.27.piece_ref = bf16[16,8,384]{2,1,0:T(8,128)(2,1)S(1)} all-to-all(bf16[16,8,384]{2,1,0:T(8,128)(2,1)S(1)} %shard_map.66), channel_id=1, replica_groups=mesh['frame'=8,'seg'=16,'coil'=4] {'seg'}, dimensions={0} | all-to-all | bytes 196608 | tf_op jit(solution)/shard_map/all_to_all | solution.py:285
  66.1 0.6 shard_map.67
  66.7 10.7 %all_to_all.28.weights_ref = bf16[8,4,8,384]{3,2,1,0:T(8,128)(2,1)S(1)} all-to-all(bf16[8,4,8,384]{3,2,1,0:T(8,128)(2,1)S(1)} %shard_map.67), channel_id=1, replica_groups=mesh['frame'=8,'seg'=16,'coil'=4] {'frame'}, dimensions={0} | all-to-all | bytes 393216 | tf_op jit(solution)/shard_map/all_to_all | solution.py:295
  77.5 0.0 copy-done.2
  77.5 0.0 copy-done.1
  77.5 0.0 copy-done.3
  77.5 0.0 copy-done
  77.5 1.5 %shard_map.68 = bf16[16,16,256]{2,1,0:T(8,128)(2,1)S(1)} custom-call(s32[1,4]{1,0:T(1,128)S(1)} %copy-done.2, s32[1,4]{1,0:T(1,128)S(1)} %copy-done.3, bf16[8,4,8,384]{3,2,1,0:T(8,128)(2,1)S(1)} %all_to_all.28.weights_ref, bf16[1,4,128,384]{3,2,1,0:T(8,128)(2,1)S(1)} %copy-done, bf16[1,4,256,128]{3,2,1,0:T(8,128)(2,1)S(1)} %copy-done.1), custom_call_target="tpu_custom_call" | custom-call | tf_op jit(solution)/shard_map/pallas_call | solution.py:296
  78.9 19.2 %all_to_all.29 = bf16[16,16,256]{2,1,0:T(8,128)(2,1)S(1)} all-to-all(bf16[16,16,256]{2,1,0:T(8,128)(2,1)S(1)} %shard_map.68), channel_id=1, replica_groups=mesh['frame'=8,'seg'=16,'coil'=4] {'seg'}, dimensions={0} | all-to-all | bytes 262144 | tf_op jit(solution)/shard_map/all_to_all | solution.py:309
  98.2 8.1 %all-gather.1 = f32[4,1,256]{2,1,0:T(1,128)S(1)} all-gather(f32[1,1,256]{2,1,0:T(1,128)S(1)} %bitcast.2), channel_id=2, replica_groups=mesh['frame'=8,'seg'=16,'coil'=4] {'coil'}, dimensions={0}, use_global_device_ids=true | all-gather | bytes 5120 | tf_op jit(solution)/shard_map/all_gather | solution.py:311
  106.4 0.6 add_sqrt_fusion
  (5 shorter events, 0.1 us)
Async XLA Ops:
  0.0 77.5 %copy-start.2 = (s32[1,4]{1,0:T(1,128)S(1)}, s32[1,4]{1,0:T(1,128)}, u32[]{:S(2)}) copy-start(s32[1,4]{1,0:T(1,128)} %reads_ref.3) | copy-start | bytes 52
  0.0 77.5 %copy-start.1 = (bf16[1,4,256,128]{3,2,1,0:T(8,128)(2,1)S(1)}, bf16[1,4,256,128]{3,2,1,0:T(8,128)(2,1)}, u32[]{:S(2)}) copy-start(bf16[1,4,256,128]{3,2,1,0:T(8,128)(2,1)} %interp_ref.1) | copy-start | bytes 786436
  0.0 77.5 %copy-start.3 = (s32[1,4]{1,0:T(1,128)S(1)}, s32[1,4]{1,0:T(1,128)}, u32[]{:S(2)}) copy-start(s32[1,4]{1,0:T(1,128)} %places_ref.1) | copy-start | bytes 52
  0.0 77.5 %copy-start = (bf16[1,4,128,384]{3,2,1,0:T(8,128)(2,1)S(1)}, bf16[1,4,128,384]{3,2,1,0:T(8,128)(2,1)}, u32[]{:S(2)}) copy-start(bf16[1,4,128,384]{3,2,1,0:T(8,128)(2,1)} %source_ref.3) | copy-start | bytes 1179652
  4.9 3.4 %collective-permute-start = (f32[4,104,128]{2,1,0:T(8,128)S(1)}, f32[4,104,128]{2,1,0:T(8,128)S(1)}, u32[]{:S(2)}, u32[]{:S(2)}) collective-permute-start(f32[4,104,128]{2,1,0:T(8,128)S(1)} %get-tuple-element.11), channel_id=1, source_target_pairs={{0,64},{64,0},{128,192},{192,128},{256,320},{320,256},{384,448},{4... | collective-permute-start | bytes 638984 | tf_op jit(solution)/shard_map/ppermute | solution.py:260

commit v7 on v6

--- a/solution.py
+++ b/solution.py
@@ -46,13 +46,26 @@
 
 
 def gram_kernel(
-    part, frames, reads_ref, source_ref, target_ref, send_ref, keep_ref, held_ref, goal_ref, turned_ref, sem
+    part,
+    frames,
+    reads_ref,
+    source_ref,
+    target_ref,
+    send_ref,
+    keep_ref,
+    held_ref,
+    goal_ref,
+    turned_ref,
+    read_ref,
+    sem,
+    read_sem,
 ):
     coil = lax.axis_index("coil")
     core = lax.rem(lax.axis_index("frame"), 2)
     count, depth, samples = turned_ref.shape
     width = depth // 2
     half = part // 2
+    base = part + half
     coils = target_ref.shape[1]
     each = count // 2
     copies = []
@@ -67,12 +80,8 @@
     for pair in copies:
         for copy in pair:
             copy.start()
-    row = lax.broadcasted_iota(jnp.int32, (8, LANES), 0)
-    lane = lax.broadcasted_iota(jnp.int32, (8, LANES), 1)
-    told = jnp.zeros((8, LANES), jnp.int32)
-    for place in range(reads_ref.shape[1]):
-        told = jnp.where((row == core) & (lane == place), lax.div(reads_ref[0, place], frames), told)
-    told = told.astype(F32)
+    listing = pltpu.make_async_copy(reads_ref, read_ref, read_sem)
+    listing.start()
     across = lax.broadcasted_iota(jnp.int32, (part, width), 1)
     down = lax.broadcasted_iota(jnp.int32, (part, width), 0) + coil * part
     first = pl.multiple_of(coil * part, 16)
@@ -113,13 +122,21 @@
             out[part : part + half] = jnp.concatenate(
                 [packed[:half, LANES:], packed[half:, LANES:]], axis=1
             )
-            base = part + half
             out[base : base + coils] = rhs_real[:, :LANES]
             out[base + coils : base + 2 * coils] = rhs_imag[:, :LANES]
             out[base + 2 * coils : base + 3 * coils] = jnp.concatenate(
                 [rhs_real[:, LANES:], rhs_imag[:, LANES:]], axis=1
             )
-            out[base + 3 * coils :] = told
+    listing.wait()
+    row = lax.broadcasted_iota(jnp.int32, (8, LANES), 0)
+    lane = lax.broadcasted_iota(jnp.int32, (8, LANES), 1)
+    told = jnp.zeros((8, LANES), jnp.int32)
+    for place in range(read_ref.shape[1]):
+        told = jnp.where((row == core) & (lane == place), lax.div(read_ref[0, place], frames), told)
+    told = told.astype(F32)
+    for slot in range(each):
+        send_ref[slot, base + 3 * coils :] = told
+        keep_ref[slot, base + 3 * coils :] = told
 
 
 def sum_kernel(gram_rows, partial_ref, spread_ref, rhs_ref, told_ref):
@@ -182,7 +199,7 @@
 
     spread = (high - shift) / (high + shift)
     spread = lax.while_loop(
-        lambda spread: spread > 0.9, functools.partial(step, fine_product), spread
+        lambda spread: spread > 0.97, functools.partial(step, fine_product), spread
     )
     spread = lax.while_loop(
         lambda spread: spread > settled, functools.partial(step, product), spread
@@ -206,20 +223,28 @@
             out_ref[frame, slot] = piece_ref[told_ref[frame, slot]]
 
 
-def fill_kernel(reads_ref, places_ref, weights_ref, source_ref, interp_ref, out_ref, grid_ref):
-    frames = weights_ref.shape[0]
-    grid_ref[...] = jnp.zeros_like(grid_ref)
-    for slot in range(weights_ref.shape[1]):
-        chosen = weights_ref[lax.rem(reads_ref[0, slot], frames), slot].astype(F32)
-        width = chosen.shape[1] // 2
+def fill_kernel(reads_ref, places_ref, weights_ref, source_ref, interp_ref, out_ref):
+    frames, slots, coils, depth = weights_ref.shape
+    width = depth // 2
+    terms = []
+    for slot in range(slots):
+        holder = jnp.broadcast_to(reads_ref[:, slot : slot + 1] & (frames - 1), (coils, depth))
+        chosen = weights_ref[0, slot].astype(F32)
+        for frame in range(1, frames):
+            chosen = jnp.where(holder == frame, weights_ref[frame, slot].astype(F32), chosen)
         real, imag = chosen[:, :width], chosen[:, width:]
         matrix = jnp.concatenate(
             [jnp.concatenate([real, -imag], axis=1), jnp.concatenate([imag, real], axis=1)], axis=0
         ).astype(BF16)
         filled = across_rows(matrix, source_ref[0, slot]).astype(BF16)
-        place = places_ref[0, slot]
-        grid_ref[place] = grid_ref[place] + across_rows(filled, interp_ref[0, slot])
-    out_ref[...] = grid_ref[...].astype(BF16)
+        terms.append(across_rows(filled, interp_ref[0, slot]))
+    shape = terms[0].shape
+    places = [jnp.broadcast_to(places_ref[:, slot : slot + 1], shape) for slot in range(slots)]
+    for block in range(out_ref.shape[0]):
+        total = jnp.zeros(shape, F32)
+        for place, term in zip(places, terms):
+            total = total + jnp.where(place == block, term, 0.0)
+        out_ref[block] = total.astype(BF16)
 
 
 def on_device(cal_source, cal_target, app_source, readers, blocks, interp):
@@ -240,7 +265,7 @@
     send, keep = pl.pallas_call(
         functools.partial(gram_kernel, part, frames),
         in_specs=[
-            pl.BlockSpec(memory_space=pltpu.SMEM),
+            pl.BlockSpec(memory_space=pltpu.HBM),
             pl.BlockSpec(memory_space=pltpu.HBM),
             pl.BlockSpec(memory_space=pltpu.HBM),
         ],
@@ -249,7 +274,9 @@
             pltpu.VMEM((held, samples, depth), BF16),
             pltpu.VMEM((held, coils, 2, samples), BF16),
             pltpu.VMEM((held, depth, samples), BF16),
+            pltpu.SMEM(readers.shape, jnp.int32),
             pltpu.SemaphoreType.DMA((2, held)),
+            pltpu.SemaphoreType.DMA,
         ],
         compiler_params=SMALL,
     )(
@@ -295,15 +322,7 @@
     chosen = lax.all_to_all(sent, "frame", 0, 0, tiled=True)
     grid = pl.pallas_call(
         fill_kernel,
-        in_specs=[
-            pl.BlockSpec(memory_space=pltpu.SMEM),
-            pl.BlockSpec(memory_space=pltpu.SMEM),
-            pl.BlockSpec(memory_space=pltpu.VMEM),
-            pl.BlockSpec(memory_space=pltpu.VMEM),
-            pl.BlockSpec(memory_space=pltpu.VMEM),
-        ],
         out_shape=jax.ShapeDtypeStruct((segs, 2 * coils, cells), BF16),
-        scratch_shapes=[pltpu.VMEM((segs, 2 * coils, cells), F32)],
         compiler_params=SMALL,
     )(readers, blocks, chosen, app_source, interp)
     terms = lax.all_to_all(grid, "seg", 0, 0, tiled=True)

time: 107 us -> 106 us (level)
  Pallas kernels: 11.9 us -> 10.6 us
where the time goes in v7:
time: 106 us
  blocking collectives  90.9 us (86%)
  Pallas kernels  10.6 us (10%)
  starting transfers between devices  1.92 us (2%)
  waiting for transfers between devices  1.43 us (1%)
    all_to_all x1, blocking collectives, on_device(): pieces = lax.all_to_all(weights, 'seg', 0, 0, tiled=True)  29.9 us
    all_to_all x1, blocking collectives, on_device(): terms = lax.all_to_all(grid, 'seg', 0, 0, tiled=True)  19.2 us
    all_to_all x1, blocking collectives, on_device(): lax.all_to_all(keep + other, 'frame', 0, 0, tiled=True, axis_index_groups...  14.6 us
    all_to_all x1, blocking collectives, on_device(): chosen = lax.all_to_all(sent, 'frame', 0, 0, tiled=True)  10.7 us
    all_to_all x1, blocking collectives, on_device(): gram = lax.all_to_all(spread, 'coil', 0, 0, tiled=True)  8.41 us
    all_gather x1, blocking collectives, on_device(): lax.all_gather(jnp.sum(total * total, axis=0, keepdims=True), 'coil', til...  8.13 us
    pallas_call x1, Pallas kernels, on_device(): pl.pallas_call(functools.partial(solve_kernel, part), out_shape=jax.Shape...  4.72 us
    pallas_call x1, Pallas kernels, on_device(): pl.pallas_call(functools.partial(gram_kernel, part, frames), in_specs=[pl...  4.22 us
  transfers between devices with their start and end apart: 1, of which 1 were waited for; matrix products, arithmetic and copies ran while one was open for 0% of the time, Pallas kernels for 0%

profile of v7, /device:TPU:32, one launch (start us, length us, event | category | flops | bytes accessed | tf_op | source)
XLA Modules:
  0.0 105.6 jit_solution(572431815726495631)
XLA Ops:
  0.0 0.0 copy-start.2
  0.0 0.0 copy-start.1
  0.0 0.0 copy-start.3
  0.0 0.0 copy-start
  0.0 4.2 %shard_map.64 = (f32[4,104,128]{2,1,0:T(8,128)S(1)}, f32[4,104,128]{2,1,0:T(8,128)S(1)}) custom-call(s32[1,4]{1,0:T(1,128)} %reads_ref.3, bf16[8,576,384]{2,1,0:T(8,128)(2,1)} %source_ref.2, bf16[8,8,2,576]{3,2,1,0:T(2,128)(2,1)} %target_ref.1), custom_call_target="tpu_custom_call" | custom-call | tf_op jit(solution)/shard_map/pallas_call | solution.py:265
  4.2 1.9 %collective-permute-start = (f32[4,104,128]{2,1,0:T(8,128)S(1)}, f32[4,104,128]{2,1,0:T(8,128)S(1)}, u32[]{:S(2)}, u32[]{:S(2)}) collective-permute-start(f32[4,104,128]{2,1,0:T(8,128)S(1)} %get-tuple-element.11), channel_id=1, source_target_pairs={{0,64},{64,0},{128,192},{192,128},{256,320},{320,256},{384,448},{4... | collective-permute-start | bytes 638984 | tf_op jit(solution)/shard_map/ppermute | solution.py:287
  6.2 1.4 %collective-permute-done = f32[4,104,128]{2,1,0:T(8,128)S(1)} collective-permute-done((f32[4,104,128]{2,1,0:T(8,128)S(1)}, f32[4,104,128]{2,1,0:T(8,128)S(1)}, u32[]{:S(2)}, u32[]{:S(2)}) %collective-permute-start) | collective-permute-done | bytes 213024 | tf_op jit(solution)/shard_map/ppermute | solution.py:287
  7.6 14.6 %all_to_all.25.partial_ref = f32[4,104,128]{2,1,0:T(8,128)S(1)} all-to-all(f32[4,104,128]{2,1,0:T(8,128)S(1)} %add.18), channel_id=1, replica_groups={{0,128,256,384},{64,192,320,448},{1,129,257,385},{65,193,321,449},{2,13..., dimensions={0} | all-to-all | bytes 425984 | tf_op jit(solution)/shard_map/all_to_all | solution.py:289
  22.2 8.4 %all_to_all.26.gram_ref = f32[4,72,128]{2,1,0:T(8,128)S(1)} all-to-all(f32[4,72,128]{2,1,0:T(8,128)S(1)} %get-tuple-element.13), channel_id=1, replica_groups=mesh['frame'=8,'seg'=16,'coil'=4] {'coil'}, dimensions={0} | all-to-all | bytes 294912 | tf_op jit(solution)/shard_map/all_to_all | solution.py:301
  30.6 4.7 %shard_map.66 = bf16[16,8,384]{2,1,0:T(8,128)(2,1)S(1)} custom-call(f32[4,72,128]{2,1,0:T(8,128)S(1)} %all_to_all.26.gram_ref, f32[24,128]{1,0:T(8,128)S(1)} %get-tuple-element.14.rhs_ref), custom_call_target="tpu_custom_call" | custom-call | tf_op jit(solution)/shard_map/pallas_call | solution.py:302
  35.4 29.9 %all_to_all.27.piece_ref = bf16[16,8,384]{2,1,0:T(8,128)(2,1)S(1)} all-to-all(bf16[16,8,384]{2,1,0:T(8,128)(2,1)S(1)} %shard_map.66), channel_id=1, replica_groups=mesh['frame'=8,'seg'=16,'coil'=4] {'seg'}, dimensions={0} | all-to-all | bytes 196608 | tf_op jit(solution)/shard_map/all_to_all | solution.py:312
  65.2 0.6 shard_map.67
  65.8 10.7 %all_to_all.28.weights_ref = bf16[8,4,8,384]{3,2,1,0:T(8,128)(2,1)S(1)} all-to-all(bf16[8,4,8,384]{3,2,1,0:T(8,128)(2,1)S(1)} %shard_map.67), channel_id=1, replica_groups=mesh['frame'=8,'seg'=16,'coil'=4] {'frame'}, dimensions={0} | all-to-all | bytes 393216 | tf_op jit(solution)/shard_map/all_to_all | solution.py:322
  76.6 0.0 copy-done.2
  76.6 0.0 copy-done.1
  76.6 0.0 copy-done.3
  76.6 0.0 copy-done
  76.6 1.0 shard_map.68
  77.6 19.2 %all_to_all.29 = bf16[16,16,256]{2,1,0:T(8,128)(2,1)S(1)} all-to-all(bf16[16,16,256]{2,1,0:T(8,128)(2,1)S(1)} %shard_map.68), channel_id=1, replica_groups=mesh['frame'=8,'seg'=16,'coil'=4] {'seg'}, dimensions={0} | all-to-all | bytes 262144 | tf_op jit(solution)/shard_map/all_to_all | solution.py:328
  96.9 8.1 %all-gather.1 = f32[4,1,256]{2,1,0:T(1,128)S(1)} all-gather(f32[1,1,256]{2,1,0:T(1,128)S(1)} %bitcast.2), channel_id=2, replica_groups=mesh['frame'=8,'seg'=16,'coil'=4] {'coil'}, dimensions={0}, use_global_device_ids=true | all-gather | bytes 5120 | tf_op jit(solution)/shard_map/all_gather | solution.py:330
  105.0 0.6 add_sqrt_fusion
  (5 shorter events, 0.1 us)
Async XLA Ops:
  0.0 76.6 %copy-start.2 = (s32[1,4]{1,0:T(1,128)S(1)}, s32[1,4]{1,0:T(1,128)}, u32[]{:S(2)}) copy-start(s32[1,4]{1,0:T(1,128)} %reads_ref.3) | copy-start | bytes 52
  0.0 76.6 %copy-start.1 = (bf16[1,4,256,128]{3,2,1,0:T(8,128)(2,1)S(1)}, bf16[1,4,256,128]{3,2,1,0:T(8,128)(2,1)}, u32[]{:S(2)}) copy-start(bf16[1,4,256,128]{3,2,1,0:T(8,128)(2,1)} %interp_ref.1) | copy-start | bytes 786436
  0.0 76.6 %copy-start.3 = (s32[1,4]{1,0:T(1,128)S(1)}, s32[1,4]{1,0:T(1,128)}, u32[]{:S(2)}) copy-start(s32[1,4]{1,0:T(1,128)} %places_ref.1) | copy-start | bytes 52
  0.0 76.6 %copy-start = (bf16[1,4,128,384]{3,2,1,0:T(8,128)(2,1)S(1)}, bf16[1,4,128,384]{3,2,1,0:T(8,128)(2,1)}, u32[]{:S(2)}) copy-start(bf16[1,4,128,384]{3,2,1,0:T(8,128)(2,1)} %source_ref.3) | copy-start | bytes 1179652
  4.2 3.4 %collective-permute-start = (f32[4,104,128]{2,1,0:T(8,128)S(1)}, f32[4,104,128]{2,1,0:T(8,128)S(1)}, u32[]{:S(2)}, u32[]{:S(2)}) collective-permute-start(f32[4,104,128]{2,1,0:T(8,128)S(1)} %get-tuple-element.11), channel_id=1, source_target_pairs={{0,64},{64,0},{128,192},{192,128},{256,320},{320,256},{384,448},{4... | collective-permute-start | bytes 638984 | tf_op jit(solution)/shard_map/ppermute | solution.py:287

commit v8 on v7

--- a/solution.py
+++ b/solution.py
@@ -13,7 +13,6 @@
 F32 = jnp.float32
 BF16 = jnp.bfloat16
 LANES = 128
-GROUPS = ((0, 1), (2, 3, 4), (5, 6, 7))
 SMALL = pltpu.CompilerParams(vmem_limit_bytes=16 * 1024 * 1024)
 
 
@@ -45,48 +44,18 @@
     )
 
 
-def gram_kernel(
-    part,
-    frames,
-    reads_ref,
-    source_ref,
-    target_ref,
-    send_ref,
-    keep_ref,
-    held_ref,
-    goal_ref,
-    turned_ref,
-    read_ref,
-    sem,
-    read_sem,
-):
+def gram_sums(part, groups, held_ref, goal_ref, turned_ref, out_ref, copies):
     coil = lax.axis_index("coil")
-    core = lax.rem(lax.axis_index("frame"), 2)
-    count, depth, samples = turned_ref.shape
+    depth = held_ref.shape[2]
     width = depth // 2
     half = part // 2
     base = part + half
-    coils = target_ref.shape[1]
-    each = count // 2
-    copies = []
-    for slot in range(count):
-        segment = 2 * (slot % each) + (1 - core if slot < each else core)
-        copies.append(
-            (
-                pltpu.make_async_copy(source_ref.at[segment], held_ref.at[slot], sem.at[0, slot]),
-                pltpu.make_async_copy(target_ref.at[segment], goal_ref.at[slot], sem.at[1, slot]),
-            )
-        )
-    for pair in copies:
-        for copy in pair:
-            copy.start()
-    listing = pltpu.make_async_copy(reads_ref, read_ref, read_sem)
-    listing.start()
+    coils = goal_ref.shape[1]
     across = lax.broadcasted_iota(jnp.int32, (part, width), 1)
     down = lax.broadcasted_iota(jnp.int32, (part, width), 0) + coil * part
     first = pl.multiple_of(coil * part, 16)
     second = pl.multiple_of(width + coil * part, 16)
-    for slots in GROUPS:
+    for slots in groups:
         for slot in slots:
             for copy in copies[slot]:
                 copy.wait()
@@ -109,7 +78,7 @@
             for left, slot in zip(lefts, slots)
         ]
         for slot, sums in zip(slots, products):
-            out = (send_ref if slot < each else keep_ref).at[slot % each]
+            out = out_ref.at[slot]
             top, bottom = sums[:part], sums[part : 2 * part]
             gram_real = top[:, :width] + bottom[:, width:]
             gram_imag = top[:, width:] - bottom[:, :width]
@@ -119,7 +88,7 @@
             rhs_real = proj_real[:, :width] + proj_imag[:, width:]
             rhs_imag = proj_imag[:, :width] - proj_real[:, width:]
             out[:part] = packed[:, :LANES]
-            out[part : part + half] = jnp.concatenate(
+            out[part:base] = jnp.concatenate(
                 [packed[:half, LANES:], packed[half:, LANES:]], axis=1
             )
             out[base : base + coils] = rhs_real[:, :LANES]
@@ -127,16 +96,69 @@
             out[base + 2 * coils : base + 3 * coils] = jnp.concatenate(
                 [rhs_real[:, LANES:], rhs_imag[:, LANES:]], axis=1
             )
-    listing.wait()
+
+
+def tell(frames, read_ref, out_ref):
+    core = lax.rem(lax.axis_index("frame"), 2)
     row = lax.broadcasted_iota(jnp.int32, (8, LANES), 0)
     lane = lax.broadcasted_iota(jnp.int32, (8, LANES), 1)
     told = jnp.zeros((8, LANES), jnp.int32)
     for place in range(read_ref.shape[1]):
         told = jnp.where((row == core) & (lane == place), lax.div(read_ref[0, place], frames), told)
-    told = told.astype(F32)
-    for slot in range(each):
-        send_ref[slot, base + 3 * coils :] = told
-        keep_ref[slot, base + 3 * coils :] = told
+    for slot in range(out_ref.shape[0]):
+        out_ref[slot, out_ref.shape[1] - 8 :] = told.astype(F32)
+
+
+def other_gram_kernel(
+    part,
+    frames,
+    reads_ref,
+    source_ref,
+    target_ref,
+    out_ref,
+    own_held_ref,
+    own_goal_ref,
+    held_ref,
+    goal_ref,
+    turned_ref,
+    read_ref,
+    sem,
+    read_sem,
+):
+    core = lax.rem(lax.axis_index("frame"), 2)
+    each = out_ref.shape[0]
+    copies = []
+    for slot in range(2 * each):
+        own, place = slot // each, slot % each
+        segment = 2 * place + (core if own else 1 - core)
+        held = (own_held_ref if own else held_ref).at[place]
+        goal = (own_goal_ref if own else goal_ref).at[place]
+        copies.append(
+            (
+                pltpu.make_async_copy(source_ref.at[segment], held, sem.at[0, slot]),
+                pltpu.make_async_copy(target_ref.at[segment], goal, sem.at[1, slot]),
+            )
+        )
+    for pair in copies:
+        for copy in pair:
+            copy.start()
+    listing = pltpu.make_async_copy(reads_ref, read_ref, read_sem)
+    listing.start()
+    gram_sums(part, ((0, 1), (2, 3)), held_ref, goal_ref, turned_ref, out_ref, copies)
+    listing.wait()
+    tell(frames, read_ref, out_ref)
+    for pair in copies[each:]:
+        for copy in pair:
+            copy.wait()
+
+
+def own_gram_kernel(part, frames, reads_ref, held_ref, goal_ref, out_ref, turned_ref, read_ref, read_sem):
+    listing = pltpu.make_async_copy(reads_ref, read_ref, read_sem)
+    listing.start()
+    slots = tuple(range(out_ref.shape[0]))
+    gram_sums(part, (slots,), held_ref, goal_ref, turned_ref, out_ref, [() for _ in slots])
+    listing.wait()
+    tell(frames, read_ref, out_ref)
 
 
 def sum_kernel(gram_rows, partial_ref, spread_ref, rhs_ref, told_ref):
@@ -262,28 +284,47 @@
 
     each = held // 2
     block = jax.ShapeDtypeStruct((each, rows, LANES), F32)
-    send, keep = pl.pallas_call(
-        functools.partial(gram_kernel, part, frames),
-        in_specs=[
-            pl.BlockSpec(memory_space=pltpu.HBM),
-            pl.BlockSpec(memory_space=pltpu.HBM),
-            pl.BlockSpec(memory_space=pltpu.HBM),
-        ],
-        out_shape=[block, block],
+    listed = pltpu.with_memory_space_constraint(readers, pltpu.HBM)
+    hbm = pl.BlockSpec(memory_space=pltpu.HBM)
+    vmem = pl.BlockSpec(memory_space=pltpu.VMEM)
+    reading = [pltpu.SMEM(readers.shape, jnp.int32)]
+    turned = pltpu.VMEM((each, depth, samples), BF16)
+    cost = pl.CostEstimate(
+        flops=2 * each * samples * depth * 2 * (part + coils),
+        bytes_accessed=2 * each * samples * (depth + 2 * coils),
+        transcendentals=0,
+    )
+    send, own_held, own_goal = pl.pallas_call(
+        functools.partial(other_gram_kernel, part, frames),
+        in_specs=[hbm, hbm, hbm],
+        out_shape=[
+            block,
+            jax.ShapeDtypeStruct((each, samples, depth), BF16),
+            jax.ShapeDtypeStruct((each, coils, 2, samples), BF16),
+        ],
         scratch_shapes=[
-            pltpu.VMEM((held, samples, depth), BF16),
-            pltpu.VMEM((held, coils, 2, samples), BF16),
-            pltpu.VMEM((held, depth, samples), BF16),
-            pltpu.SMEM(readers.shape, jnp.int32),
+            pltpu.VMEM((each, samples, depth), BF16),
+            pltpu.VMEM((each, coils, 2, samples), BF16),
+            turned,
+            *reading,
             pltpu.SemaphoreType.DMA((2, held)),
             pltpu.SemaphoreType.DMA,
         ],
         compiler_params=SMALL,
+        cost_estimate=cost,
     )(
-        pltpu.with_memory_space_constraint(readers, pltpu.HBM),
+        listed,
         pltpu.with_memory_space_constraint(cal_source, pltpu.HBM),
         pltpu.with_memory_space_constraint(cal_target, pltpu.HBM),
     )
+    keep = pl.pallas_call(
+        functools.partial(own_gram_kernel, part, frames),
+        in_specs=[hbm, vmem, vmem],
+        out_shape=block,
+        scratch_shapes=[turned, *reading, pltpu.SemaphoreType.DMA],
+        compiler_params=SMALL,
+        cost_estimate=cost,
+    )(listed, own_held, own_goal)
     other = lax.ppermute(send, "frame", [(frame, frame ^ 1) for frame in range(frames)])
     chips = [[2 * chip + core for chip in range(frames // 2)] for core in range(2)]
     received = lax.all_to_all(

time: 106 us -> 105 us (level)
  waiting for transfers between devices: 1.43 us -> 0.01 us
    ppermute x1, waiting for transfers between devices: 1.43 us -> 0.01 us  [on_device(): lax.ppermute(send, 'frame', [(frame, frame ^ 1) for frame in range(frames)])]
    pallas_call x1 -> x2, Pallas kernels: 4.22 us -> 4.44 us  [the longest x1 3 us: on_device(): pl.pallas_call(functools.partial(other_gram_kernel, part, frames), in_spe...]
  transfers between devices with their start and end apart: 1 -> 1, of which waited for: 1 -> 0; matrix products, arithmetic and copies ran while one was open for 0% -> 0% of each run, Pallas kernels for 0% -> 1%
where the time goes in v8:
time: 105 us
  blocking collectives  91.6 us (87%)
  Pallas kernels  10.8 us (10%)
  starting transfers between devices  1.92 us (2%)
    all_to_all x1, blocking collectives, on_device(): pieces = lax.all_to_all(weights, 'seg', 0, 0, tiled=True)  29.6 us
    all_to_all x1, blocking collectives, on_device(): terms = lax.all_to_all(grid, 'seg', 0, 0, tiled=True)  19.8 us
    all_to_all x1, blocking collectives, on_device(): lax.all_to_all(keep + other, 'frame', 0, 0, tiled=True, axis_index_groups...  14.9 us
    all_to_all x1, blocking collectives, on_device(): chosen = lax.all_to_all(sent, 'frame', 0, 0, tiled=True)  10.7 us
    all_to_all x1, blocking collectives, on_device(): gram = lax.all_to_all(spread, 'coil', 0, 0, tiled=True)  8.41 us
    all_gather x1, blocking collectives, on_device(): lax.all_gather(jnp.sum(total * total, axis=0, keepdims=True), 'coil', til...  8.13 us
    pallas_call x1, Pallas kernels, on_device(): pl.pallas_call(functools.partial(solve_kernel, part), out_shape=jax.Shape...  4.72 us
    pallas_call x1, Pallas kernels, on_device(): pl.pallas_call(functools.partial(other_gram_kernel, part, frames), in_spe...  3 us
  transfers between devices with their start and end apart: 1, of which 0 were waited for; matrix products, arithmetic and copies ran while one was open for 0% of the time, Pallas kernels for 1%

profile of v8, /device:TPU:32, one launch (start us, length us, event | category | flops | bytes accessed | tf_op | source)
XLA Modules:
  0.0 105.1 jit_solution(6645020752529866719)
XLA Ops:
  0.0 0.0 copy-start.2
  0.0 0.0 copy-start.1
  0.0 0.0 copy-start.3
  0.0 0.0 copy-start
  0.0 3.0 %shard_map.64 = (f32[4,104,128]{2,1,0:T(8,128)S(1)}, bf16[4,576,384]{2,1,0:T(8,128)(2,1)S(1)}, bf16[4,8,2,576]{3,2,1,0:T(2,128)(2,1)S(1)}) custom-call(s32[1,4]{1,0:T(1,128)} %reads_ref.5, bf16[8,576,384]{2,1,0:T(8,128)(2,1)} %source_ref.2, bf16[8,8,2,576]{3,2,1,0:T(2,128)(2,1)} %target_ref.1), custom_call_target="tpu_custom_call" | custom-call | flops 198180864 | bytes 1843200 | tf_op jit(solution)/shard_map/pallas_call | solution.py:297
  3.0 1.9 %collective-permute-start = (f32[4,104,128]{2,1,0:T(8,128)S(1)}, f32[4,104,128]{2,1,0:T(8,128)S(1)}, u32[]{:S(2)}, u32[]{:S(2)}) collective-permute-start(f32[4,104,128]{2,1,0:T(8,128)S(1)} %get-tuple-element.13), channel_id=1, source_target_pairs={{0,64},{64,0},{128,192},{192,128},{256,320},{320,256},{384,448},{4... | collective-permute-start | bytes 638984 | tf_op jit(solution)/shard_map/ppermute | solution.py:328
  5.0 1.4 %shard_map.65 = f32[4,104,128]{2,1,0:T(8,128)S(1)} custom-call(s32[1,4]{1,0:T(1,128)} %reads_ref.5, bf16[4,576,384]{2,1,0:T(8,128)(2,1)S(1)} %get-tuple-element.11.held_ref, bf16[4,8,2,576]{3,2,1,0:T(2,128)(2,1)S(1)} %get-tuple-element.12.goal_ref), custom_call_target="tpu_custom_call" | custom-call | flops 198180864 | bytes 1843200 | tf_op jit(solution)/shard_map/pallas_call | solution.py:320
  6.4 0.0 collective-permute-done
  6.4 14.9 %all_to_all.25.partial_ref = f32[4,104,128]{2,1,0:T(8,128)S(1)} all-to-all(f32[4,104,128]{2,1,0:T(8,128)S(1)} %add.18), channel_id=1, replica_groups={{0,128,256,384},{64,192,320,448},{1,129,257,385},{65,193,321,449},{2,13..., dimensions={0} | all-to-all | bytes 425984 | tf_op jit(solution)/shard_map/all_to_all | solution.py:330
  21.4 8.4 %all_to_all.26.gram_ref = f32[4,72,128]{2,1,0:T(8,128)S(1)} all-to-all(f32[4,72,128]{2,1,0:T(8,128)S(1)} %get-tuple-element.15), channel_id=1, replica_groups=mesh['frame'=8,'seg'=16,'coil'=4] {'coil'}, dimensions={0} | all-to-all | bytes 294912 | tf_op jit(solution)/shard_map/all_to_all | solution.py:342
  29.8 4.7 %shard_map.67 = bf16[16,8,384]{2,1,0:T(8,128)(2,1)S(1)} custom-call(f32[4,72,128]{2,1,0:T(8,128)S(1)} %all_to_all.26.gram_ref, f32[24,128]{1,0:T(8,128)S(1)} %get-tuple-element.16.rhs_ref), custom_call_target="tpu_custom_call" | custom-call | tf_op jit(solution)/shard_map/pallas_call | solution.py:343
  34.5 29.6 %all_to_all.27.piece_ref = bf16[16,8,384]{2,1,0:T(8,128)(2,1)S(1)} all-to-all(bf16[16,8,384]{2,1,0:T(8,128)(2,1)S(1)} %shard_map.67), channel_id=1, replica_groups=mesh['frame'=8,'seg'=16,'coil'=4] {'seg'}, dimensions={0} | all-to-all | bytes 196608 | tf_op jit(solution)/shard_map/all_to_all | solution.py:353
  64.2 0.6 shard_map.68
  64.8 10.7 %all_to_all.28.weights_ref = bf16[8,4,8,384]{3,2,1,0:T(8,128)(2,1)S(1)} all-to-all(bf16[8,4,8,384]{3,2,1,0:T(8,128)(2,1)S(1)} %shard_map.68), channel_id=1, replica_groups=mesh['frame'=8,'seg'=16,'coil'=4] {'frame'}, dimensions={0} | all-to-all | bytes 393216 | tf_op jit(solution)/shard_map/all_to_all | solution.py:363
  75.5 0.0 copy-done.2
  75.5 0.0 copy-done.1
  75.5 0.0 copy-done.3
  75.5 0.0 copy-done
  75.5 1.0 shard_map.69
  76.5 19.8 %all_to_all.29 = bf16[16,16,256]{2,1,0:T(8,128)(2,1)S(1)} all-to-all(bf16[16,16,256]{2,1,0:T(8,128)(2,1)S(1)} %shard_map.69), channel_id=1, replica_groups=mesh['frame'=8,'seg'=16,'coil'=4] {'seg'}, dimensions={0} | all-to-all | bytes 262144 | tf_op jit(solution)/shard_map/all_to_all | solution.py:369
  96.4 8.1 %all-gather.1 = f32[4,1,256]{2,1,0:T(1,128)S(1)} all-gather(f32[1,1,256]{2,1,0:T(1,128)S(1)} %bitcast.2), channel_id=2, replica_groups=mesh['frame'=8,'seg'=16,'coil'=4] {'coil'}, dimensions={0}, use_global_device_ids=true | all-gather | bytes 5120 | tf_op jit(solution)/shard_map/all_gather | solution.py:371
  104.5 0.6 add_sqrt_fusion
  (5 shorter events, 0.1 us)
Async XLA Ops:
  0.0 75.5 %copy-start.2 = (s32[1,4]{1,0:T(1,128)S(1)}, s32[1,4]{1,0:T(1,128)}, u32[]{:S(2)}) copy-start(s32[1,4]{1,0:T(1,128)} %reads_ref.5) | copy-start | bytes 52
  0.0 75.5 %copy-start.1 = (bf16[1,4,256,128]{3,2,1,0:T(8,128)(2,1)S(1)}, bf16[1,4,256,128]{3,2,1,0:T(8,128)(2,1)}, u32[]{:S(2)}) copy-start(bf16[1,4,256,128]{3,2,1,0:T(8,128)(2,1)} %interp_ref.1) | copy-start | bytes 786436
  0.0 75.5 %copy-start.3 = (s32[1,4]{1,0:T(1,128)S(1)}, s32[1,4]{1,0:T(1,128)}, u32[]{:S(2)}) copy-start(s32[1,4]{1,0:T(1,128)} %places_ref.1) | copy-start | bytes 52
  0.0 75.5 %copy-start = (bf16[1,4,128,384]{3,2,1,0:T(8,128)(2,1)S(1)}, bf16[1,4,128,384]{3,2,1,0:T(8,128)(2,1)}, u32[]{:S(2)}) copy-start(bf16[1,4,128,384]{3,2,1,0:T(8,128)(2,1)} %source_ref.3) | copy-start | bytes 1179652
  3.0 3.4 %collective-permute-start = (f32[4,104,128]{2,1,0:T(8,128)S(1)}, f32[4,104,128]{2,1,0:T(8,128)S(1)}, u32[]{:S(2)}, u32[]{:S(2)}) collective-permute-start(f32[4,104,128]{2,1,0:T(8,128)S(1)} %get-tuple-element.13), channel_id=1, source_target_pairs={{0,64},{64,0},{128,192},{192,128},{256,320},{320,256},{384,448},{4... | collective-permute-start | bytes 638984 | tf_op jit(solution)/shard_map/ppermute | solution.py:328

commit v9 on v8

--- a/solution.py
+++ b/solution.py
@@ -9,7 +9,7 @@
 
 regular = 0.02
 epsilon = 1e-06
-settled = 1e-3
+settled = 0.0125
 F32 = jnp.float32
 BF16 = jnp.bfloat16
 LANES = 128
@@ -30,17 +30,22 @@
 
 
 def product(left, right):
+    rows = left.shape[0]
     a, b = pieces_of(left, 2), pieces_of(right, 2)
     dot = functools.partial(jnp.dot, preferred_element_type=F32)
-    return dot(a[0], b[0]) + (dot(a[1], b[0]) + dot(a[0], b[1]))
+    first = dot(jnp.concatenate(a, axis=0), b[0])
+    return first[:rows] + (first[rows:] + dot(a[0], b[1]))
 
 
 def fine_product(left, right):
+    rows = left.shape[0]
     a, b = pieces_of(left, 3), pieces_of(right, 3)
     dot = functools.partial(jnp.dot, preferred_element_type=F32)
-    return dot(a[0], b[0]) + (
-        (dot(a[0], b[1]) + dot(a[1], b[0]))
-        + (dot(a[1], b[1]) + (dot(a[0], b[2]) + dot(a[2], b[0])))
+    first = dot(jnp.concatenate(a, axis=0), b[0])
+    second = dot(jnp.concatenate(a[:2], axis=0), b[1])
+    return first[:rows] + (
+        (first[rows : 2 * rows] + second[:rows])
+        + (first[2 * rows :] + (second[rows:] + dot(a[0], b[2])))
     )
 
 
@@ -190,14 +195,14 @@
     flipped = packed.T
     down = lax.broadcasted_iota(jnp.int32, (width, width), 0)
     across = lax.broadcasted_iota(jnp.int32, (width, width), 1)
-    real = jnp.where(across <= down, packed, flipped)
-    imag = jnp.where(across > down, packed, jnp.where(across < down, -flipped, 0.0))
     diagonal = jnp.where(across == down, packed, 0.0)
     shift = regular / width * jnp.sum(diagonal)
-    high = jnp.sqrt(jnp.sum(real * real + imag * imag)) + shift
+    high = jnp.sqrt(jnp.sum(2.0 * (packed * packed) - diagonal * diagonal)) + shift
     scale = 2.0 / (high + shift)
+    real = jnp.where(across <= down, packed, flipped)
+    imag = jnp.where(across < down, -flipped, packed)
     real_ref[...] = (real + jnp.where(across == down, shift, 0.0)) * scale
-    imag_ref[...] = imag * scale
+    imag_ref[...] = jnp.where(across == down, 0.0, imag) * scale
     rhs_real = jnp.concatenate([rhs_ref[:coils], rhs_ref[2 * coils :, :64]], axis=1)
     rhs_imag = jnp.concatenate([rhs_ref[coils : 2 * coils], rhs_ref[2 * coils :, 64:]], axis=1)
     sol_ref[...] = jnp.concatenate([rhs_real, rhs_imag], axis=0) * scale
@@ -226,23 +231,30 @@
     spread = lax.while_loop(
         lambda spread: spread > settled, functools.partial(step, product), spread
     )
-    square = spread * spread
     sol = sol_ref[...]
-    by_real = product(sol, real_ref[...])
-    by_imag = product(sol, imag_ref[...])
-    change = jnp.concatenate(
-        [by_real[:coils] + by_imag[coils:], by_real[coils:] - by_imag[:coils]], axis=0
-    )
-    sol = 2.0 / (2.0 - square) * (2.0 * sol - change)
+    total = sol
+    for _ in range(2):
+        by_real = product(total, real_ref[...])
+        by_imag = product(total, imag_ref[...])
+        change = jnp.concatenate(
+            [by_real[:coils] + by_imag[coils:], by_real[coils:] - by_imag[:coils]], axis=0
+        )
+        total = sol + (total - change)
+    sol = total
     weights = jnp.concatenate([sol[:coils], sol[coils:]], axis=1).astype(BF16)
     for copy in range(out_ref.shape[0]):
         out_ref[copy] = weights
 
 
 def select_kernel(told_ref, piece_ref, out_ref):
+    pieces = [piece_ref[place].astype(F32) for place in range(piece_ref.shape[0])]
     for frame in range(out_ref.shape[0]):
         for slot in range(out_ref.shape[1]):
-            out_ref[frame, slot] = piece_ref[told_ref[frame, slot]]
+            wanted = jnp.broadcast_to(told_ref[frame : frame + 1, slot : slot + 1], pieces[0].shape)
+            chosen = pieces[0]
+            for place in range(1, len(pieces)):
+                chosen = jnp.where(wanted == place, pieces[place], chosen)
+            out_ref[frame, slot] = chosen.astype(BF16)
 
 
 def fill_kernel(reads_ref, places_ref, weights_ref, source_ref, interp_ref, out_ref):
@@ -353,10 +365,6 @@
     pieces = lax.all_to_all(weights, "seg", 0, 0, tiled=True)
     sent = pl.pallas_call(
         select_kernel,
-        in_specs=[
-            pl.BlockSpec(memory_space=pltpu.SMEM),
-            pl.BlockSpec(memory_space=pltpu.VMEM),
-        ],
         out_shape=jax.ShapeDtypeStruct((frames, slots, coils, depth), BF16),
         compiler_params=SMALL,
     )(told, pieces)

time: 105 us -> 105 us (level)
  the two profiles are of different devices: /device:TPU:32 before, /device:TPU:8 now
where the time goes in v9:
time: 105 us; the launch traced here: 104 us
  blocking collectives  91.7 us (87%)
  Pallas kernels  9.98 us (10%)
  starting transfers between devices  1.92 us (2%)
    all_to_all x1, blocking collectives, on_device(): pieces = lax.all_to_all(weights, 'seg', 0, 0, tiled=True)  29.5 us
    all_to_all x1, blocking collectives, on_device(): terms = lax.all_to_all(grid, 'seg', 0, 0, tiled=True)  19.1 us
    all_to_all x1, blocking collectives, on_device(): lax.all_to_all(keep + other, 'frame', 0, 0, tiled=True, axis_index_groups...  14.2 us
    all_to_all x1, blocking collectives, on_device(): chosen = lax.all_to_all(sent, 'frame', 0, 0, tiled=True)  10.7 us
    all_to_all x1, blocking collectives, on_device(): gram = lax.all_to_all(spread, 'coil', 0, 0, tiled=True)  9.68 us
    all_gather x1, blocking collectives, on_device(): lax.all_gather(jnp.sum(total * total, axis=0, keepdims=True), 'coil', til...  8.42 us
    pallas_call x1, Pallas kernels, on_device(): pl.pallas_call(functools.partial(solve_kernel, part), out_shape=jax.Shape...  4.16 us
    pallas_call x1, Pallas kernels, on_device(): pl.pallas_call(functools.partial(other_gram_kernel, part, frames), in_spe...  3 us
  transfers between devices with their start and end apart: 1, of which 0 were waited for; matrix products, arithmetic and copies ran while one was open for 0% of the time, Pallas kernels for 1%

profile of v9, /device:TPU:8, one launch (start us, length us, event | category | flops | bytes accessed | tf_op | source)
XLA Modules:
  0.0 104.4 jit_solution(13189292976382205867)
XLA Ops:
  0.0 0.0 copy-start.2
  0.0 0.0 copy-start.1
  0.0 0.0 copy-start.3
  0.0 0.0 copy-start
  0.0 3.0 %shard_map.64 = (f32[4,104,128]{2,1,0:T(8,128)S(1)}, bf16[4,576,384]{2,1,0:T(8,128)(2,1)S(1)}, bf16[4,8,2,576]{3,2,1,0:T(2,128)(2,1)S(1)}) custom-call(s32[1,4]{1,0:T(1,128)} %reads_ref.5, bf16[8,576,384]{2,1,0:T(8,128)(2,1)} %source_ref.2, bf16[8,8,2,576]{3,2,1,0:T(2,128)(2,1)} %target_ref.1), custom_call_target="tpu_custom_call" | custom-call | flops 198180864 | bytes 1843200 | tf_op jit(solution)/shard_map/pallas_call | solution.py:309
  3.0 1.9 %collective-permute-start = (f32[4,104,128]{2,1,0:T(8,128)S(1)}, f32[4,104,128]{2,1,0:T(8,128)S(1)}, u32[]{:S(2)}, u32[]{:S(2)}) collective-permute-start(f32[4,104,128]{2,1,0:T(8,128)S(1)} %get-tuple-element.13), channel_id=1, source_target_pairs={{0,64},{64,0},{128,192},{192,128},{256,320},{320,256},{384,448},{4... | collective-permute-start | bytes 638984 | tf_op jit(solution)/shard_map/ppermute | solution.py:340
  5.0 1.4 %shard_map.65 = f32[4,104,128]{2,1,0:T(8,128)S(1)} custom-call(s32[1,4]{1,0:T(1,128)} %reads_ref.5, bf16[4,576,384]{2,1,0:T(8,128)(2,1)S(1)} %get-tuple-element.11.held_ref, bf16[4,8,2,576]{3,2,1,0:T(2,128)(2,1)S(1)} %get-tuple-element.12.goal_ref), custom_call_target="tpu_custom_call" | custom-call | flops 198180864 | bytes 1843200 | tf_op jit(solution)/shard_map/pallas_call | solution.py:332
  6.4 0.0 collective-permute-done
  6.5 14.2 %all_to_all.25.partial_ref = f32[4,104,128]{2,1,0:T(8,128)S(1)} all-to-all(f32[4,104,128]{2,1,0:T(8,128)S(1)} %add.18), channel_id=1, replica_groups={{0,128,256,384},{64,192,320,448},{1,129,257,385},{65,193,321,449},{2,13..., dimensions={0} | all-to-all | bytes 425984 | tf_op jit(solution)/shard_map/all_to_all | solution.py:342
  20.7 9.7 %all_to_all.26.gram_ref = f32[4,72,128]{2,1,0:T(8,128)S(1)} all-to-all(f32[4,72,128]{2,1,0:T(8,128)S(1)} %get-tuple-element.15), channel_id=1, replica_groups=mesh['frame'=8,'seg'=16,'coil'=4] {'coil'}, dimensions={0} | all-to-all | bytes 294912 | tf_op jit(solution)/shard_map/all_to_all | solution.py:354
  30.4 4.2 %shard_map.67 = bf16[16,8,384]{2,1,0:T(8,128)(2,1)S(1)} custom-call(f32[4,72,128]{2,1,0:T(8,128)S(1)} %all_to_all.26.gram_ref, f32[24,128]{1,0:T(8,128)S(1)} %get-tuple-element.16.rhs_ref), custom_call_target="tpu_custom_call" | custom-call | tf_op jit(solution)/shard_map/pallas_call | solution.py:355
  34.5 29.5 %all_to_all.27.piece_ref = bf16[16,8,384]{2,1,0:T(8,128)(2,1)S(1)} all-to-all(bf16[16,8,384]{2,1,0:T(8,128)(2,1)S(1)} %shard_map.67), channel_id=1, replica_groups=mesh['frame'=8,'seg'=16,'coil'=4] {'seg'}, dimensions={0} | all-to-all | bytes 196608 | tf_op jit(solution)/shard_map/all_to_all | solution.py:365
  64.1 0.4 shard_map.68
  64.5 10.7 %all_to_all.28.weights_ref = bf16[8,4,8,384]{3,2,1,0:T(8,128)(2,1)S(1)} all-to-all(bf16[8,4,8,384]{3,2,1,0:T(8,128)(2,1)S(1)} %shard_map.68), channel_id=1, replica_groups=mesh['frame'=8,'seg'=16,'coil'=4] {'frame'}, dimensions={0} | all-to-all | bytes 393216 | tf_op jit(solution)/shard_map/all_to_all | solution.py:371
  75.2 0.0 copy-done.2
  75.2 0.0 copy-done.1
  75.2 0.0 copy-done.3
  75.2 0.0 copy-done
  75.2 1.0 shard_map.69
  76.2 19.1 %all_to_all.29 = bf16[16,16,256]{2,1,0:T(8,128)(2,1)S(1)} all-to-all(bf16[16,16,256]{2,1,0:T(8,128)(2,1)S(1)} %shard_map.69), channel_id=1, replica_groups=mesh['frame'=8,'seg'=16,'coil'=4] {'seg'}, dimensions={0} | all-to-all | bytes 262144 | tf_op jit(solution)/shard_map/all_to_all | solution.py:377
  95.3 8.4 %all-gather.1 = f32[4,1,256]{2,1,0:T(1,128)S(1)} all-gather(f32[1,1,256]{2,1,0:T(1,128)S(1)} %bitcast.2), channel_id=2, replica_groups=mesh['frame'=8,'seg'=16,'coil'=4] {'coil'}, dimensions={0}, use_global_device_ids=true | all-gather | bytes 5120 | tf_op jit(solution)/shard_map/all_gather | solution.py:379
  103.8 0.6 add_sqrt_fusion
  (5 shorter events, 0.1 us)
Async XLA Ops:
  0.0 75.2 %copy-start.2 = (s32[1,4]{1,0:T(1,128)S(1)}, s32[1,4]{1,0:T(1,128)}, u32[]{:S(2)}) copy-start(s32[1,4]{1,0:T(1,128)} %reads_ref.5) | copy-start | bytes 52
  0.0 75.2 %copy-start.1 = (bf16[1,4,256,128]{3,2,1,0:T(8,128)(2,1)S(1)}, bf16[1,4,256,128]{3,2,1,0:T(8,128)(2,1)}, u32[]{:S(2)}) copy-start(bf16[1,4,256,128]{3,2,1,0:T(8,128)(2,1)} %interp_ref.1) | copy-start | bytes 786436
  0.0 75.2 %copy-start.3 = (s32[1,4]{1,0:T(1,128)S(1)}, s32[1,4]{1,0:T(1,128)}, u32[]{:S(2)}) copy-start(s32[1,4]{1,0:T(1,128)} %places_ref.1) | copy-start | bytes 52
  0.0 75.2 %copy-start = (bf16[1,4,128,384]{3,2,1,0:T(8,128)(2,1)S(1)}, bf16[1,4,128,384]{3,2,1,0:T(8,128)(2,1)}, u32[]{:S(2)}) copy-start(bf16[1,4,128,384]{3,2,1,0:T(8,128)(2,1)} %source_ref.3) | copy-start | bytes 1179652
  3.0 3.4 %collective-permute-start = (f32[4,104,128]{2,1,0:T(8,128)S(1)}, f32[4,104,128]{2,1,0:T(8,128)S(1)}, u32[]{:S(2)}, u32[]{:S(2)}) collective-permute-start(f32[4,104,128]{2,1,0:T(8,128)S(1)} %get-tuple-element.13), channel_id=1, source_target_pairs={{0,64},{64,0},{128,192},{192,128},{256,320},{320,256},{384,448},{4... | collective-permute-start | bytes 638984 | tf_op jit(solution)/shard_map/ppermute | solution.py:340

commit v10 on v9

--- a/solution.py
+++ b/solution.py
@@ -281,6 +281,26 @@
         out_ref[block] = total.astype(BF16)
 
 
+def near_kernel(coil_count, terms_ref, out_ref):
+    blocks = out_ref.shape[0] // coil_count
+    for block in range(blocks):
+        total = terms_ref[block].astype(F32)
+        for run in range(1, terms_ref.shape[0] // blocks):
+            total = total + terms_ref[run * blocks + block].astype(F32)
+        for coil in range(coil_count):
+            out_ref[block * coil_count + coil] = total.astype(BF16)
+
+
+def root_kernel(coil_count, terms_ref, out_ref):
+    power = None
+    for coil in range(coil_count):
+        total = terms_ref[coil].astype(F32)
+        for place in range(1, terms_ref.shape[0] // coil_count):
+            total = total + terms_ref[place * coil_count + coil].astype(F32)
+        power = total * total if power is None else power + total * total
+    out_ref[...] = jnp.sqrt(jnp.sum(power, axis=0, keepdims=True) + epsilon)
+
+
 def on_device(cal_source, cal_target, app_source, readers, blocks, interp):
     frames = lax.axis_size("frame")
     segs = lax.axis_size("seg")
@@ -374,10 +394,23 @@
         out_shape=jax.ShapeDtypeStruct((segs, 2 * coils, cells), BF16),
         compiler_params=SMALL,
     )(readers, blocks, chosen, app_source, interp)
-    terms = lax.all_to_all(grid, "seg", 0, 0, tiled=True)
-    total = jnp.sum(terms.astype(F32), axis=0)
-    power = lax.all_gather(jnp.sum(total * total, axis=0, keepdims=True), "coil", tiled=True)
-    return jnp.sqrt(jnp.sum(power, axis=0, keepdims=True) + epsilon)
+    columns = segs // 4
+    far = [[column + 4 * run for run in range(columns)] for column in range(4)]
+    terms = lax.all_to_all(grid, "seg", 0, 0, tiled=True, axis_index_groups=far)
+    spread = pl.pallas_call(
+        functools.partial(near_kernel, coil_count),
+        out_shape=jax.ShapeDtypeStruct((4 * coil_count, 2 * coils, cells), BF16),
+        compiler_params=SMALL,
+    )(terms)
+    near = [
+        [run * 4 * coil_count + member for member in range(4 * coil_count)] for run in range(columns)
+    ]
+    terms = lax.all_to_all(spread, ("seg", "coil"), 0, 0, tiled=True, axis_index_groups=near)
+    return pl.pallas_call(
+        functools.partial(root_kernel, coil_count),
+        out_shape=jax.ShapeDtypeStruct((1, cells), F32),
+        compiler_params=SMALL,
+    )(terms)
 
 
 def solution(mesh):

time: 105 us -> 106 us (level)
  the two profiles are of different devices: /device:TPU:8 before, /device:TPU:32 now
where the time goes in v10:
time: 106 us
  blocking collectives  93 us (88%)
  Pallas kernels  10.6 us (10%)
  starting transfers between devices  1.92 us (2%)
    all_to_all x1, blocking collectives, on_device(): pieces = lax.all_to_all(weights, 'seg', 0, 0, tiled=True)  29.6 us
    all_to_all x1, blocking collectives, on_device(): terms = lax.all_to_all(grid, 'seg', 0, 0, tiled=True, axis_index_groups=far)  18 us
    all_to_all x1, blocking collectives, on_device(): lax.all_to_all(keep + other, 'frame', 0, 0, tiled=True, axis_index_groups...  14.9 us
    all_to_all x1, blocking collectives, on_device(): lax.all_to_all(spread, ('seg', 'coil'), 0, 0, tiled=True, axis_index_grou...  11.4 us
    all_to_all x1, blocking collectives, on_device(): chosen = lax.all_to_all(sent, 'frame', 0, 0, tiled=True)  10.7 us
    all_to_all x1, blocking collectives, on_device(): gram = lax.all_to_all(spread, 'coil', 0, 0, tiled=True)  8.41 us
    pallas_call x1, Pallas kernels, on_device(): pl.pallas_call(functools.partial(solve_kernel, part), out_shape=jax.Shape...  4.15 us
    pallas_call x1, Pallas kernels, on_device(): pl.pallas_call(functools.partial(other_gram_kernel, part, frames), in_spe...  3 us
  transfers between devices with their start and end apart: 1, of which 0 were waited for; matrix products, arithmetic and copies ran while one was open for 0% of the time, Pallas kernels for 1%

profile of v10, /device:TPU:32, one launch (start us, length us, event | category | flops | bytes accessed | tf_op | source)
XLA Modules:
  0.0 105.6 jit_solution(4015333227906242470)
XLA Ops:
  0.0 0.0 copy-start.2
  0.0 0.0 copy-start.1
  0.0 0.0 copy-start.3
  0.0 0.0 copy-start
  0.0 3.0 %shard_map.64 = (f32[4,104,128]{2,1,0:T(8,128)S(1)}, bf16[4,576,384]{2,1,0:T(8,128)(2,1)S(1)}, bf16[4,8,2,576]{3,2,1,0:T(2,128)(2,1)S(1)}) custom-call(s32[1,4]{1,0:T(1,128)} %reads_ref.5, bf16[8,576,384]{2,1,0:T(8,128)(2,1)} %source_ref.2, bf16[8,8,2,576]{3,2,1,0:T(2,128)(2,1)} %target_ref.1), custom_call_target="tpu_custom_call" | custom-call | flops 198180864 | bytes 1843200 | tf_op jit(solution)/shard_map/pallas_call | solution.py:329
  3.0 1.9 %collective-permute-start = (f32[4,104,128]{2,1,0:T(8,128)S(1)}, f32[4,104,128]{2,1,0:T(8,128)S(1)}, u32[]{:S(2)}, u32[]{:S(2)}) collective-permute-start(f32[4,104,128]{2,1,0:T(8,128)S(1)} %get-tuple-element.13), channel_id=1, source_target_pairs={{0,64},{64,0},{128,192},{192,128},{256,320},{320,256},{384,448},{4... | collective-permute-start | bytes 638984 | tf_op jit(solution)/shard_map/ppermute | solution.py:360
  5.0 1.4 %shard_map.65 = f32[4,104,128]{2,1,0:T(8,128)S(1)} custom-call(s32[1,4]{1,0:T(1,128)} %reads_ref.5, bf16[4,576,384]{2,1,0:T(8,128)(2,1)S(1)} %get-tuple-element.11.held_ref, bf16[4,8,2,576]{3,2,1,0:T(2,128)(2,1)S(1)} %get-tuple-element.12.goal_ref), custom_call_target="tpu_custom_call" | custom-call | flops 198180864 | bytes 1843200 | tf_op jit(solution)/shard_map/pallas_call | solution.py:352
  6.4 0.0 collective-permute-done
  6.4 14.9 %all_to_all.30.partial_ref = f32[4,104,128]{2,1,0:T(8,128)S(1)} all-to-all(f32[4,104,128]{2,1,0:T(8,128)S(1)} %add.3), channel_id=1, replica_groups={{0,128,256,384},{64,192,320,448},{1,129,257,385},{65,193,321,449},{2,13..., dimensions={0} | all-to-all | bytes 425984 | tf_op jit(solution)/shard_map/all_to_all | solution.py:362
  21.4 8.4 %all_to_all.31.gram_ref = f32[4,72,128]{2,1,0:T(8,128)S(1)} all-to-all(f32[4,72,128]{2,1,0:T(8,128)S(1)} %get-tuple-element.15), channel_id=1, replica_groups=mesh['frame'=8,'seg'=16,'coil'=4] {'coil'}, dimensions={0} | all-to-all | bytes 294912 | tf_op jit(solution)/shard_map/all_to_all | solution.py:374
  29.8 4.2 %shard_map.67 = bf16[16,8,384]{2,1,0:T(8,128)(2,1)S(1)} custom-call(f32[4,72,128]{2,1,0:T(8,128)S(1)} %all_to_all.31.gram_ref, f32[24,128]{1,0:T(8,128)S(1)} %get-tuple-element.16.rhs_ref), custom_call_target="tpu_custom_call" | custom-call | tf_op jit(solution)/shard_map/pallas_call | solution.py:375
  34.0 29.6 %all_to_all.32.piece_ref = bf16[16,8,384]{2,1,0:T(8,128)(2,1)S(1)} all-to-all(bf16[16,8,384]{2,1,0:T(8,128)(2,1)S(1)} %shard_map.67), channel_id=1, replica_groups=mesh['frame'=8,'seg'=16,'coil'=4] {'seg'}, dimensions={0} | all-to-all | bytes 196608 | tf_op jit(solution)/shard_map/all_to_all | solution.py:385
  63.6 0.4 shard_map.68
  64.0 10.7 %all_to_all.33.weights_ref = bf16[8,4,8,384]{3,2,1,0:T(8,128)(2,1)S(1)} all-to-all(bf16[8,4,8,384]{3,2,1,0:T(8,128)(2,1)S(1)} %shard_map.68), channel_id=1, replica_groups=mesh['frame'=8,'seg'=16,'coil'=4] {'frame'}, dimensions={0} | all-to-all | bytes 393216 | tf_op jit(solution)/shard_map/all_to_all | solution.py:391
  74.7 0.0 copy-done.2
  74.7 0.0 copy-done.1
  74.7 0.0 copy-done.3
  74.7 0.0 copy-done
  74.7 1.0 shard_map.69
  75.7 18.0 %all_to_all.34.terms_ref = bf16[16,16,256]{2,1,0:T(8,128)(2,1)S(1)} all-to-all(bf16[16,16,256]{2,1,0:T(8,128)(2,1)S(1)} %shard_map.69), channel_id=1, replica_groups={{0,16,32,48},{4,20,36,52},{8,24,40,56},{12,28,44,60},{1,17,33,49},{5,21..., dimensions={0} | all-to-all | bytes 262144 | tf_op jit(solution)/shard_map/all_to_all | solution.py:399
  93.7 11.4 %all_to_all.35.terms_ref = bf16[16,16,256]{2,1,0:T(8,128)(2,1)S(1)} all-to-all(bf16[16,16,256]{2,1,0:T(8,128)(2,1)S(1)} %shard_map.70), channel_id=1, replica_groups={{0,1,2,3,4,5,6,7,8,9,10,11,12,13,14,15},{16,17,18,19,20,21,22,23,24,25,..., dimensions={0} | all-to-all | bytes 262144 | tf_op jit(solution)/shard_map/all_to_all | solution.py:408
  105.0 0.6 shard_map.71
  (3 shorter events, 0.1 us)
Async XLA Ops:
  0.0 74.7 %copy-start.2 = (s32[1,4]{1,0:T(1,128)S(1)}, s32[1,4]{1,0:T(1,128)}, u32[]{:S(2)}) copy-start(s32[1,4]{1,0:T(1,128)} %reads_ref.5) | copy-start | bytes 52
  0.0 74.7 %copy-start.1 = (bf16[1,4,256,128]{3,2,1,0:T(8,128)(2,1)S(1)}, bf16[1,4,256,128]{3,2,1,0:T(8,128)(2,1)}, u32[]{:S(2)}) copy-start(bf16[1,4,256,128]{3,2,1,0:T(8,128)(2,1)} %interp_ref.1) | copy-start | bytes 786436
  0.0 74.7 %copy-start.3 = (s32[1,4]{1,0:T(1,128)S(1)}, s32[1,4]{1,0:T(1,128)}, u32[]{:S(2)}) copy-start(s32[1,4]{1,0:T(1,128)} %places_ref.1) | copy-start | bytes 52
  0.0 74.7 %copy-start = (bf16[1,4,128,384]{3,2,1,0:T(8,128)(2,1)S(1)}, bf16[1,4,128,384]{3,2,1,0:T(8,128)(2,1)}, u32[]{:S(2)}) copy-start(bf16[1,4,128,384]{3,2,1,0:T(8,128)(2,1)} %source_ref.3) | copy-start | bytes 1179652
  3.0 3.4 %collective-permute-start = (f32[4,104,128]{2,1,0:T(8,128)S(1)}, f32[4,104,128]{2,1,0:T(8,128)S(1)}, u32[]{:S(2)}, u32[]{:S(2)}) collective-permute-start(f32[4,104,128]{2,1,0:T(8,128)S(1)} %get-tuple-element.13), channel_id=1, source_target_pairs={{0,64},{64,0},{128,192},{192,128},{256,320},{320,256},{384,448},{4... | collective-permute-start | bytes 638984 | tf_op jit(solution)/shard_map/ppermute | solution.py:360

commit v11 on v9

--- a/solution.py
+++ b/solution.py
@@ -149,7 +149,7 @@
             copy.start()
     listing = pltpu.make_async_copy(reads_ref, read_ref, read_sem)
     listing.start()
-    gram_sums(part, ((0, 1), (2, 3)), held_ref, goal_ref, turned_ref, out_ref, copies)
+    gram_sums(part, ((0,), (1, 2, 3)), held_ref, goal_ref, turned_ref, out_ref, copies)
     listing.wait()
     tell(frames, read_ref, out_ref)
     for pair in copies[each:]:
@@ -226,7 +226,7 @@
 
     spread = (high - shift) / (high + shift)
     spread = lax.while_loop(
-        lambda spread: spread > 0.97, functools.partial(step, fine_product), spread
+        lambda spread: spread > 0.99, functools.partial(step, fine_product), spread
     )
     spread = lax.while_loop(
         lambda spread: spread > settled, functools.partial(step, product), spread

time: 105 us -> 105 us (level)
  the two profiles are of different devices: /device:TPU:8 before, /device:TPU:32 now
where the time goes in v11:
time: 105 us; the launch traced here: 104 us
  blocking collectives  91.9 us (88%)
  Pallas kernels  9.66 us (9%)
  starting transfers between devices  1.92 us (2%)
    all_to_all x1, blocking collectives, on_device(): pieces = lax.all_to_all(weights, 'seg', 0, 0, tiled=True)  29.8 us
    all_to_all x1, blocking collectives, on_device(): terms = lax.all_to_all(grid, 'seg', 0, 0, tiled=True)  19.7 us
    all_to_all x1, blocking collectives, on_device(): lax.all_to_all(keep + other, 'frame', 0, 0, tiled=True, axis_index_groups...  14.9 us
    all_to_all x1, blocking collectives, on_device(): chosen = lax.all_to_all(sent, 'frame', 0, 0, tiled=True)  10.9 us
    all_to_all x1, blocking collectives, on_device(): gram = lax.all_to_all(spread, 'coil', 0, 0, tiled=True)  8.41 us
    all_gather x1, blocking collectives, on_device(): lax.all_gather(jnp.sum(total * total, axis=0, keepdims=True), 'coil', til...  8.13 us
    pallas_call x1, Pallas kernels, on_device(): pl.pallas_call(functools.partial(solve_kernel, part), out_shape=jax.Shape...  3.99 us
    pallas_call x1, Pallas kernels, on_device(): pl.pallas_call(functools.partial(other_gram_kernel, part, frames), in_spe...  2.86 us
  transfers between devices with their start and end apart: 1, of which 0 were waited for; matrix products, arithmetic and copies ran while one was open for 0% of the time, Pallas kernels for 1%

profile of v11, /device:TPU:32, one launch (start us, length us, event | category | flops | bytes accessed | tf_op | source)
XLA Modules:
  0.0 104.2 jit_solution(9183620540612932967)
XLA Ops:
  0.0 0.0 copy-start.2
  0.0 0.0 copy-start.1
  0.0 0.0 copy-start.3
  0.0 0.0 copy-start
  0.0 2.9 %shard_map.64 = (f32[4,104,128]{2,1,0:T(8,128)S(1)}, bf16[4,576,384]{2,1,0:T(8,128)(2,1)S(1)}, bf16[4,8,2,576]{3,2,1,0:T(2,128)(2,1)S(1)}) custom-call(s32[1,4]{1,0:T(1,128)} %reads_ref.5, bf16[8,576,384]{2,1,0:T(8,128)(2,1)} %source_ref.2, bf16[8,8,2,576]{3,2,1,0:T(2,128)(2,1)} %target_ref.1), custom_call_target="tpu_custom_call" | custom-call | flops 198180864 | bytes 1843200 | tf_op jit(solution)/shard_map/pallas_call | solution.py:309
  2.9 1.9 %collective-permute-start = (f32[4,104,128]{2,1,0:T(8,128)S(1)}, f32[4,104,128]{2,1,0:T(8,128)S(1)}, u32[]{:S(2)}, u32[]{:S(2)}) collective-permute-start(f32[4,104,128]{2,1,0:T(8,128)S(1)} %get-tuple-element.13), channel_id=1, source_target_pairs={{0,64},{64,0},{128,192},{192,128},{256,320},{320,256},{384,448},{4... | collective-permute-start | bytes 638984 | tf_op jit(solution)/shard_map/ppermute | solution.py:340
  4.8 1.5 %shard_map.65 = f32[4,104,128]{2,1,0:T(8,128)S(1)} custom-call(s32[1,4]{1,0:T(1,128)} %reads_ref.5, bf16[4,576,384]{2,1,0:T(8,128)(2,1)S(1)} %get-tuple-element.11.held_ref, bf16[4,8,2,576]{3,2,1,0:T(2,128)(2,1)S(1)} %get-tuple-element.12.goal_ref), custom_call_target="tpu_custom_call" | custom-call | flops 198180864 | bytes 1843200 | tf_op jit(solution)/shard_map/pallas_call | solution.py:332
  6.3 0.0 collective-permute-done
  6.3 14.9 %all_to_all.25.partial_ref = f32[4,104,128]{2,1,0:T(8,128)S(1)} all-to-all(f32[4,104,128]{2,1,0:T(8,128)S(1)} %add.18), channel_id=1, replica_groups={{0,128,256,384},{64,192,320,448},{1,129,257,385},{65,193,321,449},{2,13..., dimensions={0} | all-to-all | bytes 425984 | tf_op jit(solution)/shard_map/all_to_all | solution.py:342
  21.3 8.4 %all_to_all.26.gram_ref = f32[4,72,128]{2,1,0:T(8,128)S(1)} all-to-all(f32[4,72,128]{2,1,0:T(8,128)S(1)} %get-tuple-element.15), channel_id=1, replica_groups=mesh['frame'=8,'seg'=16,'coil'=4] {'coil'}, dimensions={0} | all-to-all | bytes 294912 | tf_op jit(solution)/shard_map/all_to_all | solution.py:354
  29.7 4.0 %shard_map.67 = bf16[16,8,384]{2,1,0:T(8,128)(2,1)S(1)} custom-call(f32[4,72,128]{2,1,0:T(8,128)S(1)} %all_to_all.26.gram_ref, f32[24,128]{1,0:T(8,128)S(1)} %get-tuple-element.16.rhs_ref), custom_call_target="tpu_custom_call" | custom-call | tf_op jit(solution)/shard_map/pallas_call | solution.py:355
  33.7 29.8 %all_to_all.27.piece_ref = bf16[16,8,384]{2,1,0:T(8,128)(2,1)S(1)} all-to-all(bf16[16,8,384]{2,1,0:T(8,128)(2,1)S(1)} %shard_map.67), channel_id=1, replica_groups=mesh['frame'=8,'seg'=16,'coil'=4] {'seg'}, dimensions={0} | all-to-all | bytes 196608 | tf_op jit(solution)/shard_map/all_to_all | solution.py:365
  63.5 0.4 shard_map.68
  63.8 10.9 %all_to_all.28.weights_ref = bf16[8,4,8,384]{3,2,1,0:T(8,128)(2,1)S(1)} all-to-all(bf16[8,4,8,384]{3,2,1,0:T(8,128)(2,1)S(1)} %shard_map.68), channel_id=1, replica_groups=mesh['frame'=8,'seg'=16,'coil'=4] {'frame'}, dimensions={0} | all-to-all | bytes 393216 | tf_op jit(solution)/shard_map/all_to_all | solution.py:371
  74.7 0.0 copy-done.2
  74.7 0.0 copy-done.1
  74.7 0.0 copy-done.3
  74.7 0.0 copy-done
  74.8 1.0 shard_map.69
  75.7 19.7 %all_to_all.29 = bf16[16,16,256]{2,1,0:T(8,128)(2,1)S(1)} all-to-all(bf16[16,16,256]{2,1,0:T(8,128)(2,1)S(1)} %shard_map.69), channel_id=1, replica_groups=mesh['frame'=8,'seg'=16,'coil'=4] {'seg'}, dimensions={0} | all-to-all | bytes 262144 | tf_op jit(solution)/shard_map/all_to_all | solution.py:377
  95.5 8.1 %all-gather.1 = f32[4,1,256]{2,1,0:T(1,128)S(1)} all-gather(f32[1,1,256]{2,1,0:T(1,128)S(1)} %bitcast.2), channel_id=2, replica_groups=mesh['frame'=8,'seg'=16,'coil'=4] {'coil'}, dimensions={0}, use_global_device_ids=true | all-gather | bytes 5120 | tf_op jit(solution)/shard_map/all_gather | solution.py:379
  103.7 0.6 add_sqrt_fusion
  (5 shorter events, 0.1 us)
Async XLA Ops:
  0.0 74.7 %copy-start.2 = (s32[1,4]{1,0:T(1,128)S(1)}, s32[1,4]{1,0:T(1,128)}, u32[]{:S(2)}) copy-start(s32[1,4]{1,0:T(1,128)} %reads_ref.5) | copy-start | bytes 52
  0.0 74.7 %copy-start.1 = (bf16[1,4,256,128]{3,2,1,0:T(8,128)(2,1)S(1)}, bf16[1,4,256,128]{3,2,1,0:T(8,128)(2,1)}, u32[]{:S(2)}) copy-start(bf16[1,4,256,128]{3,2,1,0:T(8,128)(2,1)} %interp_ref.1) | copy-start | bytes 786436
  0.0 74.7 %copy-start.3 = (s32[1,4]{1,0:T(1,128)S(1)}, s32[1,4]{1,0:T(1,128)}, u32[]{:S(2)}) copy-start(s32[1,4]{1,0:T(1,128)} %places_ref.1) | copy-start | bytes 52
  0.0 74.7 %copy-start = (bf16[1,4,128,384]{3,2,1,0:T(8,128)(2,1)S(1)}, bf16[1,4,128,384]{3,2,1,0:T(8,128)(2,1)}, u32[]{:S(2)}) copy-start(bf16[1,4,128,384]{3,2,1,0:T(8,128)(2,1)} %source_ref.3) | copy-start | bytes 1179652
  2.9 3.4 %collective-permute-start = (f32[4,104,128]{2,1,0:T(8,128)S(1)}, f32[4,104,128]{2,1,0:T(8,128)S(1)}, u32[]{:S(2)}, u32[]{:S(2)}) collective-permute-start(f32[4,104,128]{2,1,0:T(8,128)S(1)} %get-tuple-element.13), channel_id=1, source_target_pairs={{0,64},{64,0},{128,192},{192,128},{256,320},{320,256},{384,448},{4... | collective-permute-start | bytes 638984 | tf_op jit(solution)/shard_map/ppermute | solution.py:340

commit v12 on v11

--- a/solution.py
+++ b/solution.py
@@ -13,6 +13,8 @@
 F32 = jnp.float32
 BF16 = jnp.bfloat16
 LANES = 128
+CHIPS = (0, 3, 1, 2)
+FRAMES = (0, 2, 4, 6, 1, 3, 5, 7)
 SMALL = pltpu.CompilerParams(vmem_limit_bytes=16 * 1024 * 1024)
 
 
@@ -135,7 +137,7 @@
     copies = []
     for slot in range(2 * each):
         own, place = slot // each, slot % each
-        segment = 2 * place + (core if own else 1 - core)
+        segment = 2 * CHIPS[place] + (core if own else 1 - core)
         held = (own_held_ref if own else held_ref).at[place]
         goal = (own_goal_ref if own else goal_ref).at[place]
         copies.append(
@@ -174,8 +176,8 @@
     for copy in range(spread_ref.shape[0]):
         spread_ref[copy] = total[:gram_rows]
     rhs_ref[...] = total[gram_rows:]
-    for chip in range(partial_ref.shape[0]):
-        told_ref[2 * chip : 2 * chip + 2] = partial_ref[chip, rows : rows + 2].astype(jnp.int32)
+    for place, chip in enumerate(CHIPS):
+        told_ref[2 * chip : 2 * chip + 2] = partial_ref[place, rows : rows + 2].astype(jnp.int32)
 
 
 def solve_kernel(part, gram_ref, rhs_ref, out_ref, real_ref, imag_ref, sol_ref):
@@ -248,13 +250,13 @@
 
 def select_kernel(told_ref, piece_ref, out_ref):
     pieces = [piece_ref[place].astype(F32) for place in range(piece_ref.shape[0])]
-    for frame in range(out_ref.shape[0]):
+    for position, frame in enumerate(FRAMES):
         for slot in range(out_ref.shape[1]):
             wanted = jnp.broadcast_to(told_ref[frame : frame + 1, slot : slot + 1], pieces[0].shape)
             chosen = pieces[0]
             for place in range(1, len(pieces)):
                 chosen = jnp.where(wanted == place, pieces[place], chosen)
-            out_ref[frame, slot] = chosen.astype(BF16)
+            out_ref[position, slot] = chosen.astype(BF16)
 
 
 def fill_kernel(reads_ref, places_ref, weights_ref, source_ref, interp_ref, out_ref):
@@ -264,8 +266,9 @@
     for slot in range(slots):
         holder = jnp.broadcast_to(reads_ref[:, slot : slot + 1] & (frames - 1), (coils, depth))
         chosen = weights_ref[0, slot].astype(F32)
-        for frame in range(1, frames):
-            chosen = jnp.where(holder == frame, weights_ref[frame, slot].astype(F32), chosen)
+        for position, frame in enumerate(FRAMES):
+            if position:
+                chosen = jnp.where(holder == frame, weights_ref[position, slot].astype(F32), chosen)
         real, imag = chosen[:, :width], chosen[:, width:]
         matrix = jnp.concatenate(
             [jnp.concatenate([real, -imag], axis=1), jnp.concatenate([imag, real], axis=1)], axis=0
@@ -338,7 +341,7 @@
         cost_estimate=cost,
     )(listed, own_held, own_goal)
     other = lax.ppermute(send, "frame", [(frame, frame ^ 1) for frame in range(frames)])
-    chips = [[2 * chip + core for chip in range(frames // 2)] for core in range(2)]
+    chips = [[2 * chip + core for chip in CHIPS] for core in range(2)]
     received = lax.all_to_all(
         keep + other, "frame", 0, 0, tiled=True, axis_index_groups=chips
     )
@@ -368,7 +371,9 @@
         out_shape=jax.ShapeDtypeStruct((frames, slots, coils, depth), BF16),
         compiler_params=SMALL,
     )(told, pieces)
-    chosen = lax.all_to_all(sent, "frame", 0, 0, tiled=True)
+    chosen = lax.all_to_all(
+        sent, "frame", 0, 0, tiled=True, axis_index_groups=[list(FRAMES)]
+    )
     grid = pl.pallas_call(
         fill_kernel,
         out_shape=jax.ShapeDtypeStruct((segs, 2 * coils, cells), BF16),

time: 105 us -> 106 us (level)
  blocking collectives: 91.9 us -> 93 us
    all_to_all x1, blocking collectives: 19.7 us -> 22 us  [on_device(): terms = lax.all_to_all(grid, 'seg', 0, 0, tiled=True)]
    all_to_all x1, blocking collectives: 10.9 us -> 9.2 us  [on_device(): lax.all_to_all(sent, 'frame', 0, 0, tiled=True, axis_index_groups=[list(F...]
where the time goes in v12:
time: 106 us; the launch traced here: 105 us
  blocking collectives  93 us (88%)
  Pallas kernels  9.66 us (9%)
  starting transfers between devices  1.92 us (2%)
    all_to_all x1, blocking collectives, on_device(): pieces = lax.all_to_all(weights, 'seg', 0, 0, tiled=True)  30.1 us
    all_to_all x1, blocking collectives, on_device(): terms = lax.all_to_all(grid, 'seg', 0, 0, tiled=True)  22 us
    all_to_all x1, blocking collectives, on_device(): lax.all_to_all(keep + other, 'frame', 0, 0, tiled=True, axis_index_groups...  15.2 us
    all_to_all x1, blocking collectives, on_device(): lax.all_to_all(sent, 'frame', 0, 0, tiled=True, axis_index_groups=[list(F...  9.2 us
    all_to_all x1, blocking collectives, on_device(): gram = lax.all_to_all(spread, 'coil', 0, 0, tiled=True)  8.41 us
    all_gather x1, blocking collectives, on_device(): lax.all_gather(jnp.sum(total * total, axis=0, keepdims=True), 'coil', til...  8.14 us
    pallas_call x1, Pallas kernels, on_device(): pl.pallas_call(functools.partial(solve_kernel, part), out_shape=jax.Shape...  3.99 us
    pallas_call x1, Pallas kernels, on_device(): pl.pallas_call(functools.partial(other_gram_kernel, part, frames), in_spe...  2.86 us
  transfers between devices with their start and end apart: 1, of which 0 were waited for; matrix products, arithmetic and copies ran while one was open for 0% of the time, Pallas kernels for 1%

profile of v12, /device:TPU:32, one launch (start us, length us, event | category | flops | bytes accessed | tf_op | source)
XLA Modules:
  0.0 105.4 jit_solution(17579364871264260234)
XLA Ops:
  0.0 0.0 copy-start.2
  0.0 0.0 copy-start.1
  0.0 0.0 copy-start.3
  0.0 0.0 copy-start
  0.0 2.9 %shard_map.64 = (f32[4,104,128]{2,1,0:T(8,128)S(1)}, bf16[4,576,384]{2,1,0:T(8,128)(2,1)S(1)}, bf16[4,8,2,576]{3,2,1,0:T(2,128)(2,1)S(1)}) custom-call(s32[1,4]{1,0:T(1,128)} %reads_ref.5, bf16[8,576,384]{2,1,0:T(8,128)(2,1)} %source_ref.2, bf16[8,8,2,576]{3,2,1,0:T(2,128)(2,1)} %target_ref.1), custom_call_target="tpu_custom_call" | custom-call | flops 198180864 | bytes 1843200 | tf_op jit(solution)/shard_map/pallas_call | solution.py:312
  2.9 1.9 %collective-permute-start = (f32[4,104,128]{2,1,0:T(8,128)S(1)}, f32[4,104,128]{2,1,0:T(8,128)S(1)}, u32[]{:S(2)}, u32[]{:S(2)}) collective-permute-start(f32[4,104,128]{2,1,0:T(8,128)S(1)} %get-tuple-element.13), channel_id=1, source_target_pairs={{0,64},{64,0},{128,192},{192,128},{256,320},{320,256},{384,448},{4... | collective-permute-start | bytes 638984 | tf_op jit(solution)/shard_map/ppermute | solution.py:343
  4.8 1.5 %shard_map.65 = f32[4,104,128]{2,1,0:T(8,128)S(1)} custom-call(s32[1,4]{1,0:T(1,128)} %reads_ref.5, bf16[4,576,384]{2,1,0:T(8,128)(2,1)S(1)} %get-tuple-element.11.held_ref, bf16[4,8,2,576]{3,2,1,0:T(2,128)(2,1)S(1)} %get-tuple-element.12.goal_ref), custom_call_target="tpu_custom_call" | custom-call | flops 198180864 | bytes 1843200 | tf_op jit(solution)/shard_map/pallas_call | solution.py:335
  6.3 0.0 collective-permute-done
  6.3 15.2 %all_to_all.25.partial_ref = f32[4,104,128]{2,1,0:T(8,128)S(1)} all-to-all(f32[4,104,128]{2,1,0:T(8,128)S(1)} %add.18), channel_id=1, replica_groups={{0,384,128,256},{64,448,192,320},{1,385,129,257},{65,449,193,321},{2,38..., dimensions={0} | all-to-all | bytes 425984 | tf_op jit(solution)/shard_map/all_to_all | solution.py:345
  21.5 8.4 %all_to_all.26.gram_ref = f32[4,72,128]{2,1,0:T(8,128)S(1)} all-to-all(f32[4,72,128]{2,1,0:T(8,128)S(1)} %get-tuple-element.15), channel_id=1, replica_groups=mesh['frame'=8,'seg'=16,'coil'=4] {'coil'}, dimensions={0} | all-to-all | bytes 294912 | tf_op jit(solution)/shard_map/all_to_all | solution.py:357
  29.9 4.0 %shard_map.67 = bf16[16,8,384]{2,1,0:T(8,128)(2,1)S(1)} custom-call(f32[4,72,128]{2,1,0:T(8,128)S(1)} %all_to_all.26.gram_ref, f32[24,128]{1,0:T(8,128)S(1)} %get-tuple-element.16.rhs_ref), custom_call_target="tpu_custom_call" | custom-call | tf_op jit(solution)/shard_map/pallas_call | solution.py:358
  33.9 30.1 %all_to_all.27.piece_ref = bf16[16,8,384]{2,1,0:T(8,128)(2,1)S(1)} all-to-all(bf16[16,8,384]{2,1,0:T(8,128)(2,1)S(1)} %shard_map.67), channel_id=1, replica_groups=mesh['frame'=8,'seg'=16,'coil'=4] {'seg'}, dimensions={0} | all-to-all | bytes 196608 | tf_op jit(solution)/shard_map/all_to_all | solution.py:368
  64.0 0.4 shard_map.68
  64.3 9.2 %all_to_all.28.weights_ref = bf16[8,4,8,384]{3,2,1,0:T(8,128)(2,1)S(1)} all-to-all(bf16[8,4,8,384]{3,2,1,0:T(8,128)(2,1)S(1)} %shard_map.68), channel_id=1, replica_groups={{0,128,256,384,64,192,320,448},{1,129,257,385,65,193,321,449},{2,130,25..., dimensions={0} | all-to-all | bytes 393216 | tf_op jit(solution)/shard_map/all_to_all | solution.py:374
  73.5 0.0 copy-done.2
  73.5 0.0 copy-done.1
  73.5 0.0 copy-done.3
  73.6 0.0 copy-done
  73.6 1.0 shard_map.69
  74.6 22.0 %all_to_all.29 = bf16[16,16,256]{2,1,0:T(8,128)(2,1)S(1)} all-to-all(bf16[16,16,256]{2,1,0:T(8,128)(2,1)S(1)} %shard_map.69), channel_id=1, replica_groups=mesh['frame'=8,'seg'=16,'coil'=4] {'seg'}, dimensions={0} | all-to-all | bytes 262144 | tf_op jit(solution)/shard_map/all_to_all | solution.py:382
  96.7 8.1 %all-gather.1 = f32[4,1,256]{2,1,0:T(1,128)S(1)} all-gather(f32[1,1,256]{2,1,0:T(1,128)S(1)} %bitcast.2), channel_id=2, replica_groups=mesh['frame'=8,'seg'=16,'coil'=4] {'coil'}, dimensions={0}, use_global_device_ids=true | all-gather | bytes 5120 | tf_op jit(solution)/shard_map/all_gather | solution.py:384
  104.8 0.6 add_sqrt_fusion
  (5 shorter events, 0.1 us)
Async XLA Ops:
  0.0 73.5 %copy-start.2 = (s32[1,4]{1,0:T(1,128)S(1)}, s32[1,4]{1,0:T(1,128)}, u32[]{:S(2)}) copy-start(s32[1,4]{1,0:T(1,128)} %reads_ref.5) | copy-start | bytes 52
  0.0 73.5 %copy-start.1 = (bf16[1,4,256,128]{3,2,1,0:T(8,128)(2,1)S(1)}, bf16[1,4,256,128]{3,2,1,0:T(8,128)(2,1)}, u32[]{:S(2)}) copy-start(bf16[1,4,256,128]{3,2,1,0:T(8,128)(2,1)} %interp_ref.1) | copy-start | bytes 786436
  0.0 73.5 %copy-start.3 = (s32[1,4]{1,0:T(1,128)S(1)}, s32[1,4]{1,0:T(1,128)}, u32[]{:S(2)}) copy-start(s32[1,4]{1,0:T(1,128)} %places_ref.1) | copy-start | bytes 52
  0.0 73.5 %copy-start = (bf16[1,4,128,384]{3,2,1,0:T(8,128)(2,1)S(1)}, bf16[1,4,128,384]{3,2,1,0:T(8,128)(2,1)}, u32[]{:S(2)}) copy-start(bf16[1,4,128,384]{3,2,1,0:T(8,128)(2,1)} %source_ref.3) | copy-start | bytes 1179652
  2.9 3.4 %collective-permute-start = (f32[4,104,128]{2,1,0:T(8,128)S(1)}, f32[4,104,128]{2,1,0:T(8,128)S(1)}, u32[]{:S(2)}, u32[]{:S(2)}) collective-permute-start(f32[4,104,128]{2,1,0:T(8,128)S(1)} %get-tuple-element.13), channel_id=1, source_target_pairs={{0,64},{64,0},{128,192},{192,128},{256,320},{320,256},{384,448},{4... | collective-permute-start | bytes 638984 | tf_op jit(solution)/shard_map/ppermute | solution.py:343

commit v13 on v11

--- a/solution.py
+++ b/solution.py
@@ -49,51 +49,36 @@
     )
 
 
-def gram_sums(part, groups, held_ref, goal_ref, turned_ref, out_ref, copies):
-    coil = lax.axis_index("coil")
+def gram_sums(groups, held_ref, goal_ref, out_ref, copies):
     depth = held_ref.shape[2]
     width = depth // 2
-    half = part // 2
-    base = part + half
+    half = width // 2
+    base = width + half
     coils = goal_ref.shape[1]
-    across = lax.broadcasted_iota(jnp.int32, (part, width), 1)
-    down = lax.broadcasted_iota(jnp.int32, (part, width), 0) + coil * part
-    first = pl.multiple_of(coil * part, 16)
-    second = pl.multiple_of(width + coil * part, 16)
+    across = lax.broadcasted_iota(jnp.int32, (width, width), 1)
+    down = lax.broadcasted_iota(jnp.int32, (width, width), 0)
     for slots in groups:
         for slot in slots:
             for copy in copies[slot]:
                 copy.wait()
-        lefts = []
-        for slot in slots:
-            turned_ref[slot] = held_ref[slot].T
-            lefts.append(
-                jnp.concatenate(
-                    [
-                        turned_ref[slot, pl.ds(first, part)],
-                        turned_ref[slot, pl.ds(second, part)],
-                        goal_ref[slot, :, 0, :],
-                        goal_ref[slot, :, 1, :],
-                    ],
-                    axis=0,
-                )
+        turned = [held_ref[slot].T for slot in slots]
+        for slot, flipped in zip(slots, turned):
+            out = out_ref.at[slot]
+            source = held_ref[slot]
+            left = jnp.concatenate(
+                [flipped[:width], goal_ref[slot, :, 0, :], goal_ref[slot, :, 1, :]], axis=0
             )
-        products = [
-            jnp.dot(left, held_ref[slot], preferred_element_type=F32)
-            for left, slot in zip(lefts, slots)
-        ]
-        for slot, sums in zip(slots, products):
-            out = out_ref.at[slot]
-            top, bottom = sums[:part], sums[part : 2 * part]
-            gram_real = top[:, :width] + bottom[:, width:]
-            gram_imag = top[:, width:] - bottom[:, :width]
+            top = jnp.dot(left, source, preferred_element_type=F32)
+            bottom = jnp.dot(flipped[width:], source, preferred_element_type=F32)
+            gram_real = top[:width, :width] + bottom[:, width:]
+            gram_imag = top[:width, width:] - bottom[:, :width]
             packed = jnp.where(across <= down, gram_real, gram_imag)
-            proj_real = sums[2 * part : 2 * part + coils]
-            proj_imag = sums[2 * part + coils :]
+            proj_real = top[width : width + coils]
+            proj_imag = top[width + coils :]
             rhs_real = proj_real[:, :width] + proj_imag[:, width:]
             rhs_imag = proj_imag[:, :width] - proj_real[:, width:]
-            out[:part] = packed[:, :LANES]
-            out[part:base] = jnp.concatenate(
+            out[:width] = packed[:, :LANES]
+            out[width:base] = jnp.concatenate(
                 [packed[:half, LANES:], packed[half:, LANES:]], axis=1
             )
             out[base : base + coils] = rhs_real[:, :LANES]
@@ -115,7 +100,6 @@
 
 
 def other_gram_kernel(
-    part,
     frames,
     reads_ref,
     source_ref,
@@ -125,7 +109,6 @@
     own_goal_ref,
     held_ref,
     goal_ref,
-    turned_ref,
     read_ref,
     sem,
     read_sem,
@@ -149,7 +132,7 @@
             copy.start()
     listing = pltpu.make_async_copy(reads_ref, read_ref, read_sem)
     listing.start()
-    gram_sums(part, ((0,), (1, 2, 3)), held_ref, goal_ref, turned_ref, out_ref, copies)
+    gram_sums(((0,), (1, 2, 3)), held_ref, goal_ref, out_ref, copies)
     listing.wait()
     tell(frames, read_ref, out_ref)
     for pair in copies[each:]:
@@ -157,41 +140,31 @@
             copy.wait()
 
 
-def own_gram_kernel(part, frames, reads_ref, held_ref, goal_ref, out_ref, turned_ref, read_ref, read_sem):
+def own_gram_kernel(frames, reads_ref, held_ref, goal_ref, out_ref, read_ref, read_sem):
     listing = pltpu.make_async_copy(reads_ref, read_ref, read_sem)
     listing.start()
     slots = tuple(range(out_ref.shape[0]))
-    gram_sums(part, (slots,), held_ref, goal_ref, turned_ref, out_ref, [() for _ in slots])
+    gram_sums((slots,), held_ref, goal_ref, out_ref, [() for _ in slots])
     listing.wait()
     tell(frames, read_ref, out_ref)
 
 
-def sum_kernel(gram_rows, partial_ref, spread_ref, rhs_ref, told_ref):
-    rows = gram_rows + rhs_ref.shape[0]
+def solve_kernel(partial_ref, out_ref, told_ref, real_ref, imag_ref, sol_ref):
+    width = real_ref.shape[0]
+    half = width // 2
+    coils = out_ref.shape[1]
+    base = width + half
+    rows = base + 3 * coils
+    for chip in range(partial_ref.shape[0]):
+        told_ref[2 * chip : 2 * chip + 2] = partial_ref[chip, rows : rows + 2].astype(jnp.int32)
     total = partial_ref[0, :rows]
     for chip in range(1, partial_ref.shape[0]):
         total = total + partial_ref[chip, :rows]
-    for copy in range(spread_ref.shape[0]):
-        spread_ref[copy] = total[:gram_rows]
-    rhs_ref[...] = total[gram_rows:]
-    for chip in range(partial_ref.shape[0]):
-        told_ref[2 * chip : 2 * chip + 2] = partial_ref[chip, rows : rows + 2].astype(jnp.int32)
-
-
-def solve_kernel(part, gram_ref, rhs_ref, out_ref, real_ref, imag_ref, sol_ref):
-    width = 4 * part
-    half = part // 2
-    coils = rhs_ref.shape[0] // 3
-    pieces = []
-    for coil in range(4):
-        block = gram_ref[coil]
-        tail = block[part:]
-        pieces.append(
-            jnp.concatenate(
-                [block[:part], jnp.concatenate([tail[:, :64], tail[:, 64:]], axis=0)], axis=1
-            )
-        )
-    packed = jnp.concatenate(pieces, axis=0)
+    tail = total[width:base]
+    rhs = total[base:]
+    packed = jnp.concatenate(
+        [total[:width], jnp.concatenate([tail[:, :64], tail[:, 64:]], axis=0)], axis=1
+    )
     flipped = packed.T
     down = lax.broadcasted_iota(jnp.int32, (width, width), 0)
     across = lax.broadcasted_iota(jnp.int32, (width, width), 1)
@@ -203,8 +176,8 @@
     imag = jnp.where(across < down, -flipped, packed)
     real_ref[...] = (real + jnp.where(across == down, shift, 0.0)) * scale
     imag_ref[...] = jnp.where(across == down, 0.0, imag) * scale
-    rhs_real = jnp.concatenate([rhs_ref[:coils], rhs_ref[2 * coils :, :64]], axis=1)
-    rhs_imag = jnp.concatenate([rhs_ref[coils : 2 * coils], rhs_ref[2 * coils :, 64:]], axis=1)
+    rhs_real = jnp.concatenate([rhs[:coils], rhs[2 * coils :, :64]], axis=1)
+    rhs_imag = jnp.concatenate([rhs[coils : 2 * coils], rhs[2 * coils :, 64:]], axis=1)
     sol_ref[...] = jnp.concatenate([rhs_real, rhs_imag], axis=0) * scale
 
     def step(product, spread):
@@ -284,13 +257,10 @@
 def on_device(cal_source, cal_target, app_source, readers, blocks, interp):
     frames = lax.axis_size("frame")
     segs = lax.axis_size("seg")
-    coil_count = lax.axis_size("coil")
     held, samples, depth = cal_source.shape
     coils = cal_target.shape[1]
     width = depth // 2
-    part = width // coil_count
-    gram_rows = part + part // 2
-    rows = gram_rows + 3 * coils + 8
+    rows = width + width // 2 + 3 * coils + 8
     slots = readers.shape[1]
     cells = interp.shape[2]
 
@@ -300,14 +270,13 @@
     hbm = pl.BlockSpec(memory_space=pltpu.HBM)
     vmem = pl.BlockSpec(memory_space=pltpu.VMEM)
     reading = [pltpu.SMEM(readers.shape, jnp.int32)]
-    turned = pltpu.VMEM((each, depth, samples), BF16)
     cost = pl.CostEstimate(
-        flops=2 * each * samples * depth * 2 * (part + coils),
+        flops=2 * each * samples * depth * (depth + 2 * coils),
         bytes_accessed=2 * each * samples * (depth + 2 * coils),
         transcendentals=0,
     )
     send, own_held, own_goal = pl.pallas_call(
-        functools.partial(other_gram_kernel, part, frames),
+        functools.partial(other_gram_kernel, frames),
         in_specs=[hbm, hbm, hbm],
         out_shape=[
             block,
@@ -317,7 +286,6 @@
         scratch_shapes=[
             pltpu.VMEM((each, samples, depth), BF16),
             pltpu.VMEM((each, coils, 2, samples), BF16),
-            turned,
             *reading,
             pltpu.SemaphoreType.DMA((2, held)),
             pltpu.SemaphoreType.DMA,
@@ -330,10 +298,10 @@
         pltpu.with_memory_space_constraint(cal_target, pltpu.HBM),
     )
     keep = pl.pallas_call(
-        functools.partial(own_gram_kernel, part, frames),
+        functools.partial(own_gram_kernel, frames),
         in_specs=[hbm, vmem, vmem],
         out_shape=block,
-        scratch_shapes=[turned, *reading, pltpu.SemaphoreType.DMA],
+        scratch_shapes=[*reading, pltpu.SemaphoreType.DMA],
         compiler_params=SMALL,
         cost_estimate=cost,
     )(listed, own_held, own_goal)
@@ -342,26 +310,19 @@
     received = lax.all_to_all(
         keep + other, "frame", 0, 0, tiled=True, axis_index_groups=chips
     )
-    spread, rhs, told = pl.pallas_call(
-        functools.partial(sum_kernel, gram_rows),
+    weights, told = pl.pallas_call(
+        solve_kernel,
         out_shape=[
-            jax.ShapeDtypeStruct((coil_count, gram_rows, LANES), F32),
-            jax.ShapeDtypeStruct((3 * coils, LANES), F32),
+            jax.ShapeDtypeStruct((segs, coils, depth), BF16),
             jax.ShapeDtypeStruct((frames, LANES), jnp.int32),
         ],
-        compiler_params=SMALL,
-    )(received)
-    gram = lax.all_to_all(spread, "coil", 0, 0, tiled=True)
-    weights = pl.pallas_call(
-        functools.partial(solve_kernel, part),
-        out_shape=jax.ShapeDtypeStruct((segs, coils, depth), BF16),
         scratch_shapes=[
             pltpu.VMEM((width, width), F32),
             pltpu.VMEM((width, width), F32),
             pltpu.VMEM((2 * coils, width), F32),
         ],
         compiler_params=SMALL,
-    )(gram, rhs)
+    )(received)
     pieces = lax.all_to_all(weights, "seg", 0, 0, tiled=True)
     sent = pl.pallas_call(
         select_kernel,

time: 105 us -> 106 us (level)
    all_to_all x1, blocking collectives: 14.9 us -> 24.1 us  [on_device(): lax.all_to_all(keep + other, 'frame', 0, 0, tiled=True, axis_index_groups...]
    all_to_all x1 -> x0, blocking collectives: 8.41 us -> none  [on_device(): gram = lax.all_to_all(spread, 'coil', 0, 0, tiled=True)]
    all_to_all x1, blocking collectives: 29.8 us -> 27.7 us  [on_device(): pieces = lax.all_to_all(weights, 'seg', 0, 0, tiled=True)]
    all_gather x1, blocking collectives: 8.13 us -> 9.98 us  [on_device(): lax.all_gather(jnp.sum(total * total, axis=0, keepdims=True), 'coil', til...]
    pallas_call x4 -> x3, Pallas kernels: 8.31 us -> 9.14 us  [the longest x1 3.97 us: on_device(): pl.pallas_call(solve_kernel, out_shape=[jax.ShapeDtypeStruct((segs, coils...]
  transfers between devices with their start and end apart: 1 -> 1, of which waited for: 0 -> 1; matrix products, arithmetic and copies ran while one was open for 0% -> 0% of each run, Pallas kernels for 1% -> 2%
where the time goes in v13:
time: 106 us
  blocking collectives  92.1 us (87%)
  Pallas kernels  10.5 us (10%)
  starting transfers between devices  1.92 us (2%)
    all_to_all x1, blocking collectives, on_device(): pieces = lax.all_to_all(weights, 'seg', 0, 0, tiled=True)  27.7 us
    all_to_all x1, blocking collectives, on_device(): lax.all_to_all(keep + other, 'frame', 0, 0, tiled=True, axis_index_groups...  24.1 us
    all_to_all x1, blocking collectives, on_device(): terms = lax.all_to_all(grid, 'seg', 0, 0, tiled=True)  19.5 us
    all_to_all x1, blocking collectives, on_device(): chosen = lax.all_to_all(sent, 'frame', 0, 0, tiled=True)  10.8 us
    all_gather x1, blocking collectives, on_device(): lax.all_gather(jnp.sum(total * total, axis=0, keepdims=True), 'coil', til...  9.98 us
    pallas_call x1, Pallas kernels, on_device(): pl.pallas_call(solve_kernel, out_shape=[jax.ShapeDtypeStruct((segs, coils...  3.97 us
    pallas_call x1, Pallas kernels, on_device(): pl.pallas_call(functools.partial(other_gram_kernel, frames), in_specs=[hb...  3.37 us
  transfers between devices with their start and end apart: 1, of which 1 were waited for; matrix products, arithmetic and copies ran while one was open for 0% of the time, Pallas kernels for 2%

profile of v13, /device:TPU:32, one launch (start us, length us, event | category | flops | bytes accessed | tf_op | source)
XLA Modules:
  0.0 105.6 jit_solution(10002079152617731217)
XLA Ops:
  0.0 3.4 %shard_map.64 = (f32[4,320,128]{2,1,0:T(8,128)S(1)}, bf16[4,576,384]{2,1,0:T(8,128)(2,1)S(1)}, bf16[4,8,2,576]{3,2,1,0:T(2,128)(2,1)S(1)}) custom-call(s32[1,4]{1,0:T(1,128)} %reads_ref.5, bf16[8,576,384]{2,1,0:T(8,128)(2,1)} %source_ref.2, bf16[8,8,2,576]{3,2,1,0:T(2,128)(2,1)} %target_ref.1), custom_call_target="tpu_custom_call" | custom-call | flops 707788800 | bytes 1843200 | tf_op jit(solution)/shard_map/pallas_call | solution.py:278
  3.4 1.9 %collective-permute-start = (f32[4,320,128]{2,1,0:T(8,128)S(1)}, f32[4,320,128]{2,1,0:T(8,128)S(1)}, u32[]{:S(2)}, u32[]{:S(2)}) collective-permute-start(f32[4,320,128]{2,1,0:T(8,128)S(1)} %get-tuple-element.12), channel_id=1, source_target_pairs={{0,64},{64,0},{128,192},{192,128},{256,320},{320,256},{384,448},{4... | collective-permute-start | bytes 1966088 | tf_op jit(solution)/shard_map/ppermute | solution.py:308
  5.3 0.0 copy-start
  5.3 0.0 copy-start.1
  5.3 0.0 copy-start.2
  5.3 0.0 copy-start.3
  5.4 1.8 %shard_map.65 = f32[4,320,128]{2,1,0:T(8,128)S(1)} custom-call(s32[1,4]{1,0:T(1,128)} %reads_ref.5, bf16[4,576,384]{2,1,0:T(8,128)(2,1)S(1)} %get-tuple-element.10.held_ref, bf16[4,8,2,576]{3,2,1,0:T(2,128)(2,1)S(1)} %get-tuple-element.11.goal_ref), custom_call_target="tpu_custom_call" | custom-call | flops 707788800 | bytes 1843200 | tf_op jit(solution)/shard_map/pallas_call | solution.py:300
  7.2 0.2 collective-permute-done
  7.4 0.1 add.18
  7.5 24.1 %all_to_all.20.partial_ref = f32[4,320,128]{2,1,0:T(8,128)S(1)} all-to-all(f32[4,320,128]{2,1,0:T(8,128)S(1)} %add.18), channel_id=1, replica_groups={{0,128,256,384},{64,192,320,448},{1,129,257,385},{65,193,321,449},{2,13..., dimensions={0} | all-to-all | bytes 1310720 | tf_op jit(solution)/shard_map/all_to_all | solution.py:310
  31.6 4.0 %shard_map.66 = (bf16[16,8,384]{2,1,0:T(8,128)(2,1)S(1)}, s32[8,128]{1,0:T(8,128)S(1)}) custom-call(f32[4,320,128]{2,1,0:T(8,128)S(1)} %all_to_all.20.partial_ref), custom_call_target="tpu_custom_call" | custom-call | tf_op jit(solution)/shard_map/pallas_call | solution.py:313
  35.6 27.7 %all_to_all.21.piece_ref = bf16[16,8,384]{2,1,0:T(8,128)(2,1)S(1)} all-to-all(bf16[16,8,384]{2,1,0:T(8,128)(2,1)S(1)} %get-tuple-element.14), channel_id=1, replica_groups=mesh['frame'=8,'seg'=16,'coil'=4] {'seg'}, dimensions={0} | all-to-all | bytes 196608 | tf_op jit(solution)/shard_map/all_to_all | solution.py:326
  63.2 0.4 shard_map.67
  63.6 10.8 %all_to_all.22.weights_ref = bf16[8,4,8,384]{3,2,1,0:T(8,128)(2,1)S(1)} all-to-all(bf16[8,4,8,384]{3,2,1,0:T(8,128)(2,1)S(1)} %shard_map.67), channel_id=1, replica_groups=mesh['frame'=8,'seg'=16,'coil'=4] {'frame'}, dimensions={0} | all-to-all | bytes 393216 | tf_op jit(solution)/shard_map/all_to_all | solution.py:332
  74.4 0.0 copy-done
  74.4 0.0 copy-done.1
  74.4 0.0 copy-done.2
  74.4 0.0 copy-done.3
  74.4 1.0 shard_map.68
  75.4 19.5 %all_to_all.23 = bf16[16,16,256]{2,1,0:T(8,128)(2,1)S(1)} all-to-all(bf16[16,16,256]{2,1,0:T(8,128)(2,1)S(1)} %shard_map.68), channel_id=1, replica_groups=mesh['frame'=8,'seg'=16,'coil'=4] {'seg'}, dimensions={0} | all-to-all | bytes 262144 | tf_op jit(solution)/shard_map/all_to_all | solution.py:338
  95.0 10.0 %all-gather.1 = f32[4,1,256]{2,1,0:T(1,128)S(1)} all-gather(f32[1,1,256]{2,1,0:T(1,128)S(1)} %bitcast.2), channel_id=2, replica_groups=mesh['frame'=8,'seg'=16,'coil'=4] {'coil'}, dimensions={0}, use_global_device_ids=true | all-gather | bytes 5120 | tf_op jit(solution)/shard_map/all_gather | solution.py:340
  105.0 0.6 add_sqrt_fusion
  (3 shorter events, 0.1 us)
Async XLA Ops:
  3.4 4.0 %collective-permute-start = (f32[4,320,128]{2,1,0:T(8,128)S(1)}, f32[4,320,128]{2,1,0:T(8,128)S(1)}, u32[]{:S(2)}, u32[]{:S(2)}) collective-permute-start(f32[4,320,128]{2,1,0:T(8,128)S(1)} %get-tuple-element.12), channel_id=1, source_target_pairs={{0,64},{64,0},{128,192},{192,128},{256,320},{320,256},{384,448},{4... | collective-permute-start | bytes 1966088 | tf_op jit(solution)/shard_map/ppermute | solution.py:308
  5.3 69.1 %copy-start = (bf16[1,4,128,384]{3,2,1,0:T(8,128)(2,1)S(1)}, bf16[1,4,128,384]{3,2,1,0:T(8,128)(2,1)}, u32[]{:S(2)}) copy-start(bf16[1,4,128,384]{3,2,1,0:T(8,128)(2,1)} %source_ref.3) | copy-start | bytes 1179652
  5.3 69.1 %copy-start.1 = (bf16[1,4,256,128]{3,2,1,0:T(8,128)(2,1)S(1)}, bf16[1,4,256,128]{3,2,1,0:T(8,128)(2,1)}, u32[]{:S(2)}) copy-start(bf16[1,4,256,128]{3,2,1,0:T(8,128)(2,1)} %interp_ref.1) | copy-start | bytes 786436
  5.3 69.1 %copy-start.2 = (s32[1,4]{1,0:T(1,128)S(1)}, s32[1,4]{1,0:T(1,128)}, u32[]{:S(2)}) copy-start(s32[1,4]{1,0:T(1,128)} %reads_ref.5) | copy-start | bytes 52
  5.3 69.1 %copy-start.3 = (s32[1,4]{1,0:T(1,128)S(1)}, s32[1,4]{1,0:T(1,128)}, u32[]{:S(2)}) copy-start(s32[1,4]{1,0:T(1,128)} %places_ref.1) | copy-start | bytes 52

commit v14 on v11

--- a/solution.py
+++ b/solution.py
@@ -49,7 +49,7 @@
     )
 
 
-def gram_sums(part, groups, held_ref, goal_ref, turned_ref, out_ref, copies):
+def gram_sums(part, groups, picked, held_ref, goal_ref, turned_ref, out_ref, copies):
     coil = lax.axis_index("coil")
     depth = held_ref.shape[2]
     width = depth // 2
@@ -60,23 +60,26 @@
     down = lax.broadcasted_iota(jnp.int32, (part, width), 0) + coil * part
     first = pl.multiple_of(coil * part, 16)
     second = pl.multiple_of(width + coil * part, 16)
+    row = lax.broadcasted_iota(jnp.int32, (2 * part, depth), 0)
+    column = lax.broadcasted_iota(jnp.int32, (2 * part, depth), 1)
+    wanted = coil * part + jnp.where(row < part, row, row - part + width)
+    pick = jnp.where(column == wanted, 1.0, 0.0).astype(BF16)
     for slots in groups:
         for slot in slots:
             for copy in copies[slot]:
                 copy.wait()
         lefts = []
         for slot in slots:
-            turned_ref[slot] = held_ref[slot].T
+            if slot in picked:
+                mine = [across_rows(pick, held_ref[slot]).astype(BF16)]
+            else:
+                turned_ref[slot] = held_ref[slot].T
+                mine = [
+                    turned_ref[slot, pl.ds(first, part)],
+                    turned_ref[slot, pl.ds(second, part)],
+                ]
             lefts.append(
-                jnp.concatenate(
-                    [
-                        turned_ref[slot, pl.ds(first, part)],
-                        turned_ref[slot, pl.ds(second, part)],
-                        goal_ref[slot, :, 0, :],
-                        goal_ref[slot, :, 1, :],
-                    ],
-                    axis=0,
-                )
+                jnp.concatenate([*mine, goal_ref[slot, :, 0, :], goal_ref[slot, :, 1, :]], axis=0)
             )
         products = [
             jnp.dot(left, held_ref[slot], preferred_element_type=F32)
@@ -149,7 +152,7 @@
             copy.start()
     listing = pltpu.make_async_copy(reads_ref, read_ref, read_sem)
     listing.start()
-    gram_sums(part, ((0,), (1, 2, 3)), held_ref, goal_ref, turned_ref, out_ref, copies)
+    gram_sums(part, ((0,), (1, 2, 3)), (), held_ref, goal_ref, turned_ref, out_ref, copies)
     listing.wait()
     tell(frames, read_ref, out_ref)
     for pair in copies[each:]:
@@ -161,7 +164,7 @@
     listing = pltpu.make_async_copy(reads_ref, read_ref, read_sem)
     listing.start()
     slots = tuple(range(out_ref.shape[0]))
-    gram_sums(part, (slots,), held_ref, goal_ref, turned_ref, out_ref, [() for _ in slots])
+    gram_sums(part, (slots,), (2,), held_ref, goal_ref, turned_ref, out_ref, [() for _ in slots])
     listing.wait()
     tell(frames, read_ref, out_ref)
 

time: 105 us -> 104 us (level)
  transfers between devices with their start and end apart: 1 -> 1, of which waited for: 0 -> 1; matrix products, arithmetic and copies ran while one was open for 0% -> 0% of each run, Pallas kernels for 1% -> 1%
where the time goes in v14:
time: 104 us; the launch traced here: 103 us
  blocking collectives  91.1 us (88%)
  Pallas kernels  9.24 us (9%)
  starting transfers between devices  1.92 us (2%)
    all_to_all x1, blocking collectives, on_device(): pieces = lax.all_to_all(weights, 'seg', 0, 0, tiled=True)  29.8 us
    all_to_all x1, blocking collectives, on_device(): terms = lax.all_to_all(grid, 'seg', 0, 0, tiled=True)  19.4 us
    all_to_all x1, blocking collectives, on_device(): lax.all_to_all(keep + other, 'frame', 0, 0, tiled=True, axis_index_groups...  14.6 us
    all_to_all x1, blocking collectives, on_device(): chosen = lax.all_to_all(sent, 'frame', 0, 0, tiled=True)  10.7 us
    all_to_all x1, blocking collectives, on_device(): gram = lax.all_to_all(spread, 'coil', 0, 0, tiled=True)  8.41 us
    all_gather x1, blocking collectives, on_device(): lax.all_gather(jnp.sum(total * total, axis=0, keepdims=True), 'coil', til...  8.13 us
    pallas_call x1, Pallas kernels, on_device(): pl.pallas_call(functools.partial(solve_kernel, part), out_shape=jax.Shape...  4 us
    pallas_call x1, Pallas kernels, on_device(): pl.pallas_call(functools.partial(other_gram_kernel, part, frames), in_spe...  2.86 us
  transfers between devices with their start and end apart: 1, of which 1 were waited for; matrix products, arithmetic and copies ran while one was open for 0% of the time, Pallas kernels for 1%

profile of v14, /device:TPU:32, one launch (start us, length us, event | category | flops | bytes accessed | tf_op | source)
XLA Modules:
  0.0 103.4 jit_solution(7552244583637764652)
XLA Ops:
  0.0 0.0 copy-start.2
  0.0 0.0 copy-start.1
  0.0 0.0 copy-start.3
  0.0 0.0 copy-start
  0.0 2.9 %shard_map.64 = (f32[4,104,128]{2,1,0:T(8,128)S(1)}, bf16[4,576,384]{2,1,0:T(8,128)(2,1)S(1)}, bf16[4,8,2,576]{3,2,1,0:T(2,128)(2,1)S(1)}) custom-call(s32[1,4]{1,0:T(1,128)} %reads_ref.5, bf16[8,576,384]{2,1,0:T(8,128)(2,1)} %source_ref.2, bf16[8,8,2,576]{3,2,1,0:T(2,128)(2,1)} %target_ref.1), custom_call_target="tpu_custom_call" | custom-call | flops 198180864 | bytes 1843200 | tf_op jit(solution)/shard_map/pallas_call | solution.py:312
  2.9 1.9 %collective-permute-start = (f32[4,104,128]{2,1,0:T(8,128)S(1)}, f32[4,104,128]{2,1,0:T(8,128)S(1)}, u32[]{:S(2)}, u32[]{:S(2)}) collective-permute-start(f32[4,104,128]{2,1,0:T(8,128)S(1)} %get-tuple-element.13), channel_id=1, source_target_pairs={{0,64},{64,0},{128,192},{192,128},{256,320},{320,256},{384,448},{4... | collective-permute-start | bytes 638984 | tf_op jit(solution)/shard_map/ppermute | solution.py:343
  4.8 1.0 shard_map.65
  5.8 0.4 collective-permute-done
  6.3 14.6 %all_to_all.25.partial_ref = f32[4,104,128]{2,1,0:T(8,128)S(1)} all-to-all(f32[4,104,128]{2,1,0:T(8,128)S(1)} %add.18), channel_id=1, replica_groups={{0,128,256,384},{64,192,320,448},{1,129,257,385},{65,193,321,449},{2,13..., dimensions={0} | all-to-all | bytes 425984 | tf_op jit(solution)/shard_map/all_to_all | solution.py:345
  20.9 8.4 %all_to_all.26.gram_ref = f32[4,72,128]{2,1,0:T(8,128)S(1)} all-to-all(f32[4,72,128]{2,1,0:T(8,128)S(1)} %get-tuple-element.15), channel_id=1, replica_groups=mesh['frame'=8,'seg'=16,'coil'=4] {'coil'}, dimensions={0} | all-to-all | bytes 294912 | tf_op jit(solution)/shard_map/all_to_all | solution.py:357
  29.3 4.0 %shard_map.67 = bf16[16,8,384]{2,1,0:T(8,128)(2,1)S(1)} custom-call(f32[4,72,128]{2,1,0:T(8,128)S(1)} %all_to_all.26.gram_ref, f32[24,128]{1,0:T(8,128)S(1)} %get-tuple-element.16.rhs_ref), custom_call_target="tpu_custom_call" | custom-call | tf_op jit(solution)/shard_map/pallas_call | solution.py:358
  33.3 29.8 %all_to_all.27.piece_ref = bf16[16,8,384]{2,1,0:T(8,128)(2,1)S(1)} all-to-all(bf16[16,8,384]{2,1,0:T(8,128)(2,1)S(1)} %shard_map.67), channel_id=1, replica_groups=mesh['frame'=8,'seg'=16,'coil'=4] {'seg'}, dimensions={0} | all-to-all | bytes 196608 | tf_op jit(solution)/shard_map/all_to_all | solution.py:368
  63.1 0.4 shard_map.68
  63.5 10.7 %all_to_all.28.weights_ref = bf16[8,4,8,384]{3,2,1,0:T(8,128)(2,1)S(1)} all-to-all(bf16[8,4,8,384]{3,2,1,0:T(8,128)(2,1)S(1)} %shard_map.68), channel_id=1, replica_groups=mesh['frame'=8,'seg'=16,'coil'=4] {'frame'}, dimensions={0} | all-to-all | bytes 393216 | tf_op jit(solution)/shard_map/all_to_all | solution.py:374
  74.2 0.0 copy-done.2
  74.2 0.0 copy-done.1
  74.3 0.0 copy-done.3
  74.3 0.0 copy-done
  74.3 1.0 shard_map.69
  75.3 19.4 %all_to_all.29 = bf16[16,16,256]{2,1,0:T(8,128)(2,1)S(1)} all-to-all(bf16[16,16,256]{2,1,0:T(8,128)(2,1)S(1)} %shard_map.69), channel_id=1, replica_groups=mesh['frame'=8,'seg'=16,'coil'=4] {'seg'}, dimensions={0} | all-to-all | bytes 262144 | tf_op jit(solution)/shard_map/all_to_all | solution.py:380
  94.7 8.1 %all-gather.1 = f32[4,1,256]{2,1,0:T(1,128)S(1)} all-gather(f32[1,1,256]{2,1,0:T(1,128)S(1)} %bitcast.2), channel_id=2, replica_groups=mesh['frame'=8,'seg'=16,'coil'=4] {'coil'}, dimensions={0}, use_global_device_ids=true | all-gather | bytes 5120 | tf_op jit(solution)/shard_map/all_gather | solution.py:382
  102.8 0.6 add_sqrt_fusion
  (5 shorter events, 0.1 us)
Async XLA Ops:
  0.0 74.2 %copy-start.2 = (s32[1,4]{1,0:T(1,128)S(1)}, s32[1,4]{1,0:T(1,128)}, u32[]{:S(2)}) copy-start(s32[1,4]{1,0:T(1,128)} %reads_ref.5) | copy-start | bytes 52
  0.0 74.2 %copy-start.1 = (bf16[1,4,256,128]{3,2,1,0:T(8,128)(2,1)S(1)}, bf16[1,4,256,128]{3,2,1,0:T(8,128)(2,1)}, u32[]{:S(2)}) copy-start(bf16[1,4,256,128]{3,2,1,0:T(8,128)(2,1)} %interp_ref.1) | copy-start | bytes 786436
  0.0 74.2 %copy-start.3 = (s32[1,4]{1,0:T(1,128)S(1)}, s32[1,4]{1,0:T(1,128)}, u32[]{:S(2)}) copy-start(s32[1,4]{1,0:T(1,128)} %places_ref.1) | copy-start | bytes 52
  0.0 74.2 %copy-start = (bf16[1,4,128,384]{3,2,1,0:T(8,128)(2,1)S(1)}, bf16[1,4,128,384]{3,2,1,0:T(8,128)(2,1)}, u32[]{:S(2)}) copy-start(bf16[1,4,128,384]{3,2,1,0:T(8,128)(2,1)} %source_ref.3) | copy-start | bytes 1179652
  2.9 3.4 %collective-permute-start = (f32[4,104,128]{2,1,0:T(8,128)S(1)}, f32[4,104,128]{2,1,0:T(8,128)S(1)}, u32[]{:S(2)}, u32[]{:S(2)}) collective-permute-start(f32[4,104,128]{2,1,0:T(8,128)S(1)} %get-tuple-element.13), channel_id=1, source_target_pairs={{0,64},{64,0},{128,192},{192,128},{256,320},{320,256},{384,448},{4... | collective-permute-start | bytes 638984 | tf_op jit(solution)/shard_map/ppermute | solution.py:343

commit v15 on v14

--- a/solution.py
+++ b/solution.py
@@ -123,15 +123,19 @@
     reads_ref,
     source_ref,
     target_ref,
+    app_ref,
+    interp_ref,
     out_ref,
     own_held_ref,
     own_goal_ref,
+    own_app_ref,
+    own_interp_ref,
     held_ref,
     goal_ref,
     turned_ref,
     read_ref,
     sem,
-    read_sem,
+    late_sem,
 ):
     core = lax.rem(lax.axis_index("frame"), 2)
     each = out_ref.shape[0]
@@ -150,11 +154,18 @@
     for pair in copies:
         for copy in pair:
             copy.start()
-    listing = pltpu.make_async_copy(reads_ref, read_ref, read_sem)
-    listing.start()
+    late = [
+        pltpu.make_async_copy(reads_ref, read_ref, late_sem.at[0]),
+        pltpu.make_async_copy(app_ref, own_app_ref, late_sem.at[1]),
+        pltpu.make_async_copy(interp_ref, own_interp_ref, late_sem.at[2]),
+    ]
+    for copy in late:
+        copy.start()
     gram_sums(part, ((0,), (1, 2, 3)), (), held_ref, goal_ref, turned_ref, out_ref, copies)
-    listing.wait()
+    late[0].wait()
     tell(frames, read_ref, out_ref)
+    for copy in late[1:]:
+        copy.wait()
     for pair in copies[each:]:
         for copy in pair:
             copy.wait()
@@ -199,8 +210,9 @@
     down = lax.broadcasted_iota(jnp.int32, (width, width), 0)
     across = lax.broadcasted_iota(jnp.int32, (width, width), 1)
     diagonal = jnp.where(across == down, packed, 0.0)
-    shift = regular / width * jnp.sum(diagonal)
-    high = jnp.sqrt(jnp.sum(2.0 * (packed * packed) - diagonal * diagonal)) + shift
+    shift = regular / width * jnp.sum(diagonal, keepdims=True)
+    norm = jnp.sum(2.0 * (packed * packed) - diagonal * diagonal, keepdims=True)
+    high = jnp.sqrt(norm) + shift
     scale = 2.0 / (high + shift)
     real = jnp.where(across <= down, packed, flipped)
     imag = jnp.where(across < down, -flipped, packed)
@@ -227,7 +239,7 @@
         imag_ref[...] = factor * (2.0 * imag - (cross - turned))
         return square / (2.0 - square)
 
-    spread = (high - shift) / (high + shift)
+    spread = jnp.sum((high - shift) / (high + shift))
     spread = lax.while_loop(
         lambda spread: spread > 0.99, functools.partial(step, fine_product), spread
     )
@@ -309,13 +321,15 @@
         bytes_accessed=2 * each * samples * (depth + 2 * coils),
         transcendentals=0,
     )
-    send, own_held, own_goal = pl.pallas_call(
+    send, own_held, own_goal, own_app, own_interp = pl.pallas_call(
         functools.partial(other_gram_kernel, part, frames),
-        in_specs=[hbm, hbm, hbm],
+        in_specs=[hbm] * 5,
         out_shape=[
             block,
             jax.ShapeDtypeStruct((each, samples, depth), BF16),
             jax.ShapeDtypeStruct((each, coils, 2, samples), BF16),
+            jax.ShapeDtypeStruct(app_source.shape, BF16),
+            jax.ShapeDtypeStruct(interp.shape, BF16),
         ],
         scratch_shapes=[
             pltpu.VMEM((each, samples, depth), BF16),
@@ -323,7 +337,7 @@
             turned,
             *reading,
             pltpu.SemaphoreType.DMA((2, held)),
-            pltpu.SemaphoreType.DMA,
+            pltpu.SemaphoreType.DMA((3,)),
         ],
         compiler_params=SMALL,
         cost_estimate=cost,
@@ -331,6 +345,8 @@
         listed,
         pltpu.with_memory_space_constraint(cal_source, pltpu.HBM),
         pltpu.with_memory_space_constraint(cal_target, pltpu.HBM),
+        pltpu.with_memory_space_constraint(app_source, pltpu.HBM),
+        pltpu.with_memory_space_constraint(interp, pltpu.HBM),
     )
     keep = pl.pallas_call(
         functools.partial(own_gram_kernel, part, frames),
@@ -376,7 +392,7 @@
         fill_kernel,
         out_shape=jax.ShapeDtypeStruct((segs, 2 * coils, cells), BF16),
         compiler_params=SMALL,
-    )(readers, blocks, chosen, app_source, interp)
+    )(readers, blocks, chosen, own_app, own_interp)
     terms = lax.all_to_all(grid, "seg", 0, 0, tiled=True)
     total = jnp.sum(terms.astype(F32), axis=0)
     power = lax.all_gather(jnp.sum(total * total, axis=0, keepdims=True), "coil", tiled=True)

time: 104 us -> 103 us (level)
  no operation moved by 1% of the time
where the time goes in v15:
time: 103 us
  blocking collectives  90.9 us (88%)
  Pallas kernels  9.14 us (9%)
  starting transfers between devices  1.92 us (2%)
    all_to_all x1, blocking collectives, on_device(): pieces = lax.all_to_all(weights, 'seg', 0, 0, tiled=True)  29.9 us
    all_to_all x1, blocking collectives, on_device(): terms = lax.all_to_all(grid, 'seg', 0, 0, tiled=True)  19.2 us
    all_to_all x1, blocking collectives, on_device(): lax.all_to_all(keep + other, 'frame', 0, 0, tiled=True, axis_index_groups...  14.6 us
    all_to_all x1, blocking collectives, on_device(): chosen = lax.all_to_all(sent, 'frame', 0, 0, tiled=True)  10.7 us
    all_to_all x1, blocking collectives, on_device(): gram = lax.all_to_all(spread, 'coil', 0, 0, tiled=True)  8.41 us
    all_gather x1, blocking collectives, on_device(): lax.all_gather(jnp.sum(total * total, axis=0, keepdims=True), 'coil', til...  8.13 us
    pallas_call x1, Pallas kernels, on_device(): pl.pallas_call(functools.partial(solve_kernel, part), out_shape=jax.Shape...  3.92 us
    pallas_call x1, Pallas kernels, on_device(): pl.pallas_call(functools.partial(other_gram_kernel, part, frames), in_spe...  2.84 us
  transfers between devices with their start and end apart: 1, of which 1 were waited for; matrix products, arithmetic and copies ran while one was open for 0% of the time, Pallas kernels for 1%

profile of v15, /device:TPU:32, one launch (start us, length us, event | category | flops | bytes accessed | tf_op | source)
XLA Modules:
  0.0 103.1 jit_solution(4493699308647435365)
XLA Ops:
  0.0 0.0 copy-start
  0.0 0.0 copy-start.1
  0.0 2.8 %shard_map.64 = (f32[4,104,128]{2,1,0:T(8,128)S(1)}, bf16[4,576,384]{2,1,0:T(8,128)(2,1)S(1)}, bf16[4,8,2,576]{3,2,1,0:T(2,128)(2,1)S(1)}, bf16[1,4,128,384]{3,2...) custom-call(s32[1,4]{1,0:T(1,128)} %reads_ref.5, bf16[8,576,384]{2,1,0:T(8,128)(2,1)} %source_ref.1, ...), custom_call_target="tpu_custom_call" | custom-call | flops 198180864 | bytes 1843200 | tf_op jit(solution)/shard_map/pallas_call | solution.py:324
  2.9 1.9 %collective-permute-start = (f32[4,104,128]{2,1,0:T(8,128)S(1)}, f32[4,104,128]{2,1,0:T(8,128)S(1)}, u32[]{:S(2)}, u32[]{:S(2)}) collective-permute-start(f32[4,104,128]{2,1,0:T(8,128)S(1)} %get-tuple-element.15), channel_id=1, source_target_pairs={{0,64},{64,0},{128,192},{192,128},{256,320},{320,256},{384,448},{4... | collective-permute-start | bytes 638984 | tf_op jit(solution)/shard_map/ppermute | solution.py:359
  4.8 1.0 shard_map.65
  5.8 0.4 collective-permute-done
  6.2 14.6 %all_to_all.25.partial_ref = f32[4,104,128]{2,1,0:T(8,128)S(1)} all-to-all(f32[4,104,128]{2,1,0:T(8,128)S(1)} %add.18), channel_id=1, replica_groups={{0,128,256,384},{64,192,320,448},{1,129,257,385},{65,193,321,449},{2,13..., dimensions={0} | all-to-all | bytes 425984 | tf_op jit(solution)/shard_map/all_to_all | solution.py:361
  20.8 8.4 %all_to_all.26.gram_ref = f32[4,72,128]{2,1,0:T(8,128)S(1)} all-to-all(f32[4,72,128]{2,1,0:T(8,128)S(1)} %get-tuple-element.17), channel_id=1, replica_groups=mesh['frame'=8,'seg'=16,'coil'=4] {'coil'}, dimensions={0} | all-to-all | bytes 294912 | tf_op jit(solution)/shard_map/all_to_all | solution.py:373
  29.2 3.9 %shard_map.67 = bf16[16,8,384]{2,1,0:T(8,128)(2,1)S(1)} custom-call(f32[4,72,128]{2,1,0:T(8,128)S(1)} %all_to_all.26.gram_ref, f32[24,128]{1,0:T(8,128)S(1)} %get-tuple-element.18.rhs_ref), custom_call_target="tpu_custom_call" | custom-call | tf_op jit(solution)/shard_map/pallas_call | solution.py:374
  33.2 29.9 %all_to_all.27.piece_ref = bf16[16,8,384]{2,1,0:T(8,128)(2,1)S(1)} all-to-all(bf16[16,8,384]{2,1,0:T(8,128)(2,1)S(1)} %shard_map.67), channel_id=1, replica_groups=mesh['frame'=8,'seg'=16,'coil'=4] {'seg'}, dimensions={0} | all-to-all | bytes 196608 | tf_op jit(solution)/shard_map/all_to_all | solution.py:384
  63.0 0.4 shard_map.68
  63.4 10.7 %all_to_all.28.weights_ref = bf16[8,4,8,384]{3,2,1,0:T(8,128)(2,1)S(1)} all-to-all(bf16[8,4,8,384]{3,2,1,0:T(8,128)(2,1)S(1)} %shard_map.68), channel_id=1, replica_groups=mesh['frame'=8,'seg'=16,'coil'=4] {'frame'}, dimensions={0} | all-to-all | bytes 393216 | tf_op jit(solution)/shard_map/all_to_all | solution.py:390
  74.1 0.0 copy-done
  74.1 0.0 copy-done.1
  74.1 1.0 shard_map.69
  75.1 19.2 %all_to_all.29 = bf16[16,16,256]{2,1,0:T(8,128)(2,1)S(1)} all-to-all(bf16[16,16,256]{2,1,0:T(8,128)(2,1)S(1)} %shard_map.69), channel_id=1, replica_groups=mesh['frame'=8,'seg'=16,'coil'=4] {'seg'}, dimensions={0} | all-to-all | bytes 262144 | tf_op jit(solution)/shard_map/all_to_all | solution.py:396
  94.4 8.1 %all-gather.1 = f32[4,1,256]{2,1,0:T(1,128)S(1)} all-gather(f32[1,1,256]{2,1,0:T(1,128)S(1)} %bitcast.2), channel_id=2, replica_groups=mesh['frame'=8,'seg'=16,'coil'=4] {'coil'}, dimensions={0}, use_global_device_ids=true | all-gather | bytes 5120 | tf_op jit(solution)/shard_map/all_gather | solution.py:398
  102.6 0.6 add_sqrt_fusion
  (5 shorter events, 0.1 us)
Async XLA Ops:
  0.0 74.1 %copy-start = (s32[1,4]{1,0:T(1,128)S(1)}, s32[1,4]{1,0:T(1,128)}, u32[]{:S(2)}) copy-start(s32[1,4]{1,0:T(1,128)} %reads_ref.5) | copy-start | bytes 52
  0.0 74.1 %copy-start.1 = (s32[1,4]{1,0:T(1,128)S(1)}, s32[1,4]{1,0:T(1,128)}, u32[]{:S(2)}) copy-start(s32[1,4]{1,0:T(1,128)} %places_ref.1) | copy-start | bytes 52
  2.9 3.4 %collective-permute-start = (f32[4,104,128]{2,1,0:T(8,128)S(1)}, f32[4,104,128]{2,1,0:T(8,128)S(1)}, u32[]{:S(2)}, u32[]{:S(2)}) collective-permute-start(f32[4,104,128]{2,1,0:T(8,128)S(1)} %get-tuple-element.15), channel_id=1, source_target_pairs={{0,64},{64,0},{128,192},{192,128},{256,320},{320,256},{384,448},{4... | collective-permute-start | bytes 638984 | tf_op jit(solution)/shard_map/ppermute | solution.py:359

commit v16 on v15

--- a/solution.py
+++ b/solution.py
@@ -171,10 +171,14 @@
             copy.wait()
 
 
-def own_gram_kernel(part, frames, reads_ref, held_ref, goal_ref, out_ref, turned_ref, read_ref, read_sem):
+def own_gram_kernel(
+    part, frames, reads_ref, held_ref, goal_ref, app_ref, out_ref, flipped_ref, turned_ref, read_ref, read_sem
+):
     listing = pltpu.make_async_copy(reads_ref, read_ref, read_sem)
     listing.start()
     slots = tuple(range(out_ref.shape[0]))
+    for slot in range(app_ref.shape[1]):
+        flipped_ref[0, slot] = app_ref[0, slot].T
     gram_sums(part, (slots,), (2,), held_ref, goal_ref, turned_ref, out_ref, [() for _ in slots])
     listing.wait()
     tell(frames, read_ref, out_ref)
@@ -285,7 +289,7 @@
         matrix = jnp.concatenate(
             [jnp.concatenate([real, -imag], axis=1), jnp.concatenate([imag, real], axis=1)], axis=0
         ).astype(BF16)
-        filled = across_rows(matrix, source_ref[0, slot]).astype(BF16)
+        filled = jnp.dot(matrix, source_ref[0, slot], preferred_element_type=F32).astype(BF16)
         terms.append(across_rows(filled, interp_ref[0, slot]))
     shape = terms[0].shape
     places = [jnp.broadcast_to(places_ref[:, slot : slot + 1], shape) for slot in range(slots)]
@@ -348,14 +352,17 @@
         pltpu.with_memory_space_constraint(app_source, pltpu.HBM),
         pltpu.with_memory_space_constraint(interp, pltpu.HBM),
     )
-    keep = pl.pallas_call(
+    keep, flipped = pl.pallas_call(
         functools.partial(own_gram_kernel, part, frames),
-        in_specs=[hbm, vmem, vmem],
-        out_shape=block,
+        in_specs=[hbm, vmem, vmem, vmem],
+        out_shape=[
+            block,
+            jax.ShapeDtypeStruct((1, slots, depth, app_source.shape[2]), BF16),
+        ],
         scratch_shapes=[turned, *reading, pltpu.SemaphoreType.DMA],
         compiler_params=SMALL,
         cost_estimate=cost,
-    )(listed, own_held, own_goal)
+    )(listed, own_held, own_goal, own_app)
     other = lax.ppermute(send, "frame", [(frame, frame ^ 1) for frame in range(frames)])
     chips = [[2 * chip + core for chip in range(frames // 2)] for core in range(2)]
     received = lax.all_to_all(
@@ -392,7 +399,7 @@
         fill_kernel,
         out_shape=jax.ShapeDtypeStruct((segs, 2 * coils, cells), BF16),
         compiler_params=SMALL,
-    )(readers, blocks, chosen, own_app, own_interp)
+    )(readers, blocks, chosen, flipped, own_interp)
     terms = lax.all_to_all(grid, "seg", 0, 0, tiled=True)
     total = jnp.sum(terms.astype(F32), axis=0)
     power = lax.all_gather(jnp.sum(total * total, axis=0, keepdims=True), "coil", tiled=True)

time: 103 us -> 104 us (level)
  transfers between devices with their start and end apart: 1 -> 1, of which waited for: 1 -> 0; matrix products, arithmetic and copies ran while one was open for 0% -> 0% of each run, Pallas kernels for 1% -> 1%
where the time goes in v16:
time: 104 us
  blocking collectives  91.9 us (88%)
  Pallas kernels  9.05 us (9%)
  starting transfers between devices  1.92 us (2%)
    all_to_all x1, blocking collectives, on_device(): pieces = lax.all_to_all(weights, 'seg', 0, 0, tiled=True)  29.8 us
    all_to_all x1, blocking collectives, on_device(): terms = lax.all_to_all(grid, 'seg', 0, 0, tiled=True)  19.7 us
    all_to_all x1, blocking collectives, on_device(): lax.all_to_all(keep + other, 'frame', 0, 0, tiled=True, axis_index_groups...  14.9 us
    all_to_all x1, blocking collectives, on_device(): chosen = lax.all_to_all(sent, 'frame', 0, 0, tiled=True)  10.8 us
    all_to_all x1, blocking collectives, on_device(): gram = lax.all_to_all(spread, 'coil', 0, 0, tiled=True)  8.41 us
    all_gather x1, blocking collectives, on_device(): lax.all_gather(jnp.sum(total * total, axis=0, keepdims=True), 'coil', til...  8.14 us
    pallas_call x1, Pallas kernels, on_device(): pl.pallas_call(functools.partial(solve_kernel, part), out_shape=jax.Shape...  3.93 us
    pallas_call x1, Pallas kernels, on_device(): pl.pallas_call(functools.partial(other_gram_kernel, part, frames), in_spe...  2.8 us
  transfers between devices with their start and end apart: 1, of which 0 were waited for; matrix products, arithmetic and copies ran while one was open for 0% of the time, Pallas kernels for 1%

profile of v16, /device:TPU:32, one launch (start us, length us, event | category | flops | bytes accessed | tf_op | source)
XLA Modules:
  0.0 103.6 jit_solution(13028006623092120717)
XLA Ops:
  0.0 2.8 %shard_map.64 = (f32[4,104,128]{2,1,0:T(8,128)S(1)}, bf16[4,576,384]{2,1,0:T(8,128)(2,1)S(1)}, bf16[4,8,2,576]{3,2,1,0:T(2,128)(2,1)S(1)}, bf16[1,4,128,384]{3,2...) custom-call(s32[1,4]{1,0:T(1,128)} %reads_ref.5, bf16[8,576,384]{2,1,0:T(8,128)(2,1)} %source_ref.1, ...), custom_call_target="tpu_custom_call" | custom-call | flops 198180864 | bytes 1843200 | tf_op jit(solution)/shard_map/pallas_call | solution.py:328
  2.8 0.0 copy-start
  2.8 0.0 copy-start.1
  2.8 1.9 %collective-permute-start = (f32[4,104,128]{2,1,0:T(8,128)S(1)}, f32[4,104,128]{2,1,0:T(8,128)S(1)}, u32[]{:S(2)}, u32[]{:S(2)}) collective-permute-start(f32[4,104,128]{2,1,0:T(8,128)S(1)} %get-tuple-element.19), channel_id=1, source_target_pairs={{0,64},{64,0},{128,192},{192,128},{256,320},{320,256},{384,448},{4... | collective-permute-start | bytes 638984 | tf_op jit(solution)/shard_map/ppermute | solution.py:366
  4.8 1.4 %shard_map.65 = (f32[4,104,128]{2,1,0:T(8,128)S(1)}, bf16[1,4,384,128]{3,2,1,0:T(8,128)(2,1)S(1)}) custom-call(s32[1,4]{1,0:T(1,128)} %reads_ref.5, bf16[4,576,384]{2,1,0:T(8,128)(2,1)S(1)} %get-tuple-element.15.held_ref, bf16[4,8,2,576]{3,2,1,0:T(2,128)(2,1)S(1)} %get-tuple-element.16.goal_ref, bf16[1,4,128,384]{3,2,1,0:T(8,128)(2,1)S(1)} %get-tuple-element.17.app_ref), custom_call_target="tpu_custom_call" | custom-call | flops 198180864 | bytes 1843200 | tf_op jit(solution)/shard_map/pallas_call | solution.py:355
  6.2 0.0 collective-permute-done
  6.2 14.9 %all_to_all.25.partial_ref = f32[4,104,128]{2,1,0:T(8,128)S(1)} all-to-all(f32[4,104,128]{2,1,0:T(8,128)S(1)} %add.18), channel_id=1, replica_groups={{0,128,256,384},{64,192,320,448},{1,129,257,385},{65,193,321,449},{2,13..., dimensions={0} | all-to-all | bytes 425984 | tf_op jit(solution)/shard_map/all_to_all | solution.py:368
  21.2 8.4 %all_to_all.26.gram_ref = f32[4,72,128]{2,1,0:T(8,128)S(1)} all-to-all(f32[4,72,128]{2,1,0:T(8,128)S(1)} %get-tuple-element.21), channel_id=1, replica_groups=mesh['frame'=8,'seg'=16,'coil'=4] {'coil'}, dimensions={0} | all-to-all | bytes 294912 | tf_op jit(solution)/shard_map/all_to_all | solution.py:380
  29.6 3.9 %shard_map.67 = bf16[16,8,384]{2,1,0:T(8,128)(2,1)S(1)} custom-call(f32[4,72,128]{2,1,0:T(8,128)S(1)} %all_to_all.26.gram_ref, f32[24,128]{1,0:T(8,128)S(1)} %get-tuple-element.22.rhs_ref), custom_call_target="tpu_custom_call" | custom-call | tf_op jit(solution)/shard_map/pallas_call | solution.py:381
  33.5 29.8 %all_to_all.27.piece_ref = bf16[16,8,384]{2,1,0:T(8,128)(2,1)S(1)} all-to-all(bf16[16,8,384]{2,1,0:T(8,128)(2,1)S(1)} %shard_map.67), channel_id=1, replica_groups=mesh['frame'=8,'seg'=16,'coil'=4] {'seg'}, dimensions={0} | all-to-all | bytes 196608 | tf_op jit(solution)/shard_map/all_to_all | solution.py:391
  63.4 0.4 shard_map.68
  63.7 10.8 %all_to_all.28.weights_ref = bf16[8,4,8,384]{3,2,1,0:T(8,128)(2,1)S(1)} all-to-all(bf16[8,4,8,384]{3,2,1,0:T(8,128)(2,1)S(1)} %shard_map.68), channel_id=1, replica_groups=mesh['frame'=8,'seg'=16,'coil'=4] {'frame'}, dimensions={0} | all-to-all | bytes 393216 | tf_op jit(solution)/shard_map/all_to_all | solution.py:397
  74.6 0.0 copy-done
  74.6 0.0 copy-done.1
  74.6 0.5 shard_map.69
  75.1 19.7 %all_to_all.29 = bf16[16,16,256]{2,1,0:T(8,128)(2,1)S(1)} all-to-all(bf16[16,16,256]{2,1,0:T(8,128)(2,1)S(1)} %shard_map.69), channel_id=1, replica_groups=mesh['frame'=8,'seg'=16,'coil'=4] {'seg'}, dimensions={0} | all-to-all | bytes 262144 | tf_op jit(solution)/shard_map/all_to_all | solution.py:403
  94.9 8.1 %all-gather.1 = f32[4,1,256]{2,1,0:T(1,128)S(1)} all-gather(f32[1,1,256]{2,1,0:T(1,128)S(1)} %bitcast.2), channel_id=2, replica_groups=mesh['frame'=8,'seg'=16,'coil'=4] {'coil'}, dimensions={0}, use_global_device_ids=true | all-gather | bytes 5120 | tf_op jit(solution)/shard_map/all_gather | solution.py:405
  103.0 0.6 add_sqrt_fusion
  (5 shorter events, 0.1 us)
Async XLA Ops:
  2.8 71.8 %copy-start = (s32[1,4]{1,0:T(1,128)S(1)}, s32[1,4]{1,0:T(1,128)}, u32[]{:S(2)}) copy-start(s32[1,4]{1,0:T(1,128)} %reads_ref.5) | copy-start | bytes 52
  2.8 71.8 %copy-start.1 = (s32[1,4]{1,0:T(1,128)S(1)}, s32[1,4]{1,0:T(1,128)}, u32[]{:S(2)}) copy-start(s32[1,4]{1,0:T(1,128)} %places_ref.1) | copy-start | bytes 52
  2.8 3.4 %collective-permute-start = (f32[4,104,128]{2,1,0:T(8,128)S(1)}, f32[4,104,128]{2,1,0:T(8,128)S(1)}, u32[]{:S(2)}, u32[]{:S(2)}) collective-permute-start(f32[4,104,128]{2,1,0:T(8,128)S(1)} %get-tuple-element.19), channel_id=1, source_target_pairs={{0,64},{64,0},{128,192},{192,128},{256,320},{320,256},{384,448},{4... | collective-permute-start | bytes 638984 | tf_op jit(solution)/shard_map/ppermute | solution.py:366

commit v17 on v15

--- a/solution.py
+++ b/solution.py
@@ -49,7 +49,7 @@
     )
 
 
-def gram_sums(part, groups, picked, held_ref, goal_ref, turned_ref, out_ref, copies):
+def gram_sums(part, groups, picked, held_ref, goal_ref, turned_ref, out_ref, copies, beside=None):
     coil = lax.axis_index("coil")
     depth = held_ref.shape[2]
     width = depth // 2
@@ -68,6 +68,8 @@
         for slot in slots:
             for copy in copies[slot]:
                 copy.wait()
+        if beside is not None and slots is groups[0]:
+            beside()
         lefts = []
         for slot in slots:
             if slot in picked:
@@ -128,11 +130,12 @@
     out_ref,
     own_held_ref,
     own_goal_ref,
-    own_app_ref,
+    flipped_ref,
     own_interp_ref,
     held_ref,
     goal_ref,
     turned_ref,
+    own_app_ref,
     read_ref,
     sem,
     late_sem,
@@ -151,21 +154,28 @@
                 pltpu.make_async_copy(target_ref.at[segment], goal, sem.at[1, slot]),
             )
         )
-    for pair in copies:
+    app_copy = pltpu.make_async_copy(app_ref, own_app_ref, late_sem.at[1])
+    for slot, pair in enumerate(copies):
         for copy in pair:
             copy.start()
+        if slot == 0:
+            app_copy.start()
     late = [
         pltpu.make_async_copy(reads_ref, read_ref, late_sem.at[0]),
-        pltpu.make_async_copy(app_ref, own_app_ref, late_sem.at[1]),
         pltpu.make_async_copy(interp_ref, own_interp_ref, late_sem.at[2]),
     ]
     for copy in late:
         copy.start()
-    gram_sums(part, ((0,), (1, 2, 3)), (), held_ref, goal_ref, turned_ref, out_ref, copies)
+
+    def turn():
+        app_copy.wait()
+        for slot in range(own_app_ref.shape[1]):
+            flipped_ref[0, slot] = own_app_ref[0, slot].T
+
+    gram_sums(part, ((0,), (1, 2, 3)), (), held_ref, goal_ref, turned_ref, out_ref, copies, turn)
     late[0].wait()
     tell(frames, read_ref, out_ref)
-    for copy in late[1:]:
-        copy.wait()
+    late[1].wait()
     for pair in copies[each:]:
         for copy in pair:
             copy.wait()
@@ -285,7 +295,7 @@
         matrix = jnp.concatenate(
             [jnp.concatenate([real, -imag], axis=1), jnp.concatenate([imag, real], axis=1)], axis=0
         ).astype(BF16)
-        filled = across_rows(matrix, source_ref[0, slot]).astype(BF16)
+        filled = jnp.dot(matrix, source_ref[0, slot], preferred_element_type=F32).astype(BF16)
         terms.append(across_rows(filled, interp_ref[0, slot]))
     shape = terms[0].shape
     places = [jnp.broadcast_to(places_ref[:, slot : slot + 1], shape) for slot in range(slots)]
@@ -321,20 +331,21 @@
         bytes_accessed=2 * each * samples * (depth + 2 * coils),
         transcendentals=0,
     )
-    send, own_held, own_goal, own_app, own_interp = pl.pallas_call(
+    send, own_held, own_goal, flipped, own_interp = pl.pallas_call(
         functools.partial(other_gram_kernel, part, frames),
         in_specs=[hbm] * 5,
         out_shape=[
             block,
             jax.ShapeDtypeStruct((each, samples, depth), BF16),
             jax.ShapeDtypeStruct((each, coils, 2, samples), BF16),
-            jax.ShapeDtypeStruct(app_source.shape, BF16),
+            jax.ShapeDtypeStruct((1, slots, depth, app_source.shape[2]), BF16),
             jax.ShapeDtypeStruct(interp.shape, BF16),
         ],
         scratch_shapes=[
             pltpu.VMEM((each, samples, depth), BF16),
             pltpu.VMEM((each, coils, 2, samples), BF16),
             turned,
+            pltpu.VMEM(app_source.shape, BF16),
             *reading,
             pltpu.SemaphoreType.DMA((2, held)),
             pltpu.SemaphoreType.DMA((3,)),
@@ -392,7 +403,7 @@
         fill_kernel,
         out_shape=jax.ShapeDtypeStruct((segs, 2 * coils, cells), BF16),
         compiler_params=SMALL,
-    )(readers, blocks, chosen, own_app, own_interp)
+    )(readers, blocks, chosen, flipped, own_interp)
     terms = lax.all_to_all(grid, "seg", 0, 0, tiled=True)
     total = jnp.sum(terms.astype(F32), axis=0)
     power = lax.all_gather(jnp.sum(total * total, axis=0, keepdims=True), "coil", tiled=True)

time: 103 us -> 104 us (level)
    pallas_call x1, Pallas kernels: 2.84 us -> 3.89 us  [on_device(): pl.pallas_call(functools.partial(other_gram_kernel, part, frames), in_spe...]
where the time goes in v17:
time: 104 us
  blocking collectives  90.9 us (87%)
  Pallas kernels  9.75 us (9%)
  starting transfers between devices  1.92 us (2%)
    all_to_all x1, blocking collectives, on_device(): pieces = lax.all_to_all(weights, 'seg', 0, 0, tiled=True)  29.8 us
    all_to_all x1, blocking collectives, on_device(): terms = lax.all_to_all(grid, 'seg', 0, 0, tiled=True)  19.2 us
    all_to_all x1, blocking collectives, on_device(): lax.all_to_all(keep + other, 'frame', 0, 0, tiled=True, axis_index_groups...  14.6 us
    all_to_all x1, blocking collectives, on_device(): chosen = lax.all_to_all(sent, 'frame', 0, 0, tiled=True)  10.7 us
    all_to_all x1, blocking collectives, on_device(): gram = lax.all_to_all(spread, 'coil', 0, 0, tiled=True)  8.41 us
    all_gather x1, blocking collectives, on_device(): lax.all_gather(jnp.sum(total * total, axis=0, keepdims=True), 'coil', til...  8.13 us
    pallas_call x1, Pallas kernels, on_device(): pl.pallas_call(functools.partial(solve_kernel, part), out_shape=jax.Shape...  3.93 us
    pallas_call x1, Pallas kernels, on_device(): pl.pallas_call(functools.partial(other_gram_kernel, part, frames), in_spe...  3.89 us
  transfers between devices with their start and end apart: 1, of which 1 were waited for; matrix products, arithmetic and copies ran while one was open for 0% of the time, Pallas kernels for 1%

profile of v17, /device:TPU:32, one launch (start us, length us, event | category | flops | bytes accessed | tf_op | source)
XLA Modules:
  0.0 103.7 jit_solution(1747995985301456688)
XLA Ops:
  0.0 0.0 copy-start
  0.0 0.0 copy-start.1
  0.0 3.9 %shard_map.64 = (f32[4,104,128]{2,1,0:T(8,128)S(1)}, bf16[4,576,384]{2,1,0:T(8,128)(2,1)S(1)}, bf16[4,8,2,576]{3,2,1,0:T(2,128)(2,1)S(1)}, bf16[1,4,384,128]{3,2...) custom-call(s32[1,4]{1,0:T(1,128)} %reads_ref.5, bf16[8,576,384]{2,1,0:T(8,128)(2,1)} %source_ref.1, ...), custom_call_target="tpu_custom_call" | custom-call | flops 198180864 | bytes 1843200 | tf_op jit(solution)/shard_map/pallas_call | solution.py:334
  3.9 1.9 %collective-permute-start = (f32[4,104,128]{2,1,0:T(8,128)S(1)}, f32[4,104,128]{2,1,0:T(8,128)S(1)}, u32[]{:S(2)}, u32[]{:S(2)}) collective-permute-start(f32[4,104,128]{2,1,0:T(8,128)S(1)} %get-tuple-element.15), channel_id=1, source_target_pairs={{0,64},{64,0},{128,192},{192,128},{256,320},{320,256},{384,448},{4... | collective-permute-start | bytes 638984 | tf_op jit(solution)/shard_map/ppermute | solution.py:370
  5.8 1.0 shard_map.65
  6.9 0.4 collective-permute-done
  7.3 14.6 %all_to_all.25.partial_ref = f32[4,104,128]{2,1,0:T(8,128)S(1)} all-to-all(f32[4,104,128]{2,1,0:T(8,128)S(1)} %add.18), channel_id=1, replica_groups={{0,128,256,384},{64,192,320,448},{1,129,257,385},{65,193,321,449},{2,13..., dimensions={0} | all-to-all | bytes 425984 | tf_op jit(solution)/shard_map/all_to_all | solution.py:372
  21.9 8.4 %all_to_all.26.gram_ref = f32[4,72,128]{2,1,0:T(8,128)S(1)} all-to-all(f32[4,72,128]{2,1,0:T(8,128)S(1)} %get-tuple-element.17), channel_id=1, replica_groups=mesh['frame'=8,'seg'=16,'coil'=4] {'coil'}, dimensions={0} | all-to-all | bytes 294912 | tf_op jit(solution)/shard_map/all_to_all | solution.py:384
  30.3 3.9 %shard_map.67 = bf16[16,8,384]{2,1,0:T(8,128)(2,1)S(1)} custom-call(f32[4,72,128]{2,1,0:T(8,128)S(1)} %all_to_all.26.gram_ref, f32[24,128]{1,0:T(8,128)S(1)} %get-tuple-element.18.rhs_ref), custom_call_target="tpu_custom_call" | custom-call | tf_op jit(solution)/shard_map/pallas_call | solution.py:385
  34.2 29.8 %all_to_all.27.piece_ref = bf16[16,8,384]{2,1,0:T(8,128)(2,1)S(1)} all-to-all(bf16[16,8,384]{2,1,0:T(8,128)(2,1)S(1)} %shard_map.67), channel_id=1, replica_groups=mesh['frame'=8,'seg'=16,'coil'=4] {'seg'}, dimensions={0} | all-to-all | bytes 196608 | tf_op jit(solution)/shard_map/all_to_all | solution.py:395
  64.1 0.4 shard_map.68
  64.4 10.7 %all_to_all.28.weights_ref = bf16[8,4,8,384]{3,2,1,0:T(8,128)(2,1)S(1)} all-to-all(bf16[8,4,8,384]{3,2,1,0:T(8,128)(2,1)S(1)} %shard_map.68), channel_id=1, replica_groups=mesh['frame'=8,'seg'=16,'coil'=4] {'frame'}, dimensions={0} | all-to-all | bytes 393216 | tf_op jit(solution)/shard_map/all_to_all | solution.py:401
  75.2 0.0 copy-done
  75.2 0.0 copy-done.1
  75.2 0.5 shard_map.69
  75.7 19.2 %all_to_all.29 = bf16[16,16,256]{2,1,0:T(8,128)(2,1)S(1)} all-to-all(bf16[16,16,256]{2,1,0:T(8,128)(2,1)S(1)} %shard_map.69), channel_id=1, replica_groups=mesh['frame'=8,'seg'=16,'coil'=4] {'seg'}, dimensions={0} | all-to-all | bytes 262144 | tf_op jit(solution)/shard_map/all_to_all | solution.py:407
  95.0 8.1 %all-gather.1 = f32[4,1,256]{2,1,0:T(1,128)S(1)} all-gather(f32[1,1,256]{2,1,0:T(1,128)S(1)} %bitcast.2), channel_id=2, replica_groups=mesh['frame'=8,'seg'=16,'coil'=4] {'coil'}, dimensions={0}, use_global_device_ids=true | all-gather | bytes 5120 | tf_op jit(solution)/shard_map/all_gather | solution.py:409
  103.1 0.6 add_sqrt_fusion
  (5 shorter events, 0.1 us)
Async XLA Ops:
  0.0 75.2 %copy-start = (s32[1,4]{1,0:T(1,128)S(1)}, s32[1,4]{1,0:T(1,128)}, u32[]{:S(2)}) copy-start(s32[1,4]{1,0:T(1,128)} %reads_ref.5) | copy-start | bytes 52
  0.0 75.2 %copy-start.1 = (s32[1,4]{1,0:T(1,128)S(1)}, s32[1,4]{1,0:T(1,128)}, u32[]{:S(2)}) copy-start(s32[1,4]{1,0:T(1,128)} %places_ref.1) | copy-start | bytes 52
  3.9 3.4 %collective-permute-start = (f32[4,104,128]{2,1,0:T(8,128)S(1)}, f32[4,104,128]{2,1,0:T(8,128)S(1)}, u32[]{:S(2)}, u32[]{:S(2)}) collective-permute-start(f32[4,104,128]{2,1,0:T(8,128)S(1)} %get-tuple-element.15), channel_id=1, source_target_pairs={{0,64},{64,0},{128,192},{192,128},{256,320},{320,256},{384,448},{4... | collective-permute-start | bytes 638984 | tf_op jit(solution)/shard_map/ppermute | solution.py:370

commit v18 on v15

--- a/solution.py
+++ b/solution.py
@@ -192,7 +192,7 @@
         told_ref[2 * chip : 2 * chip + 2] = partial_ref[chip, rows : rows + 2].astype(jnp.int32)
 
 
-def solve_kernel(part, gram_ref, rhs_ref, out_ref, real_ref, imag_ref, sol_ref):
+def solve_kernel(part, gram_ref, rhs_ref, app_ref, out_ref, flipped_ref, real_ref, imag_ref, sol_ref):
     width = 4 * part
     half = part // 2
     coils = rhs_ref.shape[0] // 3
@@ -210,6 +210,8 @@
     down = lax.broadcasted_iota(jnp.int32, (width, width), 0)
     across = lax.broadcasted_iota(jnp.int32, (width, width), 1)
     diagonal = jnp.where(across == down, packed, 0.0)
+    for slot in range(app_ref.shape[1]):
+        flipped_ref[0, slot] = app_ref[0, slot].T
     shift = regular / width * jnp.sum(diagonal, keepdims=True)
     norm = jnp.sum(2.0 * (packed * packed) - diagonal * diagonal, keepdims=True)
     high = jnp.sqrt(norm) + shift
@@ -241,7 +243,7 @@
 
     spread = jnp.sum((high - shift) / (high + shift))
     spread = lax.while_loop(
-        lambda spread: spread > 0.99, functools.partial(step, fine_product), spread
+        lambda spread: spread > 0.998, functools.partial(step, fine_product), spread
     )
     spread = lax.while_loop(
         lambda spread: spread > settled, functools.partial(step, product), spread
@@ -285,7 +287,7 @@
         matrix = jnp.concatenate(
             [jnp.concatenate([real, -imag], axis=1), jnp.concatenate([imag, real], axis=1)], axis=0
         ).astype(BF16)
-        filled = across_rows(matrix, source_ref[0, slot]).astype(BF16)
+        filled = jnp.dot(matrix, source_ref[0, slot], preferred_element_type=F32).astype(BF16)
         terms.append(across_rows(filled, interp_ref[0, slot]))
     shape = terms[0].shape
     places = [jnp.broadcast_to(places_ref[:, slot : slot + 1], shape) for slot in range(slots)]
@@ -371,16 +373,19 @@
         compiler_params=SMALL,
     )(received)
     gram = lax.all_to_all(spread, "coil", 0, 0, tiled=True)
-    weights = pl.pallas_call(
+    weights, flipped = pl.pallas_call(
         functools.partial(solve_kernel, part),
-        out_shape=jax.ShapeDtypeStruct((segs, coils, depth), BF16),
+        out_shape=[
+            jax.ShapeDtypeStruct((segs, coils, depth), BF16),
+            jax.ShapeDtypeStruct((1, slots, depth, app_source.shape[2]), BF16),
+        ],
         scratch_shapes=[
             pltpu.VMEM((width, width), F32),
             pltpu.VMEM((width, width), F32),
             pltpu.VMEM((2 * coils, width), F32),
         ],
         compiler_params=SMALL,
-    )(gram, rhs)
+    )(gram, rhs, own_app)
     pieces = lax.all_to_all(weights, "seg", 0, 0, tiled=True)
     sent = pl.pallas_call(
         select_kernel,
@@ -392,7 +397,7 @@
         fill_kernel,
         out_shape=jax.ShapeDtypeStruct((segs, 2 * coils, cells), BF16),
         compiler_params=SMALL,
-    )(readers, blocks, chosen, own_app, own_interp)
+    )(readers, blocks, chosen, flipped, own_interp)
     terms = lax.all_to_all(grid, "seg", 0, 0, tiled=True)
     total = jnp.sum(terms.astype(F32), axis=0)
     power = lax.all_gather(jnp.sum(total * total, axis=0, keepdims=True), "coil", tiled=True)

time: 103 us -> 103 us (level)
  the two profiles are of different devices: /device:TPU:32 before, /device:TPU:8 now
where the time goes in v18:
time: 103 us
  blocking collectives  90.9 us (88%)
  Pallas kernels  8.6 us (8%)
  starting transfers between devices  1.92 us (2%)
    all_to_all x1, blocking collectives, on_device(): pieces = lax.all_to_all(weights, 'seg', 0, 0, tiled=True)  29.5 us
    all_to_all x1, blocking collectives, on_device(): terms = lax.all_to_all(grid, 'seg', 0, 0, tiled=True)  18.4 us
    all_to_all x1, blocking collectives, on_device(): lax.all_to_all(keep + other, 'frame', 0, 0, tiled=True, axis_index_groups...  13.8 us
    all_to_all x1, blocking collectives, on_device(): chosen = lax.all_to_all(sent, 'frame', 0, 0, tiled=True)  11 us
    all_to_all x1, blocking collectives, on_device(): gram = lax.all_to_all(spread, 'coil', 0, 0, tiled=True)  9.73 us
    all_gather x1, blocking collectives, on_device(): lax.all_gather(jnp.sum(total * total, axis=0, keepdims=True), 'coil', til...  8.44 us
    pallas_call x1, Pallas kernels, on_device(): pl.pallas_call(functools.partial(solve_kernel, part), out_shape=[jax.Shap...  3.84 us
    pallas_call x1, Pallas kernels, on_device(): pl.pallas_call(functools.partial(other_gram_kernel, part, frames), in_spe...  2.82 us
  transfers between devices with their start and end apart: 1, of which 1 were waited for; matrix products, arithmetic and copies ran while one was open for 0% of the time, Pallas kernels for 1%

profile of v18, /device:TPU:8, one launch (start us, length us, event | category | flops | bytes accessed | tf_op | source)
XLA Modules:
  0.0 102.6 jit_solution(3188142830310747447)
XLA Ops:
  0.0 2.8 %shard_map.64 = (f32[4,104,128]{2,1,0:T(8,128)S(1)}, bf16[4,576,384]{2,1,0:T(8,128)(2,1)S(1)}, bf16[4,8,2,576]{3,2,1,0:T(2,128)(2,1)S(1)}, bf16[1,4,128,384]{3,2...) custom-call(s32[1,4]{1,0:T(1,128)} %reads_ref.5, bf16[8,576,384]{2,1,0:T(8,128)(2,1)} %source_ref.1, ...), custom_call_target="tpu_custom_call" | custom-call | flops 198180864 | bytes 1843200 | tf_op jit(solution)/shard_map/pallas_call | solution.py:326
  2.8 0.0 copy-start
  2.8 0.0 copy-start.1
  2.8 1.9 %collective-permute-start = (f32[4,104,128]{2,1,0:T(8,128)S(1)}, f32[4,104,128]{2,1,0:T(8,128)S(1)}, u32[]{:S(2)}, u32[]{:S(2)}) collective-permute-start(f32[4,104,128]{2,1,0:T(8,128)S(1)} %get-tuple-element.17), channel_id=1, source_target_pairs={{0,64},{64,0},{128,192},{192,128},{256,320},{320,256},{384,448},{4... | collective-permute-start | bytes 638984 | tf_op jit(solution)/shard_map/ppermute | solution.py:361
  4.8 1.0 %shard_map.65 = f32[4,104,128]{2,1,0:T(8,128)S(1)} custom-call(s32[1,4]{1,0:T(1,128)} %reads_ref.5, bf16[4,576,384]{2,1,0:T(8,128)(2,1)S(1)} %get-tuple-element.15.held_ref, bf16[4,8,2,576]{3,2,1,0:T(2,128)(2,1)S(1)} %get-tuple-element.16.goal_ref), custom_call_target="tpu_custom_call" | custom-call | flops 198180864 | bytes 1843200 | tf_op jit(solution)/shard_map/pallas_call | solution.py:353
  5.8 0.4 collective-permute-done
  6.2 13.8 %all_to_all.25.partial_ref = f32[4,104,128]{2,1,0:T(8,128)S(1)} all-to-all(f32[4,104,128]{2,1,0:T(8,128)S(1)} %add.18), channel_id=1, replica_groups={{0,128,256,384},{64,192,320,448},{1,129,257,385},{65,193,321,449},{2,13..., dimensions={0} | all-to-all | bytes 425984 | tf_op jit(solution)/shard_map/all_to_all | solution.py:363
  20.1 9.7 %all_to_all.26.gram_ref = f32[4,72,128]{2,1,0:T(8,128)S(1)} all-to-all(f32[4,72,128]{2,1,0:T(8,128)S(1)} %get-tuple-element.19), channel_id=1, replica_groups=mesh['frame'=8,'seg'=16,'coil'=4] {'coil'}, dimensions={0} | all-to-all | bytes 294912 | tf_op jit(solution)/shard_map/all_to_all | solution.py:375
  29.8 3.8 %shard_map.67 = (bf16[16,8,384]{2,1,0:T(8,128)(2,1)S(1)}, bf16[1,4,384,128]{3,2,1,0:T(8,128)(2,1)S(1)}) custom-call(f32[4,72,128]{2,1,0:T(8,128)S(1)} %all_to_all.26.gram_ref, f32[24,128]{1,0:T(8,128)S(1)} %get-tuple-element.20.rhs_ref, bf16[1,4,128,384]{3,2,1,0:T(8,128)(2,1)S(1)} %get-tuple-element.21.app_ref), custom_call_target="tpu_custom_call" | custom-call | tf_op jit(solution)/shard_map/pallas_call | solution.py:376
  33.6 29.5 %all_to_all.27.piece_ref = bf16[16,8,384]{2,1,0:T(8,128)(2,1)S(1)} all-to-all(bf16[16,8,384]{2,1,0:T(8,128)(2,1)S(1)} %get-tuple-element.22), channel_id=1, replica_groups=mesh['frame'=8,'seg'=16,'coil'=4] {'seg'}, dimensions={0} | all-to-all | bytes 196608 | tf_op jit(solution)/shard_map/all_to_all | solution.py:389
  63.1 0.4 shard_map.68
  63.5 11.0 %all_to_all.28.weights_ref = bf16[8,4,8,384]{3,2,1,0:T(8,128)(2,1)S(1)} all-to-all(bf16[8,4,8,384]{3,2,1,0:T(8,128)(2,1)S(1)} %shard_map.68), channel_id=1, replica_groups=mesh['frame'=8,'seg'=16,'coil'=4] {'frame'}, dimensions={0} | all-to-all | bytes 393216 | tf_op jit(solution)/shard_map/all_to_all | solution.py:395
  74.5 0.0 copy-done
  74.5 0.0 copy-done.1
  74.5 0.5 shard_map.69
  75.1 18.4 %all_to_all.29 = bf16[16,16,256]{2,1,0:T(8,128)(2,1)S(1)} all-to-all(bf16[16,16,256]{2,1,0:T(8,128)(2,1)S(1)} %shard_map.69), channel_id=1, replica_groups=mesh['frame'=8,'seg'=16,'coil'=4] {'seg'}, dimensions={0} | all-to-all | bytes 262144 | tf_op jit(solution)/shard_map/all_to_all | solution.py:401
  93.5 8.4 %all-gather.1 = f32[4,1,256]{2,1,0:T(1,128)S(1)} all-gather(f32[1,1,256]{2,1,0:T(1,128)S(1)} %bitcast.2), channel_id=2, replica_groups=mesh['frame'=8,'seg'=16,'coil'=4] {'coil'}, dimensions={0}, use_global_device_ids=true | all-gather | bytes 5120 | tf_op jit(solution)/shard_map/all_gather | solution.py:403
  102.0 0.6 add_sqrt_fusion
  (5 shorter events, 0.1 us)
Async XLA Ops:
  2.8 71.7 %copy-start = (s32[1,4]{1,0:T(1,128)S(1)}, s32[1,4]{1,0:T(1,128)}, u32[]{:S(2)}) copy-start(s32[1,4]{1,0:T(1,128)} %reads_ref.5) | copy-start | bytes 52
  2.8 71.7 %copy-start.1 = (s32[1,4]{1,0:T(1,128)S(1)}, s32[1,4]{1,0:T(1,128)}, u32[]{:S(2)}) copy-start(s32[1,4]{1,0:T(1,128)} %places_ref.1) | copy-start | bytes 52
  2.8 3.4 %collective-permute-start = (f32[4,104,128]{2,1,0:T(8,128)S(1)}, f32[4,104,128]{2,1,0:T(8,128)S(1)}, u32[]{:S(2)}, u32[]{:S(2)}) collective-permute-start(f32[4,104,128]{2,1,0:T(8,128)S(1)} %get-tuple-element.17), channel_id=1, source_target_pairs={{0,64},{64,0},{128,192},{192,128},{256,320},{320,256},{384,448},{4... | collective-permute-start | bytes 638984 | tf_op jit(solution)/shard_map/ppermute | solution.py:361

commit v19 on v18

--- a/solution.py
+++ b/solution.py
@@ -13,6 +13,7 @@
 F32 = jnp.float32
 BF16 = jnp.bfloat16
 LANES = 128
+CHIPS = (0, 3, 1, 2)
 SMALL = pltpu.CompilerParams(vmem_limit_bytes=16 * 1024 * 1024)
 
 
@@ -142,7 +143,7 @@
     copies = []
     for slot in range(2 * each):
         own, place = slot // each, slot % each
-        segment = 2 * place + (core if own else 1 - core)
+        segment = 2 * CHIPS[place] + (core if own else 1 - core)
         held = (own_held_ref if own else held_ref).at[place]
         goal = (own_goal_ref if own else goal_ref).at[place]
         copies.append(
@@ -188,8 +189,8 @@
     for copy in range(spread_ref.shape[0]):
         spread_ref[copy] = total[:gram_rows]
     rhs_ref[...] = total[gram_rows:]
-    for chip in range(partial_ref.shape[0]):
-        told_ref[2 * chip : 2 * chip + 2] = partial_ref[chip, rows : rows + 2].astype(jnp.int32)
+    for place, chip in enumerate(CHIPS):
+        told_ref[2 * chip : 2 * chip + 2] = partial_ref[place, rows : rows + 2].astype(jnp.int32)
 
 
 def solve_kernel(part, gram_ref, rhs_ref, app_ref, out_ref, flipped_ref, real_ref, imag_ref, sol_ref):
@@ -359,7 +360,7 @@
         cost_estimate=cost,
     )(listed, own_held, own_goal)
     other = lax.ppermute(send, "frame", [(frame, frame ^ 1) for frame in range(frames)])
-    chips = [[2 * chip + core for chip in range(frames // 2)] for core in range(2)]
+    chips = [[2 * chip + core for chip in CHIPS] for core in range(2)]
     received = lax.all_to_all(
         keep + other, "frame", 0, 0, tiled=True, axis_index_groups=chips
     )

time: 103 us -> 103 us (level)
  no operation moved by 1% of the time
where the time goes in v19:
time: 103 us
  blocking collectives  91 us (88%)
  Pallas kernels  8.59 us (8%)
  starting transfers between devices  1.92 us (2%)
    all_to_all x1, blocking collectives, on_device(): pieces = lax.all_to_all(weights, 'seg', 0, 0, tiled=True)  29.5 us
    all_to_all x1, blocking collectives, on_device(): terms = lax.all_to_all(grid, 'seg', 0, 0, tiled=True)  18.6 us
    all_to_all x1, blocking collectives, on_device(): lax.all_to_all(keep + other, 'frame', 0, 0, tiled=True, axis_index_groups...  13.6 us
    all_to_all x1, blocking collectives, on_device(): chosen = lax.all_to_all(sent, 'frame', 0, 0, tiled=True)  11.2 us
    all_to_all x1, blocking collectives, on_device(): gram = lax.all_to_all(spread, 'coil', 0, 0, tiled=True)  9.74 us
    all_gather x1, blocking collectives, on_device(): lax.all_gather(jnp.sum(total * total, axis=0, keepdims=True), 'coil', til...  8.43 us
    pallas_call x1, Pallas kernels, on_device(): pl.pallas_call(functools.partial(solve_kernel, part), out_shape=[jax.Shap...  3.83 us
    pallas_call x1, Pallas kernels, on_device(): pl.pallas_call(functools.partial(other_gram_kernel, part, frames), in_spe...  2.82 us
  transfers between devices with their start and end apart: 1, of which 1 were waited for; matrix products, arithmetic and copies ran while one was open for 0% of the time, Pallas kernels for 1%

profile of v19, /device:TPU:8, one launch (start us, length us, event | category | flops | bytes accessed | tf_op | source)
XLA Modules:
  0.0 102.7 jit_solution(11965527603989426350)
XLA Ops:
  0.0 2.8 %shard_map.64 = (f32[4,104,128]{2,1,0:T(8,128)S(1)}, bf16[4,576,384]{2,1,0:T(8,128)(2,1)S(1)}, bf16[4,8,2,576]{3,2,1,0:T(2,128)(2,1)S(1)}, bf16[1,4,128,384]{3,2...) custom-call(s32[1,4]{1,0:T(1,128)} %reads_ref.5, bf16[8,576,384]{2,1,0:T(8,128)(2,1)} %source_ref.1, ...), custom_call_target="tpu_custom_call" | custom-call | flops 198180864 | bytes 1843200 | tf_op jit(solution)/shard_map/pallas_call | solution.py:327
  2.8 0.0 copy-start
  2.8 0.0 copy-start.1
  2.8 1.9 %collective-permute-start = (f32[4,104,128]{2,1,0:T(8,128)S(1)}, f32[4,104,128]{2,1,0:T(8,128)S(1)}, u32[]{:S(2)}, u32[]{:S(2)}) collective-permute-start(f32[4,104,128]{2,1,0:T(8,128)S(1)} %get-tuple-element.17), channel_id=1, source_target_pairs={{0,64},{64,0},{128,192},{192,128},{256,320},{320,256},{384,448},{4... | collective-permute-start | bytes 638984 | tf_op jit(solution)/shard_map/ppermute | solution.py:362
  4.8 1.0 %shard_map.65 = f32[4,104,128]{2,1,0:T(8,128)S(1)} custom-call(s32[1,4]{1,0:T(1,128)} %reads_ref.5, bf16[4,576,384]{2,1,0:T(8,128)(2,1)S(1)} %get-tuple-element.15.held_ref, bf16[4,8,2,576]{3,2,1,0:T(2,128)(2,1)S(1)} %get-tuple-element.16.goal_ref), custom_call_target="tpu_custom_call" | custom-call | flops 198180864 | bytes 1843200 | tf_op jit(solution)/shard_map/pallas_call | solution.py:354
  5.8 0.4 collective-permute-done
  6.2 13.6 %all_to_all.25.partial_ref = f32[4,104,128]{2,1,0:T(8,128)S(1)} all-to-all(f32[4,104,128]{2,1,0:T(8,128)S(1)} %add.18), channel_id=1, replica_groups={{0,384,128,256},{64,448,192,320},{1,385,129,257},{65,449,193,321},{2,38..., dimensions={0} | all-to-all | bytes 425984 | tf_op jit(solution)/shard_map/all_to_all | solution.py:364
  19.8 9.7 %all_to_all.26.gram_ref = f32[4,72,128]{2,1,0:T(8,128)S(1)} all-to-all(f32[4,72,128]{2,1,0:T(8,128)S(1)} %get-tuple-element.19), channel_id=1, replica_groups=mesh['frame'=8,'seg'=16,'coil'=4] {'coil'}, dimensions={0} | all-to-all | bytes 294912 | tf_op jit(solution)/shard_map/all_to_all | solution.py:376
  29.6 3.8 %shard_map.67 = (bf16[16,8,384]{2,1,0:T(8,128)(2,1)S(1)}, bf16[1,4,384,128]{3,2,1,0:T(8,128)(2,1)S(1)}) custom-call(f32[4,72,128]{2,1,0:T(8,128)S(1)} %all_to_all.26.gram_ref, f32[24,128]{1,0:T(8,128)S(1)} %get-tuple-element.20.rhs_ref, bf16[1,4,128,384]{3,2,1,0:T(8,128)(2,1)S(1)} %get-tuple-element.21.app_ref), custom_call_target="tpu_custom_call" | custom-call | tf_op jit(solution)/shard_map/pallas_call | solution.py:377
  33.4 29.5 %all_to_all.27.piece_ref = bf16[16,8,384]{2,1,0:T(8,128)(2,1)S(1)} all-to-all(bf16[16,8,384]{2,1,0:T(8,128)(2,1)S(1)} %get-tuple-element.22), channel_id=1, replica_groups=mesh['frame'=8,'seg'=16,'coil'=4] {'seg'}, dimensions={0} | all-to-all | bytes 196608 | tf_op jit(solution)/shard_map/all_to_all | solution.py:390
  62.9 0.4 shard_map.68
  63.3 11.2 %all_to_all.28.weights_ref = bf16[8,4,8,384]{3,2,1,0:T(8,128)(2,1)S(1)} all-to-all(bf16[8,4,8,384]{3,2,1,0:T(8,128)(2,1)S(1)} %shard_map.68), channel_id=1, replica_groups=mesh['frame'=8,'seg'=16,'coil'=4] {'frame'}, dimensions={0} | all-to-all | bytes 393216 | tf_op jit(solution)/shard_map/all_to_all | solution.py:396
  74.5 0.0 copy-done
  74.5 0.0 copy-done.1
  74.5 0.5 shard_map.69
  75.1 18.6 %all_to_all.29 = bf16[16,16,256]{2,1,0:T(8,128)(2,1)S(1)} all-to-all(bf16[16,16,256]{2,1,0:T(8,128)(2,1)S(1)} %shard_map.69), channel_id=1, replica_groups=mesh['frame'=8,'seg'=16,'coil'=4] {'seg'}, dimensions={0} | all-to-all | bytes 262144 | tf_op jit(solution)/shard_map/all_to_all | solution.py:402
  93.7 8.4 %all-gather.1 = f32[4,1,256]{2,1,0:T(1,128)S(1)} all-gather(f32[1,1,256]{2,1,0:T(1,128)S(1)} %bitcast.2), channel_id=2, replica_groups=mesh['frame'=8,'seg'=16,'coil'=4] {'coil'}, dimensions={0}, use_global_device_ids=true | all-gather | bytes 5120 | tf_op jit(solution)/shard_map/all_gather | solution.py:404
  102.1 0.6 add_sqrt_fusion
  (5 shorter events, 0.1 us)
Async XLA Ops:
  2.8 71.7 %copy-start = (s32[1,4]{1,0:T(1,128)S(1)}, s32[1,4]{1,0:T(1,128)}, u32[]{:S(2)}) copy-start(s32[1,4]{1,0:T(1,128)} %reads_ref.5) | copy-start | bytes 52
  2.8 71.7 %copy-start.1 = (s32[1,4]{1,0:T(1,128)S(1)}, s32[1,4]{1,0:T(1,128)}, u32[]{:S(2)}) copy-start(s32[1,4]{1,0:T(1,128)} %places_ref.1) | copy-start | bytes 52
  2.8 3.4 %collective-permute-start = (f32[4,104,128]{2,1,0:T(8,128)S(1)}, f32[4,104,128]{2,1,0:T(8,128)S(1)}, u32[]{:S(2)}, u32[]{:S(2)}) collective-permute-start(f32[4,104,128]{2,1,0:T(8,128)S(1)} %get-tuple-element.17), channel_id=1, source_target_pairs={{0,64},{64,0},{128,192},{192,128},{256,320},{320,256},{384,448},{4... | collective-permute-start | bytes 638984 | tf_op jit(solution)/shard_map/ppermute | solution.py:362

commit v20 on v18

--- a/solution.py
+++ b/solution.py
@@ -106,15 +106,14 @@
             )
 
 
-def tell(frames, read_ref, out_ref):
+def tell(frames, read_ref):
     core = lax.rem(lax.axis_index("frame"), 2)
     row = lax.broadcasted_iota(jnp.int32, (8, LANES), 0)
     lane = lax.broadcasted_iota(jnp.int32, (8, LANES), 1)
     told = jnp.zeros((8, LANES), jnp.int32)
     for place in range(read_ref.shape[1]):
         told = jnp.where((row == core) & (lane == place), lax.div(read_ref[0, place], frames), told)
-    for slot in range(out_ref.shape[0]):
-        out_ref[slot, out_ref.shape[1] - 8 :] = told.astype(F32)
+    return told.astype(F32)
 
 
 def other_gram_kernel(
@@ -126,6 +125,7 @@
     app_ref,
     interp_ref,
     out_ref,
+    row_ref,
     own_held_ref,
     own_goal_ref,
     own_app_ref,
@@ -163,7 +163,10 @@
         copy.start()
     gram_sums(part, ((0,), (1, 2, 3)), (), held_ref, goal_ref, turned_ref, out_ref, copies)
     late[0].wait()
-    tell(frames, read_ref, out_ref)
+    told = tell(frames, read_ref)
+    row_ref[...] = told
+    for slot in range(each):
+        out_ref[slot, out_ref.shape[1] - 8 :] = told
     for copy in late[1:]:
         copy.wait()
     for pair in copies[each:]:
@@ -171,13 +174,11 @@
             copy.wait()
 
 
-def own_gram_kernel(part, frames, reads_ref, held_ref, goal_ref, out_ref, turned_ref, read_ref, read_sem):
-    listing = pltpu.make_async_copy(reads_ref, read_ref, read_sem)
-    listing.start()
+def own_gram_kernel(part, row_ref, held_ref, goal_ref, out_ref, turned_ref):
     slots = tuple(range(out_ref.shape[0]))
     gram_sums(part, (slots,), (2,), held_ref, goal_ref, turned_ref, out_ref, [() for _ in slots])
-    listing.wait()
-    tell(frames, read_ref, out_ref)
+    for slot in slots:
+        out_ref[slot, out_ref.shape[1] - 8 :] = row_ref[...]
 
 
 def sum_kernel(gram_rows, partial_ref, spread_ref, rhs_ref, told_ref):
@@ -323,11 +324,12 @@
         bytes_accessed=2 * each * samples * (depth + 2 * coils),
         transcendentals=0,
     )
-    send, own_held, own_goal, own_app, own_interp = pl.pallas_call(
+    send, row, own_held, own_goal, own_app, own_interp = pl.pallas_call(
         functools.partial(other_gram_kernel, part, frames),
         in_specs=[hbm] * 5,
         out_shape=[
             block,
+            jax.ShapeDtypeStruct((8, LANES), F32),
             jax.ShapeDtypeStruct((each, samples, depth), BF16),
             jax.ShapeDtypeStruct((each, coils, 2, samples), BF16),
             jax.ShapeDtypeStruct(app_source.shape, BF16),
@@ -351,13 +353,13 @@
         pltpu.with_memory_space_constraint(interp, pltpu.HBM),
     )
     keep = pl.pallas_call(
-        functools.partial(own_gram_kernel, part, frames),
-        in_specs=[hbm, vmem, vmem],
+        functools.partial(own_gram_kernel, part),
+        in_specs=[vmem, vmem, vmem],
         out_shape=block,
-        scratch_shapes=[turned, *reading, pltpu.SemaphoreType.DMA],
+        scratch_shapes=[turned],
         compiler_params=SMALL,
         cost_estimate=cost,
-    )(listed, own_held, own_goal)
+    )(row, own_held, own_goal)
     other = lax.ppermute(send, "frame", [(frame, frame ^ 1) for frame in range(frames)])
     chips = [[2 * chip + core for chip in range(frames // 2)] for core in range(2)]
     received = lax.all_to_all(

time: 103 us -> 103 us (level)
  no operation moved by 1% of the time
where the time goes in v20:
time: 103 us
  blocking collectives  91.1 us (88%)
  Pallas kernels  8.56 us (8%)
  starting transfers between devices  1.92 us (2%)
    all_to_all x1, blocking collectives, on_device(): pieces = lax.all_to_all(weights, 'seg', 0, 0, tiled=True)  29.5 us
    all_to_all x1, blocking collectives, on_device(): terms = lax.all_to_all(grid, 'seg', 0, 0, tiled=True)  18.5 us
    all_to_all x1, blocking collectives, on_device(): lax.all_to_all(keep + other, 'frame', 0, 0, tiled=True, axis_index_groups...  13.8 us
    all_to_all x1, blocking collectives, on_device(): chosen = lax.all_to_all(sent, 'frame', 0, 0, tiled=True)  11 us
    all_to_all x1, blocking collectives, on_device(): gram = lax.all_to_all(spread, 'coil', 0, 0, tiled=True)  9.73 us
    all_gather x1, blocking collectives, on_device(): lax.all_gather(jnp.sum(total * total, axis=0, keepdims=True), 'coil', til...  8.45 us
    pallas_call x1, Pallas kernels, on_device(): pl.pallas_call(functools.partial(solve_kernel, part), out_shape=[jax.Shap...  3.83 us
    pallas_call x1, Pallas kernels, on_device(): pl.pallas_call(functools.partial(other_gram_kernel, part, frames), in_spe...  2.82 us
  transfers between devices with their start and end apart: 1, of which 1 were waited for; matrix products, arithmetic and copies ran while one was open for 0% of the time, Pallas kernels for 1%

profile of v20, /device:TPU:8, one launch (start us, length us, event | category | flops | bytes accessed | tf_op | source)
XLA Modules:
  0.0 102.7 jit_solution(5562198734598313760)
XLA Ops:
  0.0 2.8 %shard_map.64 = (f32[4,104,128]{2,1,0:T(8,128)S(1)}, f32[8,128]{1,0:T(8,128)S(1)}, bf16[4,576,384]{2,1,0:T(8,128)(2,1)S(1)}, bf16[4,8,2,576]{3,2,1,0:T(2,128)(2,...) custom-call(s32[1,4]{1,0:T(1,128)} %reads_ref.3, bf16[8,576,384]{2,1,0:T(8,128)(2,1)} %source_ref.1, ...), custom_call_target="tpu_custom_call" | custom-call | flops 198180864 | bytes 1843200 | tf_op jit(solution)/shard_map/pallas_call | solution.py:327
  2.8 0.0 copy-start
  2.8 0.0 copy-start.1
  2.8 1.9 %collective-permute-start = (f32[4,104,128]{2,1,0:T(8,128)S(1)}, f32[4,104,128]{2,1,0:T(8,128)S(1)}, u32[]{:S(2)}, u32[]{:S(2)}) collective-permute-start(f32[4,104,128]{2,1,0:T(8,128)S(1)} %get-tuple-element.19), channel_id=1, source_target_pairs={{0,64},{64,0},{128,192},{192,128},{256,320},{320,256},{384,448},{4... | collective-permute-start | bytes 638984 | tf_op jit(solution)/shard_map/ppermute | solution.py:363
  4.8 1.0 shard_map.65
  5.8 0.4 collective-permute-done
  6.2 13.8 %all_to_all.25.partial_ref = f32[4,104,128]{2,1,0:T(8,128)S(1)} all-to-all(f32[4,104,128]{2,1,0:T(8,128)S(1)} %add.18), channel_id=1, replica_groups={{0,128,256,384},{64,192,320,448},{1,129,257,385},{65,193,321,449},{2,13..., dimensions={0} | all-to-all | bytes 425984 | tf_op jit(solution)/shard_map/all_to_all | solution.py:365
  20.1 9.7 %all_to_all.26.gram_ref = f32[4,72,128]{2,1,0:T(8,128)S(1)} all-to-all(f32[4,72,128]{2,1,0:T(8,128)S(1)} %get-tuple-element.21), channel_id=1, replica_groups=mesh['frame'=8,'seg'=16,'coil'=4] {'coil'}, dimensions={0} | all-to-all | bytes 294912 | tf_op jit(solution)/shard_map/all_to_all | solution.py:377
  29.8 3.8 %shard_map.67 = (bf16[16,8,384]{2,1,0:T(8,128)(2,1)S(1)}, bf16[1,4,384,128]{3,2,1,0:T(8,128)(2,1)S(1)}) custom-call(f32[4,72,128]{2,1,0:T(8,128)S(1)} %all_to_all.26.gram_ref, f32[24,128]{1,0:T(8,128)S(1)} %get-tuple-element.22.rhs_ref, bf16[1,4,128,384]{3,2,1,0:T(8,128)(2,1)S(1)} %get-tuple-element.23.app_ref), custom_call_target="tpu_custom_call" | custom-call | tf_op jit(solution)/shard_map/pallas_call | solution.py:378
  33.6 29.5 %all_to_all.27.piece_ref = bf16[16,8,384]{2,1,0:T(8,128)(2,1)S(1)} all-to-all(bf16[16,8,384]{2,1,0:T(8,128)(2,1)S(1)} %get-tuple-element.24), channel_id=1, replica_groups=mesh['frame'=8,'seg'=16,'coil'=4] {'seg'}, dimensions={0} | all-to-all | bytes 196608 | tf_op jit(solution)/shard_map/all_to_all | solution.py:391
  63.2 0.4 shard_map.68
  63.5 11.0 %all_to_all.28.weights_ref = bf16[8,4,8,384]{3,2,1,0:T(8,128)(2,1)S(1)} all-to-all(bf16[8,4,8,384]{3,2,1,0:T(8,128)(2,1)S(1)} %shard_map.68), channel_id=1, replica_groups=mesh['frame'=8,'seg'=16,'coil'=4] {'frame'}, dimensions={0} | all-to-all | bytes 393216 | tf_op jit(solution)/shard_map/all_to_all | solution.py:397
  74.5 0.0 copy-done
  74.5 0.0 copy-done.1
  74.5 0.5 shard_map.69
  75.1 18.5 %all_to_all.29 = bf16[16,16,256]{2,1,0:T(8,128)(2,1)S(1)} all-to-all(bf16[16,16,256]{2,1,0:T(8,128)(2,1)S(1)} %shard_map.69), channel_id=1, replica_groups=mesh['frame'=8,'seg'=16,'coil'=4] {'seg'}, dimensions={0} | all-to-all | bytes 262144 | tf_op jit(solution)/shard_map/all_to_all | solution.py:403
  93.7 8.4 %all-gather.1 = f32[4,1,256]{2,1,0:T(1,128)S(1)} all-gather(f32[1,1,256]{2,1,0:T(1,128)S(1)} %bitcast.2), channel_id=2, replica_groups=mesh['frame'=8,'seg'=16,'coil'=4] {'coil'}, dimensions={0}, use_global_device_ids=true | all-gather | bytes 5120 | tf_op jit(solution)/shard_map/all_gather | solution.py:405
  102.1 0.6 add_sqrt_fusion
  (5 shorter events, 0.1 us)
Async XLA Ops:
  2.8 71.7 %copy-start = (s32[1,4]{1,0:T(1,128)S(1)}, s32[1,4]{1,0:T(1,128)}, u32[]{:S(2)}) copy-start(s32[1,4]{1,0:T(1,128)} %reads_ref.3) | copy-start | bytes 52
  2.8 71.7 %copy-start.1 = (s32[1,4]{1,0:T(1,128)S(1)}, s32[1,4]{1,0:T(1,128)}, u32[]{:S(2)}) copy-start(s32[1,4]{1,0:T(1,128)} %places_ref.1) | copy-start | bytes 52
  2.8 3.4 %collective-permute-start = (f32[4,104,128]{2,1,0:T(8,128)S(1)}, f32[4,104,128]{2,1,0:T(8,128)S(1)}, u32[]{:S(2)}, u32[]{:S(2)}) collective-permute-start(f32[4,104,128]{2,1,0:T(8,128)S(1)} %get-tuple-element.19), channel_id=1, source_target_pairs={{0,64},{64,0},{128,192},{192,128},{256,320},{320,256},{384,448},{4... | collective-permute-start | bytes 638984 | tf_op jit(solution)/shard_map/ppermute | solution.py:363

commit v21 on v20

--- a/solution.py
+++ b/solution.py
@@ -30,8 +30,12 @@
 
 
 def product(left, right):
+    return product_with(left, pieces_of(right, 2))
+
+
+def product_with(left, b):
     rows = left.shape[0]
-    a, b = pieces_of(left, 2), pieces_of(right, 2)
+    a = pieces_of(left, 2)
     dot = functools.partial(jnp.dot, preferred_element_type=F32)
     first = dot(jnp.concatenate(a, axis=0), b[0])
     return first[:rows] + (first[rows:] + dot(a[0], b[1]))
@@ -251,9 +255,10 @@
     )
     sol = sol_ref[...]
     total = sol
+    real_pieces, imag_pieces = pieces_of(real_ref[...], 2), pieces_of(imag_ref[...], 2)
     for _ in range(2):
-        by_real = product(total, real_ref[...])
-        by_imag = product(total, imag_ref[...])
+        by_real = product_with(total, real_pieces)
+        by_imag = product_with(total, imag_pieces)
         change = jnp.concatenate(
             [by_real[:coils] + by_imag[coils:], by_real[coils:] - by_imag[:coils]], axis=0
         )

time: 103 us -> 103 us (level)
  no operation moved by 1% of the time
where the time goes in v21:
time: 103 us
  blocking collectives  91.4 us (89%)
  Pallas kernels  8.56 us (8%)
  starting transfers between devices  1.92 us (2%)
    all_to_all x1, blocking collectives, on_device(): pieces = lax.all_to_all(weights, 'seg', 0, 0, tiled=True)  29.9 us
    all_to_all x1, blocking collectives, on_device(): terms = lax.all_to_all(grid, 'seg', 0, 0, tiled=True)  18.8 us
    all_to_all x1, blocking collectives, on_device(): lax.all_to_all(keep + other, 'frame', 0, 0, tiled=True, axis_index_groups...  13.8 us
    all_to_all x1, blocking collectives, on_device(): chosen = lax.all_to_all(sent, 'frame', 0, 0, tiled=True)  10.7 us
    all_to_all x1, blocking collectives, on_device(): gram = lax.all_to_all(spread, 'coil', 0, 0, tiled=True)  9.73 us
    all_gather x1, blocking collectives, on_device(): lax.all_gather(jnp.sum(total * total, axis=0, keepdims=True), 'coil', til...  8.41 us
    pallas_call x1, Pallas kernels, on_device(): pl.pallas_call(functools.partial(solve_kernel, part), out_shape=[jax.Shap...  3.83 us
    pallas_call x1, Pallas kernels, on_device(): pl.pallas_call(functools.partial(other_gram_kernel, part, frames), in_spe...  2.82 us
  transfers between devices with their start and end apart: 1, of which 1 were waited for; matrix products, arithmetic and copies ran while one was open for 0% of the time, Pallas kernels for 1%

profile of v21, /device:TPU:8, one launch (start us, length us, event | category | flops | bytes accessed | tf_op | source)
XLA Modules:
  0.0 103.1 jit_solution(5562198734598313760)
XLA Ops:
  0.0 2.8 %shard_map.64 = (f32[4,104,128]{2,1,0:T(8,128)S(1)}, f32[8,128]{1,0:T(8,128)S(1)}, bf16[4,576,384]{2,1,0:T(8,128)(2,1)S(1)}, bf16[4,8,2,576]{3,2,1,0:T(2,128)(2,...) custom-call(s32[1,4]{1,0:T(1,128)} %reads_ref.3, bf16[8,576,384]{2,1,0:T(8,128)(2,1)} %source_ref.1, ...), custom_call_target="tpu_custom_call" | custom-call | flops 198180864 | bytes 1843200 | tf_op jit(solution)/shard_map/pallas_call | solution.py:332
  2.8 0.0 copy-start
  2.8 0.0 copy-start.1
  2.8 1.9 %collective-permute-start = (f32[4,104,128]{2,1,0:T(8,128)S(1)}, f32[4,104,128]{2,1,0:T(8,128)S(1)}, u32[]{:S(2)}, u32[]{:S(2)}) collective-permute-start(f32[4,104,128]{2,1,0:T(8,128)S(1)} %get-tuple-element.19), channel_id=1, source_target_pairs={{0,64},{64,0},{128,192},{192,128},{256,320},{320,256},{384,448},{4... | collective-permute-start | bytes 638984 | tf_op jit(solution)/shard_map/ppermute | solution.py:368
  4.8 1.0 shard_map.65
  5.8 0.4 collective-permute-done
  6.2 13.8 %all_to_all.25.partial_ref = f32[4,104,128]{2,1,0:T(8,128)S(1)} all-to-all(f32[4,104,128]{2,1,0:T(8,128)S(1)} %add.18), channel_id=1, replica_groups={{0,128,256,384},{64,192,320,448},{1,129,257,385},{65,193,321,449},{2,13..., dimensions={0} | all-to-all | bytes 425984 | tf_op jit(solution)/shard_map/all_to_all | solution.py:370
  20.1 9.7 %all_to_all.26.gram_ref = f32[4,72,128]{2,1,0:T(8,128)S(1)} all-to-all(f32[4,72,128]{2,1,0:T(8,128)S(1)} %get-tuple-element.21), channel_id=1, replica_groups=mesh['frame'=8,'seg'=16,'coil'=4] {'coil'}, dimensions={0} | all-to-all | bytes 294912 | tf_op jit(solution)/shard_map/all_to_all | solution.py:382
  29.8 3.8 %shard_map.67 = (bf16[16,8,384]{2,1,0:T(8,128)(2,1)S(1)}, bf16[1,4,384,128]{3,2,1,0:T(8,128)(2,1)S(1)}) custom-call(f32[4,72,128]{2,1,0:T(8,128)S(1)} %all_to_all.26.gram_ref, f32[24,128]{1,0:T(8,128)S(1)} %get-tuple-element.22.rhs_ref, bf16[1,4,128,384]{3,2,1,0:T(8,128)(2,1)S(1)} %get-tuple-element.23.app_ref), custom_call_target="tpu_custom_call" | custom-call | tf_op jit(solution)/shard_map/pallas_call | solution.py:383
  33.6 29.9 %all_to_all.27.piece_ref = bf16[16,8,384]{2,1,0:T(8,128)(2,1)S(1)} all-to-all(bf16[16,8,384]{2,1,0:T(8,128)(2,1)S(1)} %get-tuple-element.24), channel_id=1, replica_groups=mesh['frame'=8,'seg'=16,'coil'=4] {'seg'}, dimensions={0} | all-to-all | bytes 196608 | tf_op jit(solution)/shard_map/all_to_all | solution.py:396
  63.6 0.4 shard_map.68
  63.9 10.7 %all_to_all.28.weights_ref = bf16[8,4,8,384]{3,2,1,0:T(8,128)(2,1)S(1)} all-to-all(bf16[8,4,8,384]{3,2,1,0:T(8,128)(2,1)S(1)} %shard_map.68), channel_id=1, replica_groups=mesh['frame'=8,'seg'=16,'coil'=4] {'frame'}, dimensions={0} | all-to-all | bytes 393216 | tf_op jit(solution)/shard_map/all_to_all | solution.py:402
  74.7 0.0 copy-done
  74.7 0.0 copy-done.1
  74.7 0.5 shard_map.69
  75.2 18.8 %all_to_all.29 = bf16[16,16,256]{2,1,0:T(8,128)(2,1)S(1)} all-to-all(bf16[16,16,256]{2,1,0:T(8,128)(2,1)S(1)} %shard_map.69), channel_id=1, replica_groups=mesh['frame'=8,'seg'=16,'coil'=4] {'seg'}, dimensions={0} | all-to-all | bytes 262144 | tf_op jit(solution)/shard_map/all_to_all | solution.py:408
  94.1 8.4 %all-gather.1 = f32[4,1,256]{2,1,0:T(1,128)S(1)} all-gather(f32[1,1,256]{2,1,0:T(1,128)S(1)} %bitcast.2), channel_id=2, replica_groups=mesh['frame'=8,'seg'=16,'coil'=4] {'coil'}, dimensions={0}, use_global_device_ids=true | all-gather | bytes 5120 | tf_op jit(solution)/shard_map/all_gather | solution.py:410
  102.5 0.6 add_sqrt_fusion
  (5 shorter events, 0.1 us)
Async XLA Ops:
  2.8 71.8 %copy-start = (s32[1,4]{1,0:T(1,128)S(1)}, s32[1,4]{1,0:T(1,128)}, u32[]{:S(2)}) copy-start(s32[1,4]{1,0:T(1,128)} %reads_ref.3) | copy-start | bytes 52
  2.8 71.8 %copy-start.1 = (s32[1,4]{1,0:T(1,128)S(1)}, s32[1,4]{1,0:T(1,128)}, u32[]{:S(2)}) copy-start(s32[1,4]{1,0:T(1,128)} %places_ref.1) | copy-start | bytes 52
  2.8 3.4 %collective-permute-start = (f32[4,104,128]{2,1,0:T(8,128)S(1)}, f32[4,104,128]{2,1,0:T(8,128)S(1)}, u32[]{:S(2)}, u32[]{:S(2)}) collective-permute-start(f32[4,104,128]{2,1,0:T(8,128)S(1)} %get-tuple-element.19), channel_id=1, source_target_pairs={{0,64},{64,0},{128,192},{192,128},{256,320},{320,256},{384,448},{4... | collective-permute-start | bytes 638984 | tf_op jit(solution)/shard_map/ppermute | solution.py:368

commit v22 on v21

--- a/solution.py
+++ b/solution.py
@@ -155,6 +155,16 @@
                 pltpu.make_async_copy(target_ref.at[segment], goal, sem.at[1, slot]),
             )
         )
+    quarter = held_ref.shape[1] // 4
+    first = [
+        pltpu.make_async_copy(
+            source_ref.at[1 - core, pl.ds(run * quarter, quarter)],
+            held_ref.at[0, pl.ds(run * quarter, quarter)],
+            late_sem.at[3 + run],
+        )
+        for run in range(4)
+    ]
+    copies[0] = (*first, copies[0][1])
     for pair in copies:
         for copy in pair:
             copy.start()
@@ -346,7 +356,7 @@
             turned,
             *reading,
             pltpu.SemaphoreType.DMA((2, held)),
-            pltpu.SemaphoreType.DMA((3,)),
+            pltpu.SemaphoreType.DMA((7,)),
         ],
         compiler_params=SMALL,
         cost_estimate=cost,

time: 103 us -> 103 us (level)
  the two profiles are of different devices: /device:TPU:8 before, /device:TPU:32 now
where the time goes in v22:
time: 103 us
  blocking collectives  91.2 us (89%)
  Pallas kernels  8.63 us (8%)
  starting transfers between devices  1.92 us (2%)
    all_to_all x1, blocking collectives, on_device(): pieces = lax.all_to_all(weights, 'seg', 0, 0, tiled=True)  29.8 us
    all_to_all x1, blocking collectives, on_device(): terms = lax.all_to_all(grid, 'seg', 0, 0, tiled=True)  19.5 us
    all_to_all x1, blocking collectives, on_device(): lax.all_to_all(keep + other, 'frame', 0, 0, tiled=True, axis_index_groups...  14.6 us
    all_to_all x1, blocking collectives, on_device(): chosen = lax.all_to_all(sent, 'frame', 0, 0, tiled=True)  10.7 us
    all_to_all x1, blocking collectives, on_device(): gram = lax.all_to_all(spread, 'coil', 0, 0, tiled=True)  8.41 us
    all_gather x1, blocking collectives, on_device(): lax.all_gather(jnp.sum(total * total, axis=0, keepdims=True), 'coil', til...  8.12 us
    pallas_call x1, Pallas kernels, on_device(): pl.pallas_call(functools.partial(solve_kernel, part), out_shape=[jax.Shap...  3.84 us
    pallas_call x1, Pallas kernels, on_device(): pl.pallas_call(functools.partial(other_gram_kernel, part, frames), in_spe...  2.88 us
  transfers between devices with their start and end apart: 1, of which 1 were waited for; matrix products, arithmetic and copies ran while one was open for 0% of the time, Pallas kernels for 1%

profile of v22, /device:TPU:32, one launch (start us, length us, event | category | flops | bytes accessed | tf_op | source)
XLA Modules:
  0.0 103.0 jit_solution(12296213493597445894)
XLA Ops:
  0.0 2.9 %shard_map.64 = (f32[4,104,128]{2,1,0:T(8,128)S(1)}, f32[8,128]{1,0:T(8,128)S(1)}, bf16[4,576,384]{2,1,0:T(8,128)(2,1)S(1)}, bf16[4,8,2,576]{3,2,1,0:T(2,128)(2,...) custom-call(s32[1,4]{1,0:T(1,128)} %reads_ref.3, bf16[8,576,384]{2,1,0:T(8,128)(2,1)} %source_ref.1, ...), custom_call_target="tpu_custom_call" | custom-call | flops 198180864 | bytes 1843200 | tf_op jit(solution)/shard_map/pallas_call | solution.py:342
  2.9 0.0 copy-start
  2.9 0.0 copy-start.1
  2.9 1.9 %collective-permute-start = (f32[4,104,128]{2,1,0:T(8,128)S(1)}, f32[4,104,128]{2,1,0:T(8,128)S(1)}, u32[]{:S(2)}, u32[]{:S(2)}) collective-permute-start(f32[4,104,128]{2,1,0:T(8,128)S(1)} %get-tuple-element.19), channel_id=1, source_target_pairs={{0,64},{64,0},{128,192},{192,128},{256,320},{320,256},{384,448},{4... | collective-permute-start | bytes 638984 | tf_op jit(solution)/shard_map/ppermute | solution.py:378
  4.8 1.0 shard_map.65
  5.8 0.4 collective-permute-done
  6.3 14.6 %all_to_all.25.partial_ref = f32[4,104,128]{2,1,0:T(8,128)S(1)} all-to-all(f32[4,104,128]{2,1,0:T(8,128)S(1)} %add.18), channel_id=1, replica_groups={{0,128,256,384},{64,192,320,448},{1,129,257,385},{65,193,321,449},{2,13..., dimensions={0} | all-to-all | bytes 425984 | tf_op jit(solution)/shard_map/all_to_all | solution.py:380
  20.9 8.4 %all_to_all.26.gram_ref = f32[4,72,128]{2,1,0:T(8,128)S(1)} all-to-all(f32[4,72,128]{2,1,0:T(8,128)S(1)} %get-tuple-element.21), channel_id=1, replica_groups=mesh['frame'=8,'seg'=16,'coil'=4] {'coil'}, dimensions={0} | all-to-all | bytes 294912 | tf_op jit(solution)/shard_map/all_to_all | solution.py:392
  29.3 3.8 %shard_map.67 = (bf16[16,8,384]{2,1,0:T(8,128)(2,1)S(1)}, bf16[1,4,384,128]{3,2,1,0:T(8,128)(2,1)S(1)}) custom-call(f32[4,72,128]{2,1,0:T(8,128)S(1)} %all_to_all.26.gram_ref, f32[24,128]{1,0:T(8,128)S(1)} %get-tuple-element.22.rhs_ref, bf16[1,4,128,384]{3,2,1,0:T(8,128)(2,1)S(1)} %get-tuple-element.23.app_ref), custom_call_target="tpu_custom_call" | custom-call | tf_op jit(solution)/shard_map/pallas_call | solution.py:393
  33.2 29.8 %all_to_all.27.piece_ref = bf16[16,8,384]{2,1,0:T(8,128)(2,1)S(1)} all-to-all(bf16[16,8,384]{2,1,0:T(8,128)(2,1)S(1)} %get-tuple-element.24), channel_id=1, replica_groups=mesh['frame'=8,'seg'=16,'coil'=4] {'seg'}, dimensions={0} | all-to-all | bytes 196608 | tf_op jit(solution)/shard_map/all_to_all | solution.py:406
  63.0 0.4 shard_map.68
  63.4 10.7 %all_to_all.28.weights_ref = bf16[8,4,8,384]{3,2,1,0:T(8,128)(2,1)S(1)} all-to-all(bf16[8,4,8,384]{3,2,1,0:T(8,128)(2,1)S(1)} %shard_map.68), channel_id=1, replica_groups=mesh['frame'=8,'seg'=16,'coil'=4] {'frame'}, dimensions={0} | all-to-all | bytes 393216 | tf_op jit(solution)/shard_map/all_to_all | solution.py:412
  74.1 0.0 copy-done
  74.1 0.0 copy-done.1
  74.1 0.5 shard_map.69
  74.7 19.5 %all_to_all.29 = bf16[16,16,256]{2,1,0:T(8,128)(2,1)S(1)} all-to-all(bf16[16,16,256]{2,1,0:T(8,128)(2,1)S(1)} %shard_map.69), channel_id=1, replica_groups=mesh['frame'=8,'seg'=16,'coil'=4] {'seg'}, dimensions={0} | all-to-all | bytes 262144 | tf_op jit(solution)/shard_map/all_to_all | solution.py:418
  94.3 8.1 %all-gather.1 = f32[4,1,256]{2,1,0:T(1,128)S(1)} all-gather(f32[1,1,256]{2,1,0:T(1,128)S(1)} %bitcast.2), channel_id=2, replica_groups=mesh['frame'=8,'seg'=16,'coil'=4] {'coil'}, dimensions={0}, use_global_device_ids=true | all-gather | bytes 5120 | tf_op jit(solution)/shard_map/all_gather | solution.py:420
  102.4 0.6 add_sqrt_fusion
  (5 shorter events, 0.1 us)
Async XLA Ops:
  2.9 71.2 %copy-start = (s32[1,4]{1,0:T(1,128)S(1)}, s32[1,4]{1,0:T(1,128)}, u32[]{:S(2)}) copy-start(s32[1,4]{1,0:T(1,128)} %reads_ref.3) | copy-start | bytes 52
  2.9 71.2 %copy-start.1 = (s32[1,4]{1,0:T(1,128)S(1)}, s32[1,4]{1,0:T(1,128)}, u32[]{:S(2)}) copy-start(s32[1,4]{1,0:T(1,128)} %places_ref.1) | copy-start | bytes 52
  2.9 3.4 %collective-permute-start = (f32[4,104,128]{2,1,0:T(8,128)S(1)}, f32[4,104,128]{2,1,0:T(8,128)S(1)}, u32[]{:S(2)}, u32[]{:S(2)}) collective-permute-start(f32[4,104,128]{2,1,0:T(8,128)S(1)} %get-tuple-element.19), channel_id=1, source_target_pairs={{0,64},{64,0},{128,192},{192,128},{256,320},{320,256},{384,448},{4... | collective-permute-start | bytes 638984 | tf_op jit(solution)/shard_map/ppermute | solution.py:378
